TPU v7x, 128 devices: a whole 4x4x4 slice. The times are simulated.
128 devices in a mesh: inp: 16 (over x, z), tim: 8 (over y, core).
Axes of the slice: x: 4, y: 4, z: 4, core: 2. Of those that a mesh axis runs over, the one named last changes fastest.
Arguments:
- voltages: int32 [2, 1024, 131072], P(None, 'inp', 'tim'), may hold values from -128 to 127
- scale_exps: int32 [1024, 32], P('inp', 'tim'), may hold values from 0 to 3
- owner_table: int32 [144], replicated, may hold values from 0 to 127, as said below
Outputs:
- visibilities: float32 [256, 1024, 1024], P(('inp', 'tim'))
Inputs may be any that keep to these rules, and one draw needn't show every extreme that they name: owner_table[o] names the device whose index along inp, times the size of tim, plus its index along tim, is the value. No device owns more than 2 output channels, and some device owns exactly 2.
All inputs are finite; a program needn't handle non-finite values.
Results may differ from a plain program's by a relative error of at most 0.0035.
Values may be sent and summed in bfloat16 or wider, within the bound.
A program may use at most 192 MiB of HBM per device.

v0:
```python
import math

import jax
import jax.numpy as jnp
from jax import lax
from jax.sharding import PartitionSpec as P

RADIX = 64
F = 4096
AVG = 24
CH = 144
TAPS = 4


def shifted(value, axis, steps):
    count = lax.axis_size(axis)
    initial, last = (max(0, -steps), min(count, count - steps))
    return lax.ppermute(value, axis, [(source, source + steps) for source in range(initial, last)])


def window_table():
    length = TAPS * F
    steps = jnp.arange(length, dtype=jnp.int32).astype(jnp.float32)
    centre = (steps + 0.5 - length / 2.0) / F
    taper = 0.5 - 0.5 * jnp.cos(2.0 * math.pi * (steps + 0.5) / length)
    return (jnp.sinc(centre) * taper).reshape(TAPS, F)


def radix_table(radix):
    index = jnp.arange(radix, dtype=jnp.int32)
    phase = index[:, None] * index[None, :] % radix
    angle = 2.0 * math.pi * phase.astype(jnp.float32) / radix
    cosine = jnp.cos(angle)
    sine = jnp.sin(angle)
    return jnp.stack(
        [jnp.stack([cosine, -sine], axis=1), jnp.stack([sine, cosine], axis=1)], axis=0
    )


def owner_rows(owner_table, cap):
    index = jnp.arange(owner_table.shape[0], dtype=jnp.int32)
    same = owner_table[:, None] == owner_table[None, :]
    earlier = index[None, :] < index[:, None]
    slot = jnp.sum((same & earlier).astype(jnp.int32), axis=1)
    return owner_table * cap + slot


def body(voltages, scale_exps, owner_table):
    n_inp = lax.axis_size("inp")
    n_tim = lax.axis_size("tim")
    devices = n_inp * n_tim
    cap = max(2, 2 * CH // devices)
    in_dev = voltages.shape[1]
    spec_dev = voltages.shape[2] // F
    scale = jnp.exp2(scale_exps.astype(jnp.float32)) / 128.0
    samples = (
        voltages.reshape(2, in_dev, spec_dev, F).astype(jnp.float32) * scale[None, :, :, None]
    ).astype(jnp.bfloat16)
    tail = samples[:, :, spec_dev - (TAPS - 1) :, :]
    before = shifted(tail, "tim", 1)
    extended = jnp.concatenate([before, samples], axis=2)
    weights = window_table()
    filtered = jnp.zeros((2, in_dev, spec_dev, F), jnp.float32)
    for tap in range(TAPS):
        filtered = filtered + weights[tap][None, None, None, :] * extended[
            :, :, tap : tap + spec_dev, :
        ].astype(jnp.float32)
    filtered = filtered.astype(jnp.bfloat16)
    table = radix_table(RADIX)
    series = filtered.reshape(2, in_dev * spec_dev, RADIX, RADIX).astype(jnp.float32)
    first = jnp.einsum("cbnm,cndk->bdkm", series, table, precision=lax.Precision.HIGHEST)
    index = jnp.arange(RADIX, dtype=jnp.int32)
    twist = 2.0 * math.pi * (index[:, None] * index[None, :] % F).astype(jnp.float32) / F
    cos_twist = jnp.cos(twist)[None]
    sin_twist = jnp.sin(twist)[None]
    turned = jnp.stack(
        [
            first[:, 0] * cos_twist + first[:, 1] * sin_twist,
            first[:, 1] * cos_twist - first[:, 0] * sin_twist,
        ],
        axis=1,
    )
    second = jnp.einsum("bdkn,dnel->belk", turned, table, precision=lax.Precision.HIGHEST)
    channels = (second * (1.0 / math.sqrt(F))).astype(jnp.bfloat16).reshape(in_dev, spec_dev, 2, F)
    rows = owner_rows(owner_table, cap)
    match = rows[None, :] == jnp.arange(devices * cap, dtype=jnp.int32)[:, None]
    valid = jnp.any(match, axis=1)
    which = jnp.sum(jnp.where(match, jnp.arange(CH, dtype=jnp.int32)[None, :], 0), axis=1)
    bins = (which[:, None] * AVG + jnp.arange(AVG, dtype=jnp.int32)[None, :] - AVG * CH // 2) % F
    picked = jnp.take(channels, bins.reshape(-1), axis=3)
    keep_mask = jnp.repeat(valid, AVG)
    picked = jnp.where(keep_mask[None, None, None, :], picked, jnp.zeros_like(picked))
    outgoing = picked.reshape(in_dev, spec_dev, 2, devices * cap, AVG).transpose(3, 0, 2, 1, 4)
    outgoing = outgoing.reshape(devices, cap, in_dev * 2 * spec_dev * AVG)
    inverse = 1.0 / (n_tim * spec_dev * AVG)
    received = lax.all_to_all(outgoing, ("inp", "tim"), split_axis=0, concat_axis=0, tiled=True)
    count = received.shape[1]
    pieces = received.reshape(n_inp, n_tim, count, in_dev, 2, spec_dev * AVG)
    ordered = pieces.transpose(2, 0, 3, 4, 1, 5).reshape(
        count, n_inp * in_dev, 2, n_tim * spec_dev * AVG
    )
    width = n_inp * in_dev
    stacked = jnp.concatenate([ordered[:, :, 0, :], ordered[:, :, 1, :]], axis=2)
    swapped = jnp.concatenate([ordered[:, :, 1, :], -ordered[:, :, 0, :]], axis=2)
    real_gram = jnp.einsum("snk,smk->snm", stacked, stacked, preferred_element_type=jnp.float32)
    imag_gram = jnp.einsum("snk,smk->snm", swapped, stacked, preferred_element_type=jnp.float32)
    upper = (
        jnp.arange(width, dtype=jnp.int32)[:, None] <= jnp.arange(width, dtype=jnp.int32)[None, :]
    )
    return jnp.where(upper[None], real_gram, imag_gram) * inverse


def solution(mesh):
    return jax.shard_map(
        body,
        mesh=mesh,
        in_specs=(P(None, "inp", "tim"), P("inp", "tim"), P()),
        out_specs=P(("inp", "tim"), None, None),
        check_vma=False,
    )
```

profile of v0, /device:TPU:1, one launch (start us, length us, event | category | flops | bytes accessed | tf_op | source)
XLA Modules:
  0.0 523.7 jit_solution(2469610838651794973)
XLA Ops:
  0.0 7.5 %convert_element_type.94 = f32[2,64,16384]{2,1,0:T(8,128)} convert(s32[2,64,16384]{2,1,0:T(8,128)} %param.3) | non-fusion elementwise | flops 2097152 | bytes 16777216 | tf_op jit(solution)/shard_map/convert_element_type | solution.py:57
  7.5 10.9 %convert_element_type.95 = f32[2,64,4,4096]{3,2,1,0:T(4,128)} reshape(f32[2,64,16384]{2,1,0:T(8,128)} %convert_element_type.94) | data formatting | bytes 16777216 | tf_op jit(solution)/shard_map/convert_element_type | solution.py:57
  18.4 0.1 copy.40
  18.5 5.8 %multiply_convert_fusion = bf16[2,64,4,4096]{3,2,1,0:T(4,128)(2,1)S(1)} fusion(f32[2,64,4,4096]{3,2,1,0:T(4,128)} %convert_element_type.95, f32[64,4]{1,0:T(8,128)S(1)} %copy.40), kind=kLoop, calls=%fused_computation.14 | loop fusion | flops 4194304 | bytes 12583936 | tf_op jit(solution)/shard_map/convert_element_type | solution.py:58
  24.3 2.0 copy-done.1
  26.3 2.5 slice.59
  28.8 2.3 copy.41
  31.1 4.8 collective-permute-start
  35.9 0.2 convert_reduce_fusion
  36.1 0.1 select_reduce_fusion
  36.2 0.1 add_add_fusion
  36.3 0.1 sub.58
  36.4 0.1 fusion.52
  36.6 0.1 fusion.50
  36.7 0.1 fusion.48
  36.9 0.1 fusion.19
  37.0 0.2 compare_and_fusion
  37.2 0.1 compare_select_fusion.1
  37.3 0.3 fusion.26
  37.6 32.2 %collective-permute-done = bf16[2,64,3,4096]{3,1,2,0:T(8,128)(2,1)} collective-permute-done((bf16[2,64,3,4096]{3,1,2,0:T(8,128)(2,1)S(1)}, bf16[2,64,3,4096]{3,1,2,0:T(8,128)(2,1)}, u32[]{:S(2)}, u32[]{:S(2)}) %collective-permute-start) | collective-permute-done | bytes 3145760 | tf_op jit(solution)/shard_map/ppermute | solution.py:18
  69.9 4.6 copy.42
  74.5 14.5 %add_convert_fusion = bf16[2,64,4,4096]{3,2,1,0:T(4,128)(2,1)} fusion(bf16[2,64,4,4096]{3,2,1,0:T(4,128)(2,1)S(1)} %copy-done.2, bf16[2,64,3,4096]{3,2,1,0:T(4,128)(2,1)S(1)} %copy.42, f32[4096]{0:T(1024)S(1)} %get-tuple-element.10, f32[4096]{0:T(1024)S(1)} %get-tuple-element.11, f32[4096]{0:T(1024)S(1)} %get-tuple-element.12, f32[4096]{0:T(1024)S(1)} %get-tuple-element.9), kind=kLoop, calls=%fused_computation.13 | loop fusion | flops 44040192 | bytes 11599872 | tf_op jit(solution)/shard_map/convert_element_type | solution.py:68
  89.0 12.7 %reshape.243 = bf16[2,256,64,64]{3,2,1,0:T(8,128)(2,1)} reshape(bf16[2,64,4,4096]{3,2,1,0:T(4,128)(2,1)} %add_convert_fusion) | data formatting | bytes 8388608 | tf_op jit(solution)/shard_map/reshape | solution.py:70
  101.7 13.6 %copy.43 = bf16[2,256,64,64]{1,2,0,3:T(8,128)(2,1)} copy(bf16[2,256,64,64]{3,2,1,0:T(8,128)(2,1)} %reshape.243) | data formatting | bytes 8388608 | tf_op jit(solution)/shard_map/reshape | solution.py:70
  115.3 5.4 %fusion.14 = f32[256,2,64,64]{0,2,3,1:T(8,128)S(1)} fusion(bf16[2,256,64,64]{1,2,0,3:T(8,128)(2,1)} %copy.43, f32[1,64,2,64]{1,3,0,2:T(8,128)S(1)} %get-tuple-element.14, f32[1,64,2,64]{1,3,0,2:T(8,128)S(1)} %get-tuple-element.13), kind=kOutput, calls=%fused_computation.30 | convolution fusion | flops 3221241856 | bytes 12648448 | tf_op jit(solution)/shard_map/cbnm,cndk->bdkm/dot_general | solution.py:71
  120.7 1.5 multiply_add_fusion
  122.2 1.1 pad_maximum_fusion
  123.3 13.0 %fusion.8 = bf16[256,2,64,64]{0,2,3,1:T(8,128)(2,1)} fusion(f32[256,2,64,64]{0,2,3,1:T(8,128)S(1)} %pad_maximum_fusion, f32[1,64,2,64]{1,3,0,2:T(8,128)S(1)} %get-tuple-element.14, f32[1,64,2,64]{1,3,0,2:T(8,128)S(1)} %get-tuple-element.13), kind=kOutput, calls=%fused_computation.20 | convolution fusion | flops 3225436160 | bytes 12648448 | tf_op jit(solution)/shard_map/bdkn,dnel->belk/dot_general | solution.py:83
  136.3 15.6 %copy.45 = bf16[256,2,64,64]{3,2,1,0:T(8,128)(2,1)} copy(bf16[256,2,64,64]{0,2,3,1:T(8,128)(2,1)} %fusion.8) | data formatting | bytes 8388608 | tf_op jit(solution)/shard_map/convert_element_type | solution.py:84
  151.9 14.0 %reshape.244 = bf16[64,4,2,4096]{3,2,1,0:T(2,128)(2,1)} reshape(bf16[256,2,64,64]{3,2,1,0:T(8,128)(2,1)} %copy.45) | data formatting | bytes 8388608 | tf_op jit(solution)/shard_map/reshape | solution.py:84
  165.9 21.6 %copy.46 = bf16[64,4,2,4096]{0,1,3,2:T(4,128)(2,1)} copy(bf16[64,4,2,4096]{3,2,1,0:T(2,128)(2,1)} %reshape.244) | data formatting | bytes 8388608 | tf_op jit(solution)/shard_map/reshape | solution.py:84
  187.5 54.0 %gather_fusion = bf16[6144,64,4,2]{1,2,3,0:T(4,128)(2,1)} fusion(bf16[64,4,2,4096]{0,1,3,2:T(4,128)(2,1)} %copy.46, s32[6144]{0:T(1024)S(1)} %broadcast_clamp_fusion), kind=kCustom, calls=%fused_computation | custom fusion | bytes 12607488 | tf_op jit(solution)/shard_map/jit(_take)/gather | solution.py:90
  241.5 7.4 %copy.47 = bf16[64,4,2,6144]{0,3,2,1:T(8,128)(2,1)S(1)} copy(bf16[64,4,2,6144]{0,1,2,3:T(4,128)(2,1)} %bitcast.58) | data formatting | bytes 12582912 | tf_op jit(solution)/shard_map/jit(_take)/gather | solution.py:90
  248.9 5.9 %select_bitcast_fusion = bf16[256,64,2,4,24]{1,4,0,2,3:T(8,128)(2,1)} fusion(bf16[64,4,2,256,24]{0,4,3,2,1:T(8,128)(2,1)S(1)} %bitcast.56, pred[256]{0:T(512)(128)(4,1)S(1)} %fusion.19, pred[256,24]{1,0:T(8,128)(4,1)S(1)} %compare_and_fusion), kind=kLoop, calls=%fused_computation.1 | loop fusion | flops 6291456 | bytes 12589312 | tf_op jit(solution)/shard_map/transpose | solution.py:93
  254.8 41.1 %copy.48 = bf16[256,64,2,4,24]{4,3,2,1,0:T(4,128)(2,1)} copy(bf16[256,64,2,4,24]{1,4,0,2,3:T(8,128)(2,1)} %select_bitcast_fusion) | data formatting | bytes 12582912 | tf_op jit(solution)/shard_map/transpose | solution.py:93
  295.9 45.1 %reshape.245 = bf16[128,2,12288]{2,1,0:T(2,128)(2,1)} reshape(bf16[256,64,2,4,24]{4,3,2,1,0:T(4,128)(2,1)} %copy.48) | data formatting | bytes 12582912 | tf_op jit(solution)/shard_map/reshape | solution.py:94
  341.0 12.4 %all-to-all-start = ((bf16[128,2,12288]{2,1,0:T(2,128)(2,1)}), bf16[128,2,12288]{2,1,0:T(2,128)(2,1)}, u32[]{:S(2)}, u32[]{:S(2)}) async-start(bf16[128,2,12288]{2,1,0:T(2,128)(2,1)} %reshape.245), calls=%async_computation | async-start | bytes 12582912 | tf_op jit(solution)/shard_map/all_to_all | solution.py:96
  353.4 1.3 iota_compare_fusion
  354.7 74.2 %all-to-all-done = bf16[128,2,12288]{2,1,0:T(2,128)(2,1)} async-done(((bf16[128,2,12288]{2,1,0:T(2,128)(2,1)}), bf16[128,2,12288]{2,1,0:T(2,128)(2,1)}, u32[]{:S(2)}, u32[]{:S(2)}) %all-to-all-start) | async-done | bytes 6291488 | tf_op jit(solution)/shard_map/all_to_all | solution.py:96
  428.9 9.4 %copy.49 = bf16[128,2,12288]{2,0,1:T(8,128)(2,1)} copy(bf16[128,2,12288]{2,1,0:T(2,128)(2,1)} %all-to-all-done) | data formatting | bytes 12582912 | tf_op jit(solution)/shard_map/all_to_all | solution.py:96
  438.3 25.5 %reshape.246 = bf16[16,8,2,64,2,96]{5,4,3,1,0,2:T(2,128)(2,1)} reshape(bf16[128,2,12288]{2,0,1:T(8,128)(2,1)} %copy.49) | data formatting | bytes 12582912 | tf_op jit(solution)/shard_map/reshape | solution.py:98
  463.7 14.6 %copy.50 = bf16[2,16,64,2,8,96]{5,4,2,1,0,3:T(8,128)(2,1)} copy(bf16[2,16,64,2,8,96]{5,3,2,4,1,0:T(2,128)(2,1)} %bitcast.57) | data formatting | bytes 12582912 | tf_op jit(solution)/shard_map/transpose | solution.py:99
  478.3 13.9 %reshape.247 = bf16[2,1024,2,768]{3,1,0,2:T(8,128)(2,1)} reshape(bf16[2,16,64,2,8,96]{5,4,2,1,0,3:T(8,128)(2,1)} %copy.50) | data formatting | bytes 12582912 | tf_op jit(solution)/shard_map/reshape | solution.py:99
  492.3 5.0 slice_bitcast_fusion.1
  497.3 0.2 copy-done
  497.5 0.2 fusion.57
  497.7 12.9 %fusion.4 = f32[2,1024,1024]{2,1,0:T(8,128)} fusion(bf16[2,1024,768]{2,1,0:T(8,128)(2,1)S(1)} %fusion.57, bf16[2,1024,768]{2,1,0:T(8,128)(2,1)} %get-tuple-element.8, bf16[2,1024,768]{2,1,0:T(8,128)(2,1)S(1)} %get-tuple-element.7), kind=kOutput, calls=%fused_computation.16 | convolution fusion | flops 6467616768 | bytes 17825792 | tf_op jit(solution)/shard_map/snk,smk->snm/dot_general | solution.py:106
  510.6 12.9 %select_multiply_fusion = f32[2,1024,1024]{2,1,0:T(8,128)} fusion(f32[2,1024,1024]{2,1,0:T(8,128)} %fusion.4, pred[1024,1024]{1,0:T(8,128)(4,1)} %iota_compare_fusion, bf16[2,1024,768]{2,1,0:T(8,128)(2,1)} %get-tuple-element.8, bf16[2,1024,768]{2,1,0:T(8,128)(2,1)S(1)} %get-tuple-element.7), kind=kOutput, calls=%fused_computation.12 | convolution fusion | flops 6459228160 | bytes 24117248 | tf_op jit(solution)/shard_map/snk,smk->snm/dot_general | solution.py:105
  (14 shorter events, 0.1 us)
Async XLA Ops:
  7.5 10.9 %copy-start.4 = (s32[64,4]{0,1:T(4,128)S(1)}, s32[64,4]{0,1:T(4,128)}, u32[]{:S(2)}) copy-start(s32[64,4]{0,1:T(4,128)} %param.4) | copy-start | bytes 3076
  24.3 2.0 copy-start.1
  26.3 9.6 %copy-start.3 = (s32[144]{0:T(256)S(1)}, s32[144]{0:T(256)}, u32[]{:S(2)}) copy-start(s32[144]{0:T(256)} %param.5) | copy-start | bytes 1732
  31.1 38.8 %collective-permute-start = (bf16[2,64,3,4096]{3,1,2,0:T(8,128)(2,1)S(1)}, bf16[2,64,3,4096]{3,1,2,0:T(8,128)(2,1)}, u32[]{:S(2)}, u32[]{:S(2)}) collective-permute-start(bf16[2,64,3,4096]{3,1,2,0:T(8,128)(2,1)S(1)} %copy.41), channel_id=1, source_target_pairs={{0,1},{1,2},{2,3},{3,4},{4,5},{5,6},{6,7},{8,9},{9,10},{10,11},{11... | collective-permute-start | bytes 9437192 | tf_op jit(solution)/shard_map/ppermute | solution.py:18
  36.4 38.0 %copy-start.2 = (bf16[2,64,4,4096]{3,2,1,0:T(4,128)(2,1)S(1)}, bf16[2,64,4,4096]{3,2,1,0:T(4,128)(2,1)}, u32[]{:S(2)}) copy-start(bf16[2,64,4,4096]{3,2,1,0:T(4,128)(2,1)} %copy-done.1) | copy-start | bytes 12582916
  341.0 87.9 %all-to-all-start = ((bf16[128,2,12288]{2,1,0:T(2,128)(2,1)}), bf16[128,2,12288]{2,1,0:T(2,128)(2,1)}, u32[]{:S(2)}, u32[]{:S(2)}) async-start(bf16[128,2,12288]{2,1,0:T(2,128)(2,1)} %reshape.245), calls=%async_computation | async-start | bytes 12582912 | tf_op jit(solution)/shard_map/all_to_all | solution.py:96
  492.2 5.3 %copy-start = (bf16[2,1024,2,768]{3,1,0,2:T(8,128)(2,1)S(1)}, bf16[2,1024,2,768]{3,1,0,2:T(8,128)(2,1)}, u32[]{:S(2)}) copy-start(bf16[2,1024,2,768]{3,1,0,2:T(8,128)(2,1)} %reshape.247) | copy-start | bytes 18874372
where the time goes:
time: 534 us; the launch traced here: 524 us
  local copies, waits for them, and re-layouts  316 us (59%)
  waiting for transfers between devices  106 us (20%)
  matrix products  44.2 us (8%)
  other arithmetic  39.4 us (7%)
  starting transfers between devices  17.1 us (3%)
    all_to_all x1, waiting for transfers between devices, body(): lax.all_to_all(outgoing, ('inp', 'tim'), split_axis=0, concat_axis=0, til...  74.2 us
    gather x2, local copies, waits for them, and re-layouts, body(): picked = jnp.take(channels, bins.reshape(-1), axis=3)  61.4 us
    reshape x1, local copies, waits for them, and re-layouts, body(): outgoing = outgoing.reshape(devices, cap, in_dev * 2 * spec_dev * AVG)  45.1 us
    transpose x1, local copies, waits for them, and re-layouts, body(): picked.reshape(in_dev, spec_dev, 2, devices * cap, AVG)  41.1 us
    reshape x2, local copies, waits for them, and re-layouts, body(): (second * (1.0 / math.sqrt(F))).astype(jnp.bfloat16)  35.6 us
    ppermute x1, waiting for transfers between devices, shifted(): lax.ppermute(value, axis, [(source, source + steps) for source in range(i...  32.2 us
    reshape x2, local copies, waits for them, and re-layouts, body(): filtered.reshape(2, in_dev * spec_dev, RADIX, RADIX).astype(jnp.float32)  26.3 us
    reshape x1, local copies, waits for them, and re-layouts, body(): pieces = received.reshape(n_inp, n_tim, count, in_dev, 2, spec_dev * AVG)  25.5 us
  transfers between devices with their start and end apart: 2, of which 2 were waited for; matrix products, arithmetic and copies ran while one was open for 1% of the time, Pallas kernels for 0%

commit v1 on v0

v1 whole, which is shorter than its diff:
```python
import functools
import math

import jax
import jax.numpy as jnp
import numpy as np
from jax import lax
from jax.experimental import pallas as pl
from jax.experimental.pallas import tpu as pltpu
from jax.sharding import PartitionSpec as P

F = 4096
AVG = 24
CH = 144
TAPS = 4
CAP = 2
R1 = 16
R2 = 256
LANES = 128


def window_table():
    length = TAPS * F
    steps = np.arange(length, dtype=np.float64)
    centre = (steps + 0.5 - length / 2.0) / F
    taper = 0.5 - 0.5 * np.cos(2.0 * math.pi * (steps + 0.5) / length)
    table = (np.sinc(centre) * taper).reshape(TAPS, 1, F)
    return np.broadcast_to(table, (TAPS, 8, F)).astype(np.float32)


def twist_table():
    phase = np.arange(R1)[:, None] * np.arange(R2)[None, :]
    angle = 2.0 * math.pi * phase / F
    table = np.stack([np.cos(angle), np.sin(angle)]) / math.sqrt(F)
    return np.broadcast_to(table[:, :, None, :], (2, R1, 8, R2)).astype(np.float32)


def radix_table():
    phase = np.arange(R2)[:, None] * np.arange(R2)[None, :] % R2
    angle = 2.0 * math.pi * phase / R2
    cosine, sine = np.cos(angle), np.sin(angle)
    table = np.concatenate(
        [np.concatenate([cosine, sine], axis=1), np.concatenate([-sine, cosine], axis=1)], axis=0
    )
    return table.astype(np.float32)


def owner_rows(owner_table, cap):
    index = jnp.arange(owner_table.shape[0], dtype=jnp.int32)
    same = owner_table[:, None] == owner_table[None, :]
    earlier = index[None, :] < index[:, None]
    slot = jnp.sum((same & earlier).astype(jnp.int32), axis=1)
    return owner_table * cap + slot


def four(a, b, c, d):
    sr, si = a[0] + c[0], a[1] + c[1]
    tr, ti = a[0] - c[0], a[1] - c[1]
    ur, ui = b[0] + d[0], b[1] + d[1]
    vr, vi = b[0] - d[0], b[1] - d[1]
    return (sr + ur, si + ui), (tr + vi, ti - vr), (sr - ur, si - ui), (tr - vi, ti + vr)


def turn(value, power):
    re, im = value
    power %= 16
    if power == 0:
        return value
    if power == 4:
        return im, -re
    root = math.sqrt(0.5)
    if power == 2:
        return (re + im) * root, (im - re) * root
    if power == 6:
        return (im - re) * root, (re + im) * (-root)
    cosine, sine = math.cos(2 * math.pi * power / 16), math.sin(2 * math.pi * power / 16)
    return re * cosine + im * sine, im * cosine - re * sine


def sixteen(x):
    inner = [four(x[b], x[4 + b], x[8 + b], x[12 + b]) for b in range(4)]
    out = [None] * 16
    for c in range(4):
        row = four(*[turn(inner[b][c], b * c) for b in range(4)])
        for d in range(4):
            out[c + 4 * d] = row[d]
    return out


def channel_kernel(first_ref, x0, x1, x2, x3, x4, window, twist, table, out, turned, spectrum):
    xs = (x0, x1, x2, x3, x4)
    step = pl.program_id(0)
    block = 16

    def columns(half, carry):
        base = half * LANES
        lanes2 = pl.ds(pl.multiple_of(base, LANES), LANES)
        for s in range(2):
            for r in range(2):
                series = []
                for n in range(R1):
                    lanes = pl.ds(pl.multiple_of(base + n * R2, LANES), LANES)
                    parts = []
                    for c in range(2):
                        total = None
                        for tap in range(TAPS):
                            value = xs[s + tap][c, :, lanes].astype(jnp.float32)[8 * r : 8 * r + 8]
                            term = window[tap, :, lanes] * value
                            total = term if total is None else total + term
                        parts.append(total.astype(jnp.bfloat16).astype(jnp.float32))
                    series.append(tuple(parts))
                result = sixteen(series)
                row = pl.multiple_of(step * block + s * 64 + 8 * r, 8)
                for m in range(R1):
                    re, im = result[m]
                    cosine, sine = twist[0, m, :, lanes2], twist[1, m, :, lanes2]
                    turned[m, pl.ds(row, 8), lanes2] = re * cosine + im * sine
                    turned[m, pl.ds(row, 8), pl.ds(pl.multiple_of(base + R2, LANES), LANES)] = (
                        im * cosine - re * sine
                    )
        return carry

    lax.fori_loop(0, R2 // LANES, columns, 0)

    @pl.when(step == pl.num_programs(0) - 1)
    def _():
        weights = table[...]
        for m in range(0, R1, 2):
            pair = turned[m : m + 2].reshape(2 * LANES, 2 * R2).astype(jnp.bfloat16)
            result = lax.dot_general(
                weights, pair, (((1,), (1,)), ((), ())), preferred_element_type=jnp.float32
            )
            for d in range(2):
                for e in range(2):
                    spectrum[d, pl.ds(m + e, R2, stride=R1), :] = result[
                        d * R2 : (d + 1) * R2, e * LANES : (e + 1) * LANES
                    ]

        def place(slot, carry):
            start = pl.multiple_of(first_ref[slot], 8)
            both = [spectrum[d, pl.ds(start, AVG), :] for d in range(2)]
            out[slot] = jnp.concatenate(both, axis=0).astype(jnp.bfloat16)
            return carry

        lax.fori_loop(0, out.shape[0], place, 0, unroll=4)


def channel_call(first, xs, window, twist, table):
    slots = first.shape[0]
    block = 16
    steps = xs[0].shape[1] // block
    spec = pl.BlockSpec((2, block, F), lambda i, *_: (0, i, 0))
    whole = lambda shape: pl.BlockSpec(shape, lambda i, *_: (0,) * len(shape))
    return pl.pallas_call(
        channel_kernel,
        out_shape=jax.ShapeDtypeStruct((slots, 2 * AVG, LANES), jnp.bfloat16),
        grid_spec=pltpu.PrefetchScalarGridSpec(
            num_scalar_prefetch=1,
            grid=(steps,),
            in_specs=[spec] * 5 + [whole(window.shape), whole(twist.shape), whole(table.shape)],
            out_specs=whole((slots, 2 * AVG, LANES)),
            scratch_shapes=[
                pltpu.VMEM((R1, LANES, 2 * R2), jnp.float32),
                pltpu.VMEM((2, F, LANES), jnp.float32),
            ],
        ),
        compiler_params=pltpu.CompilerParams(vmem_limit_bytes=48 * 2**20),
        cost_estimate=pl.CostEstimate(flops=2 * 10**9, bytes_accessed=9 * 2**20, transcendentals=0),
        name="channels",
    )(first, *xs, window, twist, table)


def correlate_kernel(n_inp, n_tim, valid_ref, *refs):
    chunks = len(refs) - 3
    pieces, out, rows_k, rows_i = refs[:chunks], refs[chunks], refs[chunks + 1], refs[chunks + 2]
    slot = pl.program_id(0)
    width = out.shape[1]
    depth = rows_k.shape[1]
    inverse = 1.0 / depth

    @pl.when(valid_ref[slot] == 0)
    def _():
        out[...] = jnp.zeros_like(out)

    @pl.when(valid_ref[slot] != 0)
    def _():
        low = lax.broadcasted_iota(jnp.int32, (2 * AVG, LANES), 1) < LANES // 2

        def arrange(q, carry):
            lanes = pl.ds(pl.multiple_of(q * LANES, LANES), LANES)
            for chunk in range(chunks):
                for u in range(n_tim // 2):
                    group = [
                        [
                            pieces[chunk][(2 * q + e) * n_tim + 2 * u + v, 0].astype(jnp.float32)
                            for v in range(2)
                        ]
                        for e in range(2)
                    ]
                    for c in range(2):
                        even, odd = [
                            jnp.concatenate([group[e][v][AVG * c : AVG * c + AVG] for v in range(2)], axis=0)
                            for e in range(2)
                        ]
                        first = jnp.where(low, even, pltpu.roll(odd, LANES // 2, 1))
                        second = jnp.where(low, pltpu.roll(even, LANES // 2, 1), odd)
                        base = (chunk * (n_tim // 2) + u) * 4 * AVG
                        rows_k[c, base : base + 2 * AVG, lanes] = first.astype(jnp.bfloat16)
                        rows_k[c, base + 2 * AVG : base + 4 * AVG, lanes] = second.astype(jnp.bfloat16)
            for c in range(2):
                rows_i[c, lanes, :] = rows_k[c, :, lanes].T
            return carry

        lax.fori_loop(0, width // LANES, arrange, 0)
        tile = 256
        upper = lax.broadcasted_iota(jnp.int32, (tile, tile), 0) <= lax.broadcasted_iota(
            jnp.int32, (tile, tile), 1
        )

        def dot(a, b):
            return jnp.dot(a, b, preferred_element_type=jnp.float32)

        for i in range(width // tile):
            re_i, im_i = [rows_i[c, i * tile : (i + 1) * tile, :] for c in range(2)]
            for j in range(width // tile):
                re_j, im_j = [rows_k[c, :, j * tile : (j + 1) * tile] for c in range(2)]
                real = imag = None
                if i <= j:
                    real = dot(re_i, re_j) + dot(im_i, im_j)
                if i >= j:
                    imag = dot(im_i, re_j) - dot(re_i, im_j)
                value = real if imag is None else imag if real is None else jnp.where(upper, real, imag)
                out[0, i * tile : (i + 1) * tile, j * tile : (j + 1) * tile] = value * inverse


def correlate_call(n_inp, n_tim, valid, pieces):
    width = n_inp * LANES // 2
    depth = n_tim * len(pieces) * 2 * AVG
    pieces = [p.reshape(n_inp * n_tim, CAP, 2 * AVG, LANES) for p in pieces]
    return pl.pallas_call(
        functools.partial(correlate_kernel, n_inp, n_tim),
        out_shape=jax.ShapeDtypeStruct((CAP, width, width), jnp.float32),
        grid_spec=pltpu.PrefetchScalarGridSpec(
            num_scalar_prefetch=1,
            grid=(CAP,),
            in_specs=[pl.BlockSpec((n_inp * n_tim, 1, 2 * AVG, LANES), lambda s, *_: (0, s, 0, 0))]
            * len(pieces),
            out_specs=pl.BlockSpec((1, width, width), lambda s, *_: (s, 0, 0)),
            scratch_shapes=[
                pltpu.VMEM((2, depth, width), jnp.bfloat16),
                pltpu.VMEM((2, width, depth), jnp.bfloat16),
            ],
        ),
        compiler_params=pltpu.CompilerParams(vmem_limit_bytes=48 * 2**20),
        cost_estimate=pl.CostEstimate(flops=10**10, bytes_accessed=15 * 2**20, transcendentals=0),
        name="correlate",
    )(valid, *pieces)


def body(voltages, scale_exps, owner_table):
    n_inp = lax.axis_size("inp")
    n_tim = lax.axis_size("tim")
    devices = n_inp * n_tim
    spec_dev = voltages.shape[2] // F
    scale = jnp.exp2(scale_exps.astype(jnp.float32)) / 128.0
    own = [
        (voltages[:, :, s * F : (s + 1) * F].astype(jnp.float32) * scale[None, :, s : s + 1]).astype(
            jnp.bfloat16
        )
        for s in range(spec_dev)
    ]
    ahead = [(source, source + 1) for source in range(n_tim - 1)]
    before = {s: lax.ppermute(own[s], "tim", ahead) for s in (3, 2, 1)}

    rows = owner_rows(owner_table, CAP)
    match = rows[None, :] == jnp.arange(devices * CAP, dtype=jnp.int32)[:, None]
    valid = jnp.any(match, axis=1).astype(jnp.int32)
    which = jnp.sum(jnp.where(match, jnp.arange(CH, dtype=jnp.int32)[None, :], 0), axis=1)
    first = (which * AVG - AVG * CH // 2) % F
    me = lax.axis_index("inp") * n_tim + lax.axis_index("tim")
    mine = lax.dynamic_slice(valid, (me * CAP,), (CAP,))

    window = jnp.asarray(window_table())
    twist = jnp.asarray(twist_table())
    table = jnp.asarray(radix_table()).astype(jnp.bfloat16)

    late = channel_call(first, (before[3], own[0], own[1], own[2], own[3]), window, twist, table)
    late = lax.all_to_all(late, ("inp", "tim"), split_axis=0, concat_axis=0, tiled=True)
    early = channel_call(first, (before[1], before[2], before[3], own[0], own[1]), window, twist, table)
    early = lax.all_to_all(early, ("inp", "tim"), split_axis=0, concat_axis=0, tiled=True)
    return correlate_call(n_inp, n_tim, mine, [late, early])


def solution(mesh):
    return jax.shard_map(
        body,
        mesh=mesh,
        in_specs=(P(None, "inp", "tim"), P("inp", "tim"), P()),
        out_specs=P(("inp", "tim"), None, None),
        check_vma=False,
    )
```

time: 534 us -> 185 us (0.35)
  the two profiles are of different devices: /device:TPU:1 before, /device:TPU:32 now
where the time goes in v1:
time: 185 us
  starting transfers between devices  68.4 us (37%)
  waiting for transfers between devices  65.7 us (36%)
  Pallas kernels  39.7 us (21%)
  other arithmetic  6 us (3%)
  local copies, waits for them, and re-layouts  4.87 us (3%)
    all_to_all x1, waiting for transfers between devices, body(): lax.all_to_all(early, ('inp', 'tim'), split_axis=0, concat_axis=0, tiled=...  41.1 us
    all_to_all x1, starting transfers between devices, body(): lax.all_to_all(early, ('inp', 'tim'), split_axis=0, concat_axis=0, tiled=...  38.3 us
    all_to_all x1, starting transfers between devices, body(): lax.all_to_all(late, ('inp', 'tim'), split_axis=0, concat_axis=0, tiled=T...  22.8 us
    pallas_call x2, Pallas kernels, channel_call(): pl.pallas_call(channel_kernel, out_shape=jax.ShapeDtypeStruct((slots, 2 *...  21.6 us
    all_to_all x1, waiting for transfers between devices, body(): lax.all_to_all(late, ('inp', 'tim'), split_axis=0, concat_axis=0, tiled=T...  20.5 us
    pallas_call x1, Pallas kernels, correlate_call(): pl.pallas_call(functools.partial(correlate_kernel, n_inp, n_tim), out_sha...  18.2 us
    ppermute x3, starting transfers between devices, body(): before = {s: lax.ppermute(own[s], 'tim', ahead) for s in (3, 2, 1)}  7.33 us
    convert_element_type x1, other arithmetic, body(): (voltages[:, :, s * F:(s + 1) * F].astype(jnp.float32) * scale[None, :, s...  4.89 us
  transfers between devices with their start and end apart: 5, of which 4 were waited for; matrix products, arithmetic and copies ran while one was open for 0% of the time, Pallas kernels for 6%

profile of v1, /device:TPU:32, one launch (start us, length us, event | category | flops | bytes accessed | tf_op | source)
XLA Modules:
  0.0 184.8 jit_solution(12346482165222295701)
XLA Ops:
  0.0 0.7 exponential_multiply_fusion
  0.7 0.0 copy-start.9
  0.7 0.0 copy-start.2
  0.7 0.0 copy-start.4
  0.7 0.0 copy-start.6
  0.7 4.9 %multiply_convert_fusion = (bf16[2,64,4096]{2,1,0:T(8,128)(2,1)S(1)}, bf16[2,64,4096]{2,1,0:T(8,128)(2,1)S(1)}, bf16[2,64,4096]{2,1,0:T(8,128)(2,1)S(1)}, bf16[2,64,4096]{2,1,0:T(8,128)(2,1)S(1)}) fusion(s32[2,64,16384]{2,1,0:T(8,128)} %param.6, f32[64]{0:T(128)S(1)} %get-tuple-element.9, f32[64]{0:T(128)S(1)} %get-tuple-element.11, ...), kind=kLoop, calls=%fused_computation | loop fusion | flops 6291456 | bytes 12583936 | tf_op jit(solution)/shard_map/convert_element_type | solution.py:267
  5.6 0.0 copy-start.7
  5.6 0.0 copy-start
  5.7 1.8 collective-permute-start
  7.5 0.0 copy-done.9
  7.5 0.2 convert_reduce_fusion
  7.7 0.1 select_reduce_fusion
  7.8 1.9 %collective-permute-done.x0.x2 = bf16[2,64,4096]{2,1,0:T(8,128)(2,1)S(1)} collective-permute-done((bf16[2,64,4096]{2,1,0:T(8,128)(2,1)S(1)}, bf16[2,64,4096]{2,1,0:T(8,128)(2,1)S(1)}, u32[]{:S(2)}, u32[]{:S(2)}) %collective-permute-start) | collective-permute-done | bytes 1048608 | tf_op jit(solution)/shard_map/ppermute | solution.py:273
  9.7 0.0 copy-done.7
  9.7 0.0 copy-done.2
  9.7 0.0 copy-done.4
  9.7 0.0 copy-done.6
  9.7 10.8 %channels.2 = bf16[256,48,128]{2,1,0:T(8,128)(2,1)} custom-call(s32[256]{0:T(256)S(1)} %and_select_fusion.first_ref, bf16[2,64,4096]{2,1,0:T(8,128)(2,1)S(1)} %collective-permute-done.x0.x2, bf16[2,64,4096]{2,1,0:T(8,128)(2,1)S(1)} %get-tuple-element.6.x1.x3, bf16[2,64,4096]{2,1,0:T(8,128)(2,1)S(1)} %get-tuple-element.8.x2.x4, ...), custom_call_target="tpu_custom_call" | custom-call | flops 2000000000 | bytes 9437184 | tf_op jit(solution)/shard_map/channels/pallas_call | solution.py:154
  20.5 0.0 copy-start.1
  20.5 1.0 copy-done.1
  21.5 22.8 %all-to-all-start = ((bf16[256,48,128]{2,1,0:T(8,128)(2,1)}), bf16[256,48,128]{2,1,0:T(8,128)(2,1)}, u32[]{:S(2)}, u32[]{:S(2)}) async-start(bf16[256,48,128]{2,1,0:T(8,128)(2,1)} %channels.2), calls=%async_computation | async-start | bytes 6291456 | tf_op jit(solution)/shard_map/all_to_all | solution.py:288
  44.2 2.1 %collective-permute-start.2 = (bf16[2,64,4096]{2,1,0:T(8,128)(2,1)}, bf16[2,64,4096]{2,1,0:T(8,128)(2,1)S(1)}, u32[]{:S(2)}, u32[]{:S(2)}) collective-permute-start(bf16[2,64,4096]{2,1,0:T(8,128)(2,1)} %copy-done.1), channel_id=1, source_target_pairs={{0,1},{1,2},{2,3},{3,4},{4,5},{5,6},{6,7},{8,9},{9,10},{10,11},{11... | collective-permute-start | bytes 3145736 | tf_op jit(solution)/shard_map/ppermute | solution.py:273
  46.3 0.0 copy-done
  46.3 3.4 %collective-permute-start.1 = (bf16[2,64,4096]{2,1,0:T(8,128)(2,1)S(1)}, bf16[2,64,4096]{2,1,0:T(8,128)(2,1)S(1)}, u32[]{:S(2)}, u32[]{:S(2)}) collective-permute-start(bf16[2,64,4096]{2,1,0:T(8,128)(2,1)S(1)} %get-tuple-element.8.x2.x4), channel_id=1, source_target_pairs={{0,1},{1,2},{2,3},{3,4},{4,5},{5,6},{6,7},{8,9},{9,10},{10,11},{11... | collective-permute-start | bytes 3145736 | tf_op jit(solution)/shard_map/ppermute | solution.py:273
  49.8 0.0 collective-permute-done.2.x1
  49.8 2.2 %collective-permute-done.1.x0 = bf16[2,64,4096]{2,1,0:T(8,128)(2,1)S(1)} collective-permute-done((bf16[2,64,4096]{2,1,0:T(8,128)(2,1)S(1)}, bf16[2,64,4096]{2,1,0:T(8,128)(2,1)S(1)}, u32[]{:S(2)}, u32[]{:S(2)}) %collective-permute-start.1) | collective-permute-done | bytes 1048608 | tf_op jit(solution)/shard_map/ppermute | solution.py:273
  52.0 0.0 copy-start.3
  52.0 1.0 copy-done.3
  53.0 0.0 copy-start.5
  53.0 1.0 copy-done.5
  54.0 10.8 %channels.3 = bf16[256,48,128]{2,1,0:T(8,128)(2,1)} custom-call(s32[256]{0:T(256)S(1)} %and_select_fusion.first_ref, bf16[2,64,4096]{2,1,0:T(8,128)(2,1)S(1)} %collective-permute-done.1.x0, bf16[2,64,4096]{2,1,0:T(8,128)(2,1)S(1)} %collective-permute-done.2.x1, bf16[2,64,4096]{2,1,0:T(8,128)(2,1)S(1)} %collective-permute-done.x0.x2, ...), custom_call_target="tpu_custom_call" | custom-call | flops 2000000000 | bytes 9437184 | tf_op jit(solution)/shard_map/channels/pallas_call | solution.py:154
  64.8 20.5 %all-to-all-done = bf16[256,48,128]{2,1,0:T(8,128)(2,1)} async-done(((bf16[256,48,128]{2,1,0:T(8,128)(2,1)}), bf16[256,48,128]{2,1,0:T(8,128)(2,1)}, u32[]{:S(2)}, u32[]{:S(2)}) %all-to-all-start) | async-done | bytes 3145760 | tf_op jit(solution)/shard_map/all_to_all | solution.py:288
  85.3 38.3 %all-to-all-start.1 = ((bf16[256,48,128]{2,1,0:T(8,128)(2,1)}), bf16[256,48,128]{2,1,0:T(8,128)(2,1)S(1)}, u32[]{:S(2)}, u32[]{:S(2)}) async-start(bf16[256,48,128]{2,1,0:T(8,128)(2,1)} %channels.3), calls=%async_computation.1 | async-start | bytes 6291456 | tf_op jit(solution)/shard_map/all_to_all | solution.py:290
  123.7 0.1 fusion
  123.8 0.1 dynamic_slice.3.valid_ref
  123.9 41.1 %all-to-all-done.1 = bf16[256,48,128]{2,1,0:T(8,128)(2,1)S(1)} async-done(((bf16[256,48,128]{2,1,0:T(8,128)(2,1)}), bf16[256,48,128]{2,1,0:T(8,128)(2,1)S(1)}, u32[]{:S(2)}, u32[]{:S(2)}) %all-to-all-start.1) | async-done | bytes 3145760 | tf_op jit(solution)/shard_map/all_to_all | solution.py:290
  165.0 0.0 copy-start.8
  165.0 1.7 copy-done.8
  166.7 18.2 %correlate.1 = f32[2,1024,1024]{2,1,0:T(8,128)} custom-call(s32[2]{0:T(128)S(1)} %dynamic_slice.3.valid_ref, bf16[128,2,48,128]{3,2,1,0:T(8,128)(2,1)} %bitcast.4.refs_0_, bf16[128,2,48,128]{3,2,1,0:T(8,128)(2,1)} %bitcast.10), custom_call_target="tpu_custom_call" | custom-call | flops 10000000000 | bytes 15728640 | tf_op jit(solution)/shard_map/correlate/pallas_call | solution.py:240
  (4 shorter events, 0.0 us)
Async XLA Ops:
  0.7 6.8 %copy-start.9 = (s32[144]{0:T(256)S(1)}, s32[144]{0:T(256)}, u32[]{:S(2)}) copy-start(s32[144]{0:T(256)} %param.8) | copy-start | bytes 1732
  0.7 9.0 %copy-start.2 = (bf16[512,512]{1,0:T(8,128)(2,1)S(1)}, bf16[512,512]{1,0:T(8,128)(2,1)}, u32[]{:S(2)}) copy-start(bf16[512,512]{1,0:T(8,128)(2,1)} %constant.54.table) | copy-start | bytes 1572868
  0.7 9.0 %copy-start.4 = (f32[4,8,4096]{2,1,0:T(8,128)S(1)}, f32[4,8,4096]{2,1,0:T(8,128)}, u32[]{:S(2)}) copy-start(f32[4,8,4096]{2,1,0:T(8,128)} %constant.50.clone.window) | copy-start | bytes 1572868
  0.7 9.0 %copy-start.6 = (f32[2,16,8,256]{3,2,1,0:T(8,128)S(1)}, f32[2,16,8,256]{3,2,1,0:T(8,128)}, u32[]{:S(2)}) copy-start(f32[2,16,8,256]{3,2,1,0:T(8,128)} %constant.51.clone.twist) | copy-start | bytes 786436
  5.6 4.0 %copy-start.7 = (bf16[2,64,4096]{2,1,0:T(8,128)(2,1)}, bf16[2,64,4096]{2,1,0:T(8,128)(2,1)S(1)}, u32[]{:S(2)}) copy-start(bf16[2,64,4096]{2,1,0:T(8,128)(2,1)S(1)} %get-tuple-element.7.x4) | copy-start | bytes 3145732
  5.6 40.7 %copy-start = (bf16[2,64,4096]{2,1,0:T(8,128)(2,1)}, bf16[2,64,4096]{2,1,0:T(8,128)(2,1)S(1)}, u32[]{:S(2)}) copy-start(bf16[2,64,4096]{2,1,0:T(8,128)(2,1)S(1)} %get-tuple-element.8.x2.x4) | copy-start | bytes 3145732
  5.7 4.0 %collective-permute-start = (bf16[2,64,4096]{2,1,0:T(8,128)(2,1)S(1)}, bf16[2,64,4096]{2,1,0:T(8,128)(2,1)S(1)}, u32[]{:S(2)}, u32[]{:S(2)}) collective-permute-start(bf16[2,64,4096]{2,1,0:T(8,128)(2,1)S(1)} %get-tuple-element.7.x4), channel_id=1, source_target_pairs={{0,1},{1,2},{2,3},{3,4},{4,5},{5,6},{6,7},{8,9},{9,10},{10,11},{11... | collective-permute-start | bytes 3145736 | tf_op jit(solution)/shard_map/ppermute | solution.py:273
  20.5 1.0 copy-start.1
  21.5 63.9 %all-to-all-start = ((bf16[256,48,128]{2,1,0:T(8,128)(2,1)}), bf16[256,48,128]{2,1,0:T(8,128)(2,1)}, u32[]{:S(2)}, u32[]{:S(2)}) async-start(bf16[256,48,128]{2,1,0:T(8,128)(2,1)} %channels.2), calls=%async_computation | async-start | bytes 6291456 | tf_op jit(solution)/shard_map/all_to_all | solution.py:288
  44.2 5.6 %collective-permute-start.2 = (bf16[2,64,4096]{2,1,0:T(8,128)(2,1)}, bf16[2,64,4096]{2,1,0:T(8,128)(2,1)S(1)}, u32[]{:S(2)}, u32[]{:S(2)}) collective-permute-start(bf16[2,64,4096]{2,1,0:T(8,128)(2,1)} %copy-done.1), channel_id=1, source_target_pairs={{0,1},{1,2},{2,3},{3,4},{4,5},{5,6},{6,7},{8,9},{9,10},{10,11},{11... | collective-permute-start | bytes 3145736 | tf_op jit(solution)/shard_map/ppermute | solution.py:273
  46.3 5.6 %collective-permute-start.1 = (bf16[2,64,4096]{2,1,0:T(8,128)(2,1)S(1)}, bf16[2,64,4096]{2,1,0:T(8,128)(2,1)S(1)}, u32[]{:S(2)}, u32[]{:S(2)}) collective-permute-start(bf16[2,64,4096]{2,1,0:T(8,128)(2,1)S(1)} %get-tuple-element.8.x2.x4), channel_id=1, source_target_pairs={{0,1},{1,2},{2,3},{3,4},{4,5},{5,6},{6,7},{8,9},{9,10},{10,11},{11... | collective-permute-start | bytes 3145736 | tf_op jit(solution)/shard_map/ppermute | solution.py:273
  52.0 1.0 copy-start.3
  53.0 1.0 copy-start.5
  85.3 79.7 %all-to-all-start.1 = ((bf16[256,48,128]{2,1,0:T(8,128)(2,1)}), bf16[256,48,128]{2,1,0:T(8,128)(2,1)S(1)}, u32[]{:S(2)}, u32[]{:S(2)}) async-start(bf16[256,48,128]{2,1,0:T(8,128)(2,1)} %channels.3), calls=%async_computation.1 | async-start | bytes 6291456 | tf_op jit(solution)/shard_map/all_to_all | solution.py:290
  165.0 1.7 copy-start.8

commit v2 on v1

v2 whole, which is shorter than its diff:
```python
import functools
import math

import jax
import jax.numpy as jnp
import numpy as np
from jax import lax
from jax.experimental import pallas as pl
from jax.experimental.pallas import tpu as pltpu
from jax.sharding import PartitionSpec as P

F = 4096
AVG = 24
CH = 144
TAPS = 4
CAP = 2
R1 = 16
R2 = 256
LANES = 128
VMEM = 60 * 2**20
MIXED = 16


def window_table():
    length = TAPS * F
    steps = np.arange(length, dtype=np.float64)
    centre = (steps + 0.5 - length / 2.0) / F
    taper = 0.5 - 0.5 * np.cos(2.0 * math.pi * (steps + 0.5) / length)
    table = (np.sinc(centre) * taper).reshape(TAPS, 1, F)
    table = np.concatenate([table, np.zeros((1, 1, F))], axis=0)
    return np.broadcast_to(table, (TAPS + 1, 8, F)).astype(np.float32)


def twist_table():
    phase = np.arange(R1)[:, None] * np.arange(R2)[None, :]
    angle = 2.0 * math.pi * phase / F
    table = np.stack([np.cos(angle), np.sin(angle)]) / math.sqrt(F)
    return np.broadcast_to(table[:, :, None, :], (2, R1, 8, R2)).astype(np.float32)


def radix_table():
    phase = np.arange(R2)[:, None] * np.arange(R2)[None, :] % R2
    angle = 2.0 * math.pi * phase / R2
    cosine, sine = np.cos(angle), np.sin(angle)
    table = np.concatenate(
        [np.concatenate([cosine, sine], axis=1), np.concatenate([-sine, cosine], axis=1)], axis=0
    )
    return table.astype(np.float32)


def owner_rows(owner_table, cap):
    index = jnp.arange(owner_table.shape[0], dtype=jnp.int32)
    same = owner_table[:, None] == owner_table[None, :]
    earlier = index[None, :] < index[:, None]
    slot = jnp.sum((same & earlier).astype(jnp.int32), axis=1)
    return owner_table * cap + slot


def four(a, b, c, d):
    sr, si = a[0] + c[0], a[1] + c[1]
    tr, ti = a[0] - c[0], a[1] - c[1]
    ur, ui = b[0] + d[0], b[1] + d[1]
    vr, vi = b[0] - d[0], b[1] - d[1]
    return (sr + ur, si + ui), (tr + vi, ti - vr), (sr - ur, si - ui), (tr - vi, ti + vr)


def turn(value, power):
    re, im = value
    power %= 16
    if power == 0:
        return value
    if power == 4:
        return im, -re
    root = math.sqrt(0.5)
    if power == 2:
        return (re + im) * root, (im - re) * root
    if power == 6:
        return (im - re) * root, (re + im) * (-root)
    cosine, sine = math.cos(2 * math.pi * power / 16), math.sin(2 * math.pi * power / 16)
    return re * cosine + im * sine, im * cosine - re * sine


def sixteen(x):
    inner = [four(x[b], x[4 + b], x[8 + b], x[12 + b]) for b in range(4)]
    out = [None] * 16
    for c in range(4):
        row = four(*[turn(inner[b][c], b * c) for b in range(4)])
        for d in range(4):
            out[c + 4 * d] = row[d]
    return out


def channel_kernel(plans, count, first_ref, *refs):
    xs, (window, twist, table) = refs[:count], refs[count : count + 3]
    prior, (out, turned, spectrum) = refs[count + 3 : -3], refs[-3:]
    step = pl.program_id(0)
    spectra = len(plans[0])
    block = xs[0].shape[1]
    inputs = turned.shape[1] // spectra
    slots = out.shape[0] * out.shape[1]
    wrapped = first_ref[slots] != 0

    def columns(plan, half):
        base = half * LANES
        lanes2 = pl.ds(pl.multiple_of(base, LANES), LANES)
        lanes3 = pl.ds(pl.multiple_of(base + R2, LANES), LANES)
        for s, (blocks, cut) in enumerate(plan):
            for r in range(block // 8):
                series = []
                for n in range(R1):
                    lanes = pl.ds(pl.multiple_of(base + n * R2, LANES), LANES)
                    parts = []
                    for c in range(2):
                        total = None
                        for tap in range(TAPS):
                            index, part = blocks[tap]
                            value = xs[index][part + c, :, lanes].astype(jnp.float32)[8 * r : 8 * r + 8]
                            which = tap if tap >= cut else jnp.where(wrapped, TAPS, tap)
                            term = window[which, :, lanes] * value
                            total = term if total is None else total + term
                        parts.append(total.astype(jnp.bfloat16).astype(jnp.float32))
                    series.append(tuple(parts))
                result = sixteen(series)
                row = pl.ds(pl.multiple_of(step * block + s * inputs + 8 * r, 8), 8)
                for m in range(R1):
                    re, im = result[m]
                    cosine, sine = twist[0, m, :, lanes2], twist[1, m, :, lanes2]
                    turned[m, row, lanes2] = re * cosine + im * sine
                    turned[m, row, lanes3] = im * cosine - re * sine

    def filtered(plan):
        lax.fori_loop(0, R2 // LANES, lambda half, carry: (columns(plan, half), carry)[1], 0)

    if len(plans) == 1:
        filtered(plans[0])
    else:
        pl.when(step == 0)(lambda: filtered(plans[0]))
        pl.when(step != 0)(lambda: filtered(plans[1]))

    @pl.when(step == pl.num_programs(0) - 1)
    def _():
        weights = table[...]
        low = lax.broadcasted_iota(jnp.int32, (R2, LANES), 1) < LANES // 2
        many = 4
        for m in range(0, R1, many):
            rows = turned[m : m + many].reshape(many * spectra * inputs, 2 * R2).astype(jnp.bfloat16)
            result = lax.dot_general(
                weights, rows, (((1,), (1,)), ((), ())), preferred_element_type=jnp.float32
            )
            for tile in range(many * spectra // 2):
                lanes = slice(tile * LANES, (tile + 1) * LANES)
                re, im = result[:R2, lanes], result[R2:, lanes]
                pair = (
                    jnp.where(low, re, pltpu.roll(im, LANES // 2, 1)),
                    jnp.where(low, pltpu.roll(re, LANES // 2, 1), im),
                )
                for e in range(2):
                    more, s = divmod(2 * tile + e, spectra)
                    spectrum[s, pl.ds(m + more, R2, stride=R1), :] = pair[e]

        def place(owner, carry):
            for slot in range(CAP):
                start = pl.multiple_of(first_ref[owner * CAP + slot], 8)
                rows = [p[owner, slot].astype(jnp.float32) for p in prior]
                rows += [spectrum[s, pl.ds(start, AVG), :] for s in range(spectra)]
                rows = rows[0] if len(rows) == 1 else jnp.concatenate(rows, axis=0)
                out[owner, slot] = rows.astype(jnp.bfloat16)
            return carry

        lax.fori_loop(0, out.shape[0], place, 0, unroll=2)


def channel_call(plans, first, xs, window, twist, table, prior=()):
    owners = (first.shape[0] - 1) // CAP
    block = 16
    inputs = max(x.shape[1] for x in xs)
    spectra = len(plans[0])

    def spec(x):
        skip, most = (inputs - x.shape[1]) // block, x.shape[1] // block - 1
        if most == 0:
            skip = 0
        return pl.BlockSpec((x.shape[0], block, F), lambda i, *_: (0, jnp.clip(i - skip, 0, most), 0))

    whole = lambda shape: pl.BlockSpec(shape, lambda i, *_: (0,) * len(shape))
    shape = (owners, CAP, (spectra + len(prior)) * AVG, LANES)
    return pl.pallas_call(
        functools.partial(channel_kernel, plans, len(xs)),
        out_shape=jax.ShapeDtypeStruct(shape, jnp.bfloat16),
        grid_spec=pltpu.PrefetchScalarGridSpec(
            num_scalar_prefetch=1,
            grid=(inputs // block,),
            in_specs=[spec(x) for x in xs] + [whole(x.shape) for x in (window, twist, table, *prior)],
            out_specs=whole(shape),
            scratch_shapes=[
                pltpu.VMEM((R1, spectra * inputs, 2 * R2), jnp.float32),
                pltpu.VMEM((spectra, F, LANES), jnp.float32),
            ],
        ),
        compiler_params=pltpu.CompilerParams(vmem_limit_bytes=VMEM),
        cost_estimate=pl.CostEstimate(flops=10**9 * spectra, bytes_accessed=8 * 2**20, transcendentals=0),
        name="channels",
    )(first, *xs, window, twist, table, *prior)


def correlate_kernel(n_tim, mixed, scale, valid_ref, piece, *refs):
    partial = refs[0] if len(refs) == 4 else None
    out, rows_k, rows_i = refs[-3:]
    slot, block = pl.program_id(0), pl.program_id(1)
    depth, width = rows_k.shape[1], rows_k.shape[2]
    tile = out.shape[1]
    blocks = width // tile
    half = depth // 2

    def arrange(which, q):
        lane = lax.broadcasted_iota(jnp.int32, (2 * AVG, LANES), 1)
        low, ahead = lane < LANES // 2, lane % (LANES // 2) < mixed
        lanes = pl.ds(pl.multiple_of(q * LANES, LANES), LANES)

        def rows(e, t):
            value = piece[(2 * q + e) * n_tim + t, which].astype(jnp.float32)
            if mixed:
                other = piece[(2 * q + e) * n_tim + (t + 1) % n_tim, which].astype(jnp.float32)
                value = jnp.where(ahead, other, value)
            return value

        base = 0
        for u in range(n_tim // 2):
            group = [[rows(e, 2 * u + v) for v in range(2)] for e in range(2)]
            for s in range(piece.shape[2] // AVG):
                even, odd = [
                    jnp.concatenate([group[e][v][AVG * s : AVG * s + AVG] for v in range(2)], axis=0)
                    for e in range(2)
                ]
                re = jnp.where(low, even, pltpu.roll(odd, LANES // 2, 1))
                im = jnp.where(low, pltpu.roll(even, LANES // 2, 1), odd)
                rows_k[which, base : base + 2 * AVG, lanes] = re.astype(jnp.bfloat16)
                rows_k[which, half + base : half + base + 2 * AVG, lanes] = im.astype(jnp.bfloat16)
                base += 2 * AVG
        turned = rows_k[which, :, lanes].T
        rows_i[which, lanes, :depth] = turned
        rows_i[which, lanes, depth:] = -turned[:, :half]

    @pl.when(jnp.logical_and(slot == 0, block == 0))
    def _():
        lax.fori_loop(0, width // LANES, lambda q, carry: (arrange(0, q), carry)[1], 0)

    def strip(which, i):
        upper = lax.broadcasted_iota(jnp.int32, (tile, tile), 0) <= lax.broadcasted_iota(
            jnp.int32, (tile, tile), 1
        )
        keep = valid_ref[which] != 0
        rows = slice(i * tile, (i + 1) * tile)
        for j in range(blocks):
            lanes = slice(j * tile, (j + 1) * tile)
            other = rows_k[which, :, lanes]
            real = imag = None
            if i <= j:
                real = jnp.dot(rows_i[which, rows, :depth], other, preferred_element_type=jnp.float32)
            if i >= j:
                imag = jnp.dot(rows_i[which, rows, half:], other, preferred_element_type=jnp.float32)
            value = real if imag is None else imag if real is None else jnp.where(upper, real, imag)
            if partial is not None:
                value = value + partial[0, :, lanes]
            out[0, :, lanes] = jnp.where(keep, value * scale, 0.0)

    each = width // LANES // blocks
    for which in range(CAP):
        for i in range(blocks):

            @pl.when(jnp.logical_and(slot == which, block == i))
            def _():
                if which + 1 < CAP:
                    for q in range(each):
                        arrange(which + 1, i * each + q)
                strip(which, i)


def correlate_call(n_inp, n_tim, mixed, scale, valid, piece, partial=None):
    width = n_inp * LANES // 2
    depth = n_tim * piece.shape[2] * 2
    tile = 256
    block = pl.BlockSpec((1, tile, width), lambda s, i, *_: (s, i, 0))
    more = [] if partial is None else [partial]
    return pl.pallas_call(
        functools.partial(correlate_kernel, n_tim, mixed, scale),
        out_shape=jax.ShapeDtypeStruct((CAP, width, width), jnp.float32),
        grid_spec=pltpu.PrefetchScalarGridSpec(
            num_scalar_prefetch=1,
            grid=(CAP, width // tile),
            in_specs=[pl.BlockSpec(piece.shape, lambda s, i, *_: (0, 0, 0, 0))] + [block] * len(more),
            out_specs=block,
            scratch_shapes=[
                pltpu.VMEM((CAP, depth, width), jnp.bfloat16),
                pltpu.VMEM((CAP, width, depth + depth // 2), jnp.bfloat16),
            ],
        ),
        compiler_params=pltpu.CompilerParams(vmem_limit_bytes=VMEM),
        cost_estimate=pl.CostEstimate(flops=5 * 10**9, bytes_accessed=19 * 2**20, transcendentals=0),
        name="correlate",
    )(valid, piece, *more)


def body(voltages, scale_exps, owner_table):
    n_inp = lax.axis_size("inp")
    n_tim = lax.axis_size("tim")
    devices = n_inp * n_tim
    spec_dev = voltages.shape[2] // F
    scale = jnp.exp2(scale_exps.astype(jnp.float32)) / 128.0
    own = [
        (voltages[:, :, s * F : (s + 1) * F].astype(jnp.float32) * scale[None, :, s : s + 1]).astype(
            jnp.bfloat16
        )
        for s in range(spec_dev)
    ]
    ahead = [(source, source + 1) for source in range(n_tim - 1)]
    back = [(source, (source - 1) % n_tim) for source in range(n_tim)]
    before = lax.ppermute(own[3], "tim", ahead)
    earlier = lax.ppermute(jnp.concatenate([own[1][:, :MIXED], own[2][:, :MIXED]]), "tim", ahead)
    after = lax.ppermute(jnp.concatenate([own[0][:, MIXED:], own[1][:, MIXED:]]), "tim", back)

    rows = owner_rows(owner_table, CAP)
    match = rows[None, :] == jnp.arange(devices * CAP, dtype=jnp.int32)[:, None]
    valid = jnp.any(match, axis=1).astype(jnp.int32)
    which = jnp.sum(jnp.where(match, jnp.arange(CH, dtype=jnp.int32)[None, :], 0), axis=1)
    first = (which * AVG - AVG * CH // 2) % F
    me = lax.axis_index("inp") * n_tim + lax.axis_index("tim")
    mine = lax.dynamic_slice(valid, (me * CAP,), (CAP,))

    window = jnp.asarray(window_table())
    twist = jnp.asarray(twist_table())
    table = jnp.asarray(radix_table()).astype(jnp.bfloat16)

    last = (lax.axis_index("tim") == n_tim - 1).astype(jnp.int32)
    first = jnp.concatenate([first, last[None]])
    tables = (window, twist, table)
    third = channel_call([[(((0, 0), (1, 0), (2, 0), (3, 0)), 0)]], first, own, *tables)
    second = [[(((3, 0), (0, 0), (1, 0), (2, 0)), 0)]]
    near = channel_call(second, first, (*own[:3], before), *tables, prior=(third,))
    near, earlier, after = lax.optimization_barrier((near, earlier, after))
    near = lax.all_to_all(near, ("inp", "tim"), split_axis=0, concat_axis=0, tiled=True)
    xs = (*own, before, earlier, after)
    e3, e2, e1, x0, x1, x2, x3, a0, a1 = (5, 0), (5, 2), (4, 0), (0, 0), (1, 0), (2, 0), (3, 0), (6, 0), (6, 2)
    plans = [
        [((e3, e2, e1, x0), 0), ((e2, e1, x0, x1), 0)],
        [((x1, x2, x3, a0), 3), ((x2, x3, a0, a1), 2)],
    ]
    far = channel_call(plans, first, xs, *tables)
    far = lax.all_to_all(far, ("inp", "tim"), split_axis=0, concat_axis=0, tiled=True)
    partial = correlate_call(n_inp, n_tim, 0, 1.0, mine, near)
    return correlate_call(n_inp, n_tim, MIXED, 1.0 / (n_tim * spec_dev * AVG), mine, far, partial)


def solution(mesh):
    return jax.shard_map(
        body,
        mesh=mesh,
        in_specs=(P(None, "inp", "tim"), P("inp", "tim"), P()),
        out_specs=P(("inp", "tim"), None, None),
        check_vma=False,
    )
```

time: 185 us -> 153 us (0.83)
  the two profiles are of different devices: /device:TPU:32 before, /device:TPU:1 now
where the time goes in v2:
time: 153 us; the launch traced here: 152 us
  waiting for transfers between devices  58.5 us (38%)
  Pallas kernels  57 us (37%)
  starting transfers between devices  22.8 us (15%)
  other arithmetic  8.03 us (5%)
  local copies, waits for them, and re-layouts  5.96 us (4%)
    pallas_call x3, Pallas kernels, channel_call(): pl.pallas_call(functools.partial(channel_kernel, plans, len(xs)), out_sha...  30.3 us
    all_to_all x1, waiting for transfers between devices, body(): lax.all_to_all(near, ('inp', 'tim'), split_axis=0, concat_axis=0, tiled=T...  29.4 us
    all_to_all x1, waiting for transfers between devices, body(): lax.all_to_all(far, ('inp', 'tim'), split_axis=0, concat_axis=0, tiled=True)  29.1 us
    pallas_call x2, Pallas kernels, correlate_call(): pl.pallas_call(functools.partial(correlate_kernel, n_tim, mixed, scale),...  26.6 us
    all_to_all x1, starting transfers between devices, body(): lax.all_to_all(near, ('inp', 'tim'), split_axis=0, concat_axis=0, tiled=T...  11.2 us
    unnamed x18, local copies, waits for them, and re-layouts  5.23 us
    convert_element_type x1, other arithmetic, body(): (voltages[:, :, s * F:(s + 1) * F].astype(jnp.float32) * scale[None, :, s...  4.74 us
    all_to_all x1, starting transfers between devices, body(): lax.all_to_all(far, ('inp', 'tim'), split_axis=0, concat_axis=0, tiled=True)  4.57 us
  transfers between devices with their start and end apart: 5, of which 2 were waited for; matrix products, arithmetic and copies ran while one was open for 1% of the time, Pallas kernels for 28%

profile of v2, /device:TPU:1, one launch (start us, length us, event | category | flops | bytes accessed | tf_op | source)
XLA Modules:
  0.0 152.4 jit_solution(8167554203687611029)
XLA Ops:
  0.0 0.7 exponential_multiply_fusion
  0.7 4.7 %multiply_convert_fusion = (bf16[2,64,4096]{2,1,0:T(8,128)(2,1)S(1)}, bf16[2,64,4096]{2,1,0:T(8,128)(2,1)S(1)}, bf16[2,64,4096]{2,1,0:T(8,128)(2,1)S(1)}, bf16[2,64,4096]{2,1,0:T(8,128)(2,1)S(1)}) fusion(s32[2,64,16384]{2,1,0:T(8,128)} %param.6, f32[64]{0:T(128)S(1)} %get-tuple-element.15, f32[64]{0:T(128)S(1)} %get-tuple-element.17, ...), kind=kLoop, calls=%fused_computation | loop fusion | flops 6291456 | bytes 12583936 | tf_op jit(solution)/shard_map/convert_element_type | solution.py:311
  5.4 0.0 copy-start.1
  5.5 0.0 copy-start.4
  5.5 0.0 copy-start
  5.5 0.0 copy-start.2
  5.5 0.1 slice.50
  5.5 0.1 slice.51
  5.6 0.0 copy-start.8
  5.6 1.5 %pad_maximum_fusion = bf16[4,48,4096]{2,1,0:T(8,128)(2,1)} fusion(bf16[2,48,4096]{2,1,0:T(8,128)(2,1)S(1)} %slice.51, bf16[2,48,4096]{2,1,0:T(8,128)(2,1)S(1)} %slice.50), kind=kLoop, calls=%fused_computation.4 | loop fusion | flops 786432 | bytes 3145728 | tf_op jit(solution)/shard_map/concatenate | solution.py:320
  7.2 0.0 copy-done.1
  7.2 1.4 collective-permute-start.2
  8.6 0.0 copy-done.4
  8.6 3.3 %collective-permute-start = (bf16[2,64,4096]{2,1,0:T(8,128)(2,1)S(1)}, bf16[2,64,4096]{2,1,0:T(8,128)(2,1)S(1)}, u32[]{:S(2)}, u32[]{:S(2)}) collective-permute-start(bf16[2,64,4096]{2,1,0:T(8,128)(2,1)S(1)} %get-tuple-element.11.refs_3_), channel_id=1, source_target_pairs={{0,1},{1,2},{2,3},{3,4},{4,5},{5,6},{6,7},{8,9},{9,10},{10,11},{11... | collective-permute-start | bytes 3145736 | tf_op jit(solution)/shard_map/ppermute | solution.py:318
  11.9 0.0 copy-done
  11.9 0.0 copy-done.2
  12.0 2.3 %collective-permute-start.1 = (bf16[4,16,4096]{2,1,0:T(8,128)(2,1)S(1)}, bf16[4,16,4096]{2,1,0:T(8,128)(2,1)S(1)}, u32[]{:S(2)}, u32[]{:S(2)}) collective-permute-start(bf16[4,16,4096]{2,1,0:T(8,128)(2,1)S(1)} %pad_maximum_fusion.1), channel_id=1, source_target_pairs={{0,1},{1,2},{2,3},{3,4},{4,5},{5,6},{6,7},{8,9},{9,10},{10,11},{11... | collective-permute-start | bytes 1572872 | tf_op jit(solution)/shard_map/ppermute | solution.py:319
  14.3 0.0 copy-done.8
  14.3 0.2 convert_reduce_fusion
  14.5 0.1 select_reduce_fusion
  14.7 0.6 pad_add_fusion.first_ref
  15.2 8.5 %channels.3.refs_7_ = bf16[128,2,24,128]{3,2,1,0:T(8,128)(2,1)} custom-call(s32[257]{0:T(512)} %pad_add_fusion.first_ref, bf16[2,64,4096]{2,1,0:T(8,128)(2,1)} %copy-done.1, bf16[2,64,4096]{2,1,0:T(8,128)(2,1)} %copy-done, bf16[2,64,4096]{2,1,0:T(8,128)(2,1)} %copy-done.2, bf16[2,64,4096]{2,1,0:T(8,128)(2,1)} %copy-done.4, ...), custom_call_target="tpu_custom_call" | custom-call | flops 1000000000 | bytes 8388608 | tf_op jit(solution)/shard_map/channels/pallas_call | solution.py:187
  23.7 0.0 collective-permute-done.refs_3_.refs_4_
  23.7 0.0 copy-start.5
  23.7 1.0 copy-done.5
  24.7 9.6 %channels.4 = bf16[128,2,48,128]{3,2,1,0:T(8,128)(2,1)} custom-call(s32[257]{0:T(512)} %pad_add_fusion.first_ref, bf16[2,64,4096]{2,1,0:T(8,128)(2,1)} %copy-done.1, bf16[2,64,4096]{2,1,0:T(8,128)(2,1)} %copy-done, bf16[2,64,4096]{2,1,0:T(8,128)(2,1)} %copy-done.2, bf16[2,64,4096]{2,1,0:T(8,128)(2,1)} %copy-done.5, ...), custom_call_target="tpu_custom_call" | custom-call | flops 1000000000 | bytes 8388608 | tf_op jit(solution)/shard_map/channels/pallas_call | solution.py:187
  34.3 0.0 collective-permute-done.1.refs_5_
  34.3 0.0 copy-start.7
  34.3 0.0 collective-permute-done.2.refs_6_
  34.3 0.8 copy-done.7
  35.1 11.2 %all-to-all-start.1 = ((bf16[128,2,48,128]{3,2,1,0:T(8,128)(2,1)}), bf16[128,2,48,128]{3,2,1,0:T(8,128)(2,1)S(1)}, u32[]{:S(2)}, u32[]{:S(2)}) async-start(bf16[128,2,48,128]{3,2,1,0:T(8,128)(2,1)} %channels.4), calls=%async_computation.1 | async-start | bytes 6291456 | tf_op jit(solution)/shard_map/all_to_all | solution.py:341
  46.3 12.3 %channels.5 = bf16[128,2,48,128]{3,2,1,0:T(8,128)(2,1)} custom-call(s32[257]{0:T(512)} %pad_add_fusion.first_ref, bf16[2,64,4096]{2,1,0:T(8,128)(2,1)} %copy-done.1, bf16[2,64,4096]{2,1,0:T(8,128)(2,1)} %copy-done, bf16[2,64,4096]{2,1,0:T(8,128)(2,1)} %copy-done.2, bf16[2,64,4096]{2,1,0:T(8,128)(2,1)} %copy-done.4, bf16[2,64,4096]{2,1,0:T(8,128)(2,1)} %copy-done.5, ...), custom_call_target="tpu_custom_call" | custom-call | flops 2000000000 | bytes 8388608 | tf_op jit(solution)/shard_map/channels/pallas_call | solution.py:187
  58.6 29.4 %all-to-all-done.1.piece = bf16[128,2,48,128]{3,2,1,0:T(8,128)(2,1)S(1)} async-done(((bf16[128,2,48,128]{3,2,1,0:T(8,128)(2,1)}), bf16[128,2,48,128]{3,2,1,0:T(8,128)(2,1)S(1)}, u32[]{:S(2)}, u32[]{:S(2)}) %all-to-all-start.1) | async-done | bytes 3145760 | tf_op jit(solution)/shard_map/all_to_all | solution.py:341
  88.0 0.0 copy-start.6
  88.0 1.7 %copy-done.6 = bf16[128,2,48,128]{3,2,1,0:T(8,128)(2,1)} copy-done((bf16[128,2,48,128]{3,2,1,0:T(8,128)(2,1)}, bf16[128,2,48,128]{3,2,1,0:T(8,128)(2,1)S(1)}, u32[]{:S(2)}) %copy-start.6) | copy-done | bytes 3145752
  89.7 4.6 %all-to-all-start = ((bf16[128,2,48,128]{3,2,1,0:T(8,128)(2,1)}), bf16[128,2,48,128]{3,2,1,0:T(8,128)(2,1)S(1)}, u32[]{:S(2)}, u32[]{:S(2)}) async-start(bf16[128,2,48,128]{3,2,1,0:T(8,128)(2,1)} %channels.5), calls=%async_computation | async-start | bytes 6291456 | tf_op jit(solution)/shard_map/all_to_all | solution.py:349
  94.3 0.1 fusion
  94.4 0.6 dynamic_slice.3.valid_ref
  95.0 12.0 %correlate.2.refs_0_ = f32[2,1024,1024]{2,1,0:T(8,128)} custom-call(s32[2]{0:T(128)} %dynamic_slice.3.valid_ref, bf16[128,2,48,128]{3,2,1,0:T(8,128)(2,1)} %copy-done.6), custom_call_target="tpu_custom_call" | custom-call | flops 5000000000 | bytes 19922944 | tf_op jit(solution)/shard_map/correlate/pallas_call | solution.py:285
  107.0 29.1 %all-to-all-done.piece = bf16[128,2,48,128]{3,2,1,0:T(8,128)(2,1)S(1)} async-done(((bf16[128,2,48,128]{3,2,1,0:T(8,128)(2,1)}), bf16[128,2,48,128]{3,2,1,0:T(8,128)(2,1)S(1)}, u32[]{:S(2)}, u32[]{:S(2)}) %all-to-all-start) | async-done | bytes 3145760 | tf_op jit(solution)/shard_map/all_to_all | solution.py:349
  136.1 0.0 copy-start.3
  136.1 1.7 %copy-done.3 = bf16[128,2,48,128]{3,2,1,0:T(8,128)(2,1)} copy-done((bf16[128,2,48,128]{3,2,1,0:T(8,128)(2,1)}, bf16[128,2,48,128]{3,2,1,0:T(8,128)(2,1)S(1)}, u32[]{:S(2)}) %copy-start.3) | copy-done | bytes 3145752
  137.8 14.6 %correlate.3 = f32[2,1024,1024]{2,1,0:T(8,128)} custom-call(s32[2]{0:T(128)} %dynamic_slice.3.valid_ref, bf16[128,2,48,128]{3,2,1,0:T(8,128)(2,1)} %copy-done.3, f32[2,1024,1024]{2,1,0:T(8,128)} %correlate.2.refs_0_), custom_call_target="tpu_custom_call" | custom-call | flops 5000000000 | bytes 19922944 | tf_op jit(solution)/shard_map/correlate/pallas_call | solution.py:285
  (7 shorter events, 0.1 us)
Async XLA Ops:
  5.4 1.7 %copy-start.1 = (bf16[2,64,4096]{2,1,0:T(8,128)(2,1)}, bf16[2,64,4096]{2,1,0:T(8,128)(2,1)S(1)}, u32[]{:S(2)}) copy-start(bf16[2,64,4096]{2,1,0:T(8,128)(2,1)S(1)} %get-tuple-element.13.refs_0_) | copy-start | bytes 3145732
  5.5 3.1 %copy-start.4 = (bf16[2,64,4096]{2,1,0:T(8,128)(2,1)}, bf16[2,64,4096]{2,1,0:T(8,128)(2,1)S(1)}, u32[]{:S(2)}) copy-start(bf16[2,64,4096]{2,1,0:T(8,128)(2,1)S(1)} %get-tuple-element.11.refs_3_) | copy-start | bytes 3145732
  5.5 6.4 %copy-start = (bf16[2,64,4096]{2,1,0:T(8,128)(2,1)}, bf16[2,64,4096]{2,1,0:T(8,128)(2,1)S(1)}, u32[]{:S(2)}) copy-start(bf16[2,64,4096]{2,1,0:T(8,128)(2,1)S(1)} %get-tuple-element.12.refs_1_) | copy-start | bytes 3145732
  5.5 6.5 %copy-start.2 = (bf16[2,64,4096]{2,1,0:T(8,128)(2,1)}, bf16[2,64,4096]{2,1,0:T(8,128)(2,1)S(1)}, u32[]{:S(2)}) copy-start(bf16[2,64,4096]{2,1,0:T(8,128)(2,1)S(1)} %get-tuple-element.14.refs_2_) | copy-start | bytes 3145732
  5.6 8.7 %copy-start.8 = (s32[144]{0:T(256)S(1)}, s32[144]{0:T(256)}, u32[]{:S(2)}) copy-start(s32[144]{0:T(256)} %param.8) | copy-start | bytes 1732
  7.2 27.1 %collective-permute-start.2 = (bf16[4,48,4096]{2,1,0:T(8,128)(2,1)}, bf16[4,48,4096]{2,1,0:T(8,128)(2,1)}, u32[]{:S(2)}, u32[]{:S(2)}) collective-permute-start(bf16[4,48,4096]{2,1,0:T(8,128)(2,1)} %pad_maximum_fusion), channel_id=1, source_target_pairs={{0,7},{1,0},{2,1},{3,2},{4,3},{5,4},{6,5},{7,6},{8,15},{9,8},{10,9... | collective-permute-start | bytes 4718600 | tf_op jit(solution)/shard_map/ppermute | solution.py:320
  8.6 15.1 %collective-permute-start = (bf16[2,64,4096]{2,1,0:T(8,128)(2,1)S(1)}, bf16[2,64,4096]{2,1,0:T(8,128)(2,1)S(1)}, u32[]{:S(2)}, u32[]{:S(2)}) collective-permute-start(bf16[2,64,4096]{2,1,0:T(8,128)(2,1)S(1)} %get-tuple-element.11.refs_3_), channel_id=1, source_target_pairs={{0,1},{1,2},{2,3},{3,4},{4,5},{5,6},{6,7},{8,9},{9,10},{10,11},{11... | collective-permute-start | bytes 3145736 | tf_op jit(solution)/shard_map/ppermute | solution.py:318
  12.0 22.3 %collective-permute-start.1 = (bf16[4,16,4096]{2,1,0:T(8,128)(2,1)S(1)}, bf16[4,16,4096]{2,1,0:T(8,128)(2,1)S(1)}, u32[]{:S(2)}, u32[]{:S(2)}) collective-permute-start(bf16[4,16,4096]{2,1,0:T(8,128)(2,1)S(1)} %pad_maximum_fusion.1), channel_id=1, source_target_pairs={{0,1},{1,2},{2,3},{3,4},{4,5},{5,6},{6,7},{8,9},{9,10},{10,11},{11... | collective-permute-start | bytes 1572872 | tf_op jit(solution)/shard_map/ppermute | solution.py:319
  23.7 1.0 copy-start.5
  34.3 0.8 copy-start.7
  35.1 52.9 %all-to-all-start.1 = ((bf16[128,2,48,128]{3,2,1,0:T(8,128)(2,1)}), bf16[128,2,48,128]{3,2,1,0:T(8,128)(2,1)S(1)}, u32[]{:S(2)}, u32[]{:S(2)}) async-start(bf16[128,2,48,128]{3,2,1,0:T(8,128)(2,1)} %channels.4), calls=%async_computation.1 | async-start | bytes 6291456 | tf_op jit(solution)/shard_map/all_to_all | solution.py:341
  88.0 1.7 %copy-start.6 = (bf16[128,2,48,128]{3,2,1,0:T(8,128)(2,1)}, bf16[128,2,48,128]{3,2,1,0:T(8,128)(2,1)S(1)}, u32[]{:S(2)}) copy-start(bf16[128,2,48,128]{3,2,1,0:T(8,128)(2,1)S(1)} %all-to-all-done.1.piece) | copy-start | bytes 9437188
  89.7 46.4 %all-to-all-start = ((bf16[128,2,48,128]{3,2,1,0:T(8,128)(2,1)}), bf16[128,2,48,128]{3,2,1,0:T(8,128)(2,1)S(1)}, u32[]{:S(2)}, u32[]{:S(2)}) async-start(bf16[128,2,48,128]{3,2,1,0:T(8,128)(2,1)} %channels.5), calls=%async_computation | async-start | bytes 6291456 | tf_op jit(solution)/shard_map/all_to_all | solution.py:349
  136.1 1.7 %copy-start.3 = (bf16[128,2,48,128]{3,2,1,0:T(8,128)(2,1)}, bf16[128,2,48,128]{3,2,1,0:T(8,128)(2,1)S(1)}, u32[]{:S(2)}) copy-start(bf16[128,2,48,128]{3,2,1,0:T(8,128)(2,1)S(1)} %all-to-all-done.piece) | copy-start | bytes 9437188

commit v3 on v2

--- a/solution.py
+++ b/solution.py
@@ -17,8 +17,9 @@
 R1 = 16
 R2 = 256
 LANES = 128
-VMEM = 60 * 2**20
-MIXED = 16
+CHANNEL_VMEM = 30 * 2**20
+CORRELATE_VMEM = 34 * 2**20
+TILE = 256
 
 
 def window_table():
@@ -90,18 +91,19 @@
     return out
 
 
-def channel_kernel(plans, count, first_ref, *refs):
+def channel_kernel(plan, count, first_ref, *refs):
     xs, (window, twist, table) = refs[:count], refs[count : count + 3]
     prior, (out, turned, spectrum) = refs[count + 3 : -3], refs[-3:]
     step = pl.program_id(0)
-    spectra = len(plans[0])
-    block = xs[0].shape[1]
+    spectra = len(plan)
+    block = 16
     inputs = turned.shape[1] // spectra
     slots = out.shape[0] * out.shape[1]
     wrapped = first_ref[slots] != 0
 
-    def columns(plan, half):
+    def columns(half, carry):
         base = half * LANES
+        members = pl.ds(pl.multiple_of(step * block, block), block)
         lanes2 = pl.ds(pl.multiple_of(base, LANES), LANES)
         lanes3 = pl.ds(pl.multiple_of(base + R2, LANES), LANES)
         for s, (blocks, cut) in enumerate(plan):
@@ -113,8 +115,9 @@
                     for c in range(2):
                         total = None
                         for tap in range(TAPS):
-                            index, part = blocks[tap]
-                            value = xs[index][part + c, :, lanes].astype(jnp.float32)[8 * r : 8 * r + 8]
+                            index, place = blocks[tap]
+                            shifted = pl.ds(pl.multiple_of(base + n * R2 + place * F, LANES), LANES)
+                            value = xs[index][c, members, shifted].astype(jnp.float32)[8 * r : 8 * r + 8]
                             which = tap if tap >= cut else jnp.where(wrapped, TAPS, tap)
                             term = window[which, :, lanes] * value
                             total = term if total is None else total + term
@@ -127,15 +130,9 @@
                     cosine, sine = twist[0, m, :, lanes2], twist[1, m, :, lanes2]
                     turned[m, row, lanes2] = re * cosine + im * sine
                     turned[m, row, lanes3] = im * cosine - re * sine
-
-    def filtered(plan):
-        lax.fori_loop(0, R2 // LANES, lambda half, carry: (columns(plan, half), carry)[1], 0)
-
-    if len(plans) == 1:
-        filtered(plans[0])
-    else:
-        pl.when(step == 0)(lambda: filtered(plans[0]))
-        pl.when(step != 0)(lambda: filtered(plans[1]))
+        return carry
+
+    lax.fori_loop(0, R2 // LANES, columns, 0)
 
     @pl.when(step == pl.num_programs(0) - 1)
     def _():
@@ -170,63 +167,53 @@
         lax.fori_loop(0, out.shape[0], place, 0, unroll=2)
 
 
-def channel_call(plans, first, xs, window, twist, table, prior=()):
+def channel_call(plan, first, xs, window, twist, table, prior=()):
     owners = (first.shape[0] - 1) // CAP
     block = 16
-    inputs = max(x.shape[1] for x in xs)
-    spectra = len(plans[0])
-
-    def spec(x):
-        skip, most = (inputs - x.shape[1]) // block, x.shape[1] // block - 1
-        if most == 0:
-            skip = 0
-        return pl.BlockSpec((x.shape[0], block, F), lambda i, *_: (0, jnp.clip(i - skip, 0, most), 0))
-
-    whole = lambda shape: pl.BlockSpec(shape, lambda i, *_: (0,) * len(shape))
+    inputs = xs[0].shape[1]
+    spectra = len(plan)
+    held = pl.BlockSpec(memory_space=pltpu.VMEM)
     shape = (owners, CAP, (spectra + len(prior)) * AVG, LANES)
     return pl.pallas_call(
-        functools.partial(channel_kernel, plans, len(xs)),
+        functools.partial(channel_kernel, plan, len(xs)),
         out_shape=jax.ShapeDtypeStruct(shape, jnp.bfloat16),
         grid_spec=pltpu.PrefetchScalarGridSpec(
             num_scalar_prefetch=1,
             grid=(inputs // block,),
-            in_specs=[spec(x) for x in xs] + [whole(x.shape) for x in (window, twist, table, *prior)],
-            out_specs=whole(shape),
+            in_specs=[held] * (len(xs) + 3 + len(prior)),
+            out_specs=held,
             scratch_shapes=[
                 pltpu.VMEM((R1, spectra * inputs, 2 * R2), jnp.float32),
                 pltpu.VMEM((spectra, F, LANES), jnp.float32),
             ],
         ),
-        compiler_params=pltpu.CompilerParams(vmem_limit_bytes=VMEM),
+        compiler_params=pltpu.CompilerParams(vmem_limit_bytes=CHANNEL_VMEM),
         cost_estimate=pl.CostEstimate(flops=10**9 * spectra, bytes_accessed=8 * 2**20, transcendentals=0),
         name="channels",
     )(first, *xs, window, twist, table, *prior)
 
 
-def correlate_kernel(n_tim, mixed, scale, valid_ref, piece, *refs):
+def correlate_kernel(n_tim, scale, valid_ref, piece, *refs):
     partial = refs[0] if len(refs) == 4 else None
     out, rows_k, rows_i = refs[-3:]
     slot, block = pl.program_id(0), pl.program_id(1)
     depth, width = rows_k.shape[1], rows_k.shape[2]
-    tile = out.shape[1]
+    held = partial is None
+    tile = TILE
     blocks = width // tile
     half = depth // 2
 
     def arrange(which, q):
         lane = lax.broadcasted_iota(jnp.int32, (2 * AVG, LANES), 1)
-        low, ahead = lane < LANES // 2, lane % (LANES // 2) < mixed
+        low = lane < LANES // 2
         lanes = pl.ds(pl.multiple_of(q * LANES, LANES), LANES)
-
-        def rows(e, t):
-            value = piece[(2 * q + e) * n_tim + t, which].astype(jnp.float32)
-            if mixed:
-                other = piece[(2 * q + e) * n_tim + (t + 1) % n_tim, which].astype(jnp.float32)
-                value = jnp.where(ahead, other, value)
-            return value
 
         base = 0
         for u in range(n_tim // 2):
-            group = [[rows(e, 2 * u + v) for v in range(2)] for e in range(2)]
+            group = [
+                [piece[(2 * q + e) * n_tim + 2 * u + v, which].astype(jnp.float32) for v in range(2)]
+                for e in range(2)
+            ]
             for s in range(piece.shape[2] // AVG):
                 even, odd = [
                     jnp.concatenate([group[e][v][AVG * s : AVG * s + AVG] for v in range(2)], axis=0)
@@ -261,8 +248,12 @@
                 imag = jnp.dot(rows_i[which, rows, half:], other, preferred_element_type=jnp.float32)
             value = real if imag is None else imag if real is None else jnp.where(upper, real, imag)
             if partial is not None:
-                value = value + partial[0, :, lanes]
-            out[0, :, lanes] = jnp.where(keep, value * scale, 0.0)
+                value = value + partial[which, rows, lanes]
+            value = jnp.where(keep, value * scale, 0.0)
+            if held:
+                out[which, rows, lanes] = value
+            else:
+                out[0, :, lanes] = value
 
     each = width // LANES // blocks
     for which in range(CAP):
@@ -276,26 +267,27 @@
                 strip(which, i)
 
 
-def correlate_call(n_inp, n_tim, mixed, scale, valid, piece, partial=None):
+def correlate_call(n_inp, n_tim, scale, valid, piece, partial=None):
     width = n_inp * LANES // 2
     depth = n_tim * piece.shape[2] * 2
-    tile = 256
+    tile = TILE
     block = pl.BlockSpec((1, tile, width), lambda s, i, *_: (s, i, 0))
+    held = pl.BlockSpec(memory_space=pltpu.VMEM)
     more = [] if partial is None else [partial]
     return pl.pallas_call(
-        functools.partial(correlate_kernel, n_tim, mixed, scale),
+        functools.partial(correlate_kernel, n_tim, scale),
         out_shape=jax.ShapeDtypeStruct((CAP, width, width), jnp.float32),
         grid_spec=pltpu.PrefetchScalarGridSpec(
             num_scalar_prefetch=1,
             grid=(CAP, width // tile),
-            in_specs=[pl.BlockSpec(piece.shape, lambda s, i, *_: (0, 0, 0, 0))] + [block] * len(more),
-            out_specs=block,
+            in_specs=[held] + [held] * len(more),
+            out_specs=block if more else held,
             scratch_shapes=[
                 pltpu.VMEM((CAP, depth, width), jnp.bfloat16),
                 pltpu.VMEM((CAP, width, depth + depth // 2), jnp.bfloat16),
             ],
         ),
-        compiler_params=pltpu.CompilerParams(vmem_limit_bytes=VMEM),
+        compiler_params=pltpu.CompilerParams(vmem_limit_bytes=CORRELATE_VMEM),
         cost_estimate=pl.CostEstimate(flops=5 * 10**9, bytes_accessed=19 * 2**20, transcendentals=0),
         name="correlate",
     )(valid, piece, *more)
@@ -307,17 +299,19 @@
     devices = n_inp * n_tim
     spec_dev = voltages.shape[2] // F
     scale = jnp.exp2(scale_exps.astype(jnp.float32)) / 128.0
-    own = [
-        (voltages[:, :, s * F : (s + 1) * F].astype(jnp.float32) * scale[None, :, s : s + 1]).astype(
-            jnp.bfloat16
-        )
-        for s in range(spec_dev)
-    ]
+    lane = lax.broadcasted_iota(jnp.int32, (1, 1, 2 * F), 2)
+
+    def samples(s, count):
+        factor = scale[None, :, s : s + 1]
+        if count == 2:
+            factor = jnp.where(lane < F, factor, scale[None, :, s + 1 : s + 2])
+        return (voltages[:, :, s * F : (s + count) * F].astype(jnp.float32) * factor).astype(jnp.bfloat16)
+
+    own01, own2, own3 = samples(0, 2), samples(2, 1), samples(3, 1)
     ahead = [(source, source + 1) for source in range(n_tim - 1)]
     back = [(source, (source - 1) % n_tim) for source in range(n_tim)]
-    before = lax.ppermute(own[3], "tim", ahead)
-    earlier = lax.ppermute(jnp.concatenate([own[1][:, :MIXED], own[2][:, :MIXED]]), "tim", ahead)
-    after = lax.ppermute(jnp.concatenate([own[0][:, MIXED:], own[1][:, MIXED:]]), "tim", back)
+    before = lax.ppermute(own3, "tim", ahead)
+    after = lax.ppermute(own01, "tim", back)
 
     rows = owner_rows(owner_table, CAP)
     match = rows[None, :] == jnp.arange(devices * CAP, dtype=jnp.int32)[:, None]
@@ -334,21 +328,16 @@
     last = (lax.axis_index("tim") == n_tim - 1).astype(jnp.int32)
     first = jnp.concatenate([first, last[None]])
     tables = (window, twist, table)
-    third = channel_call([[(((0, 0), (1, 0), (2, 0), (3, 0)), 0)]], first, own, *tables)
-    second = [[(((3, 0), (0, 0), (1, 0), (2, 0)), 0)]]
-    near = channel_call(second, first, (*own[:3], before), *tables, prior=(third,))
-    near, earlier, after = lax.optimization_barrier((near, earlier, after))
+    x0, x1, x2, x3 = (0, 0), (0, 1), (1, 0), (2, 0)
+    third = channel_call([((x0, x1, x2, x3), 0)], first, (own01, own2, own3), *tables)
+    near = channel_call([(((2, 0), x0, x1, x2), 0)], first, (own01, own2, before), *tables, prior=(third,))
+    near, after = lax.optimization_barrier((near, after))
     near = lax.all_to_all(near, ("inp", "tim"), split_axis=0, concat_axis=0, tiled=True)
-    xs = (*own, before, earlier, after)
-    e3, e2, e1, x0, x1, x2, x3, a0, a1 = (5, 0), (5, 2), (4, 0), (0, 0), (1, 0), (2, 0), (3, 0), (6, 0), (6, 2)
-    plans = [
-        [((e3, e2, e1, x0), 0), ((e2, e1, x0, x1), 0)],
-        [((x1, x2, x3, a0), 3), ((x2, x3, a0, a1), 2)],
-    ]
-    far = channel_call(plans, first, xs, *tables)
+    plan = [((x1, x2, x3, (3, 0)), 3), ((x2, x3, (3, 0), (3, 1)), 2)]
+    far = channel_call(plan, first, (own01, own2, own3, after), *tables)
     far = lax.all_to_all(far, ("inp", "tim"), split_axis=0, concat_axis=0, tiled=True)
-    partial = correlate_call(n_inp, n_tim, 0, 1.0, mine, near)
-    return correlate_call(n_inp, n_tim, MIXED, 1.0 / (n_tim * spec_dev * AVG), mine, far, partial)
+    partial = correlate_call(n_inp, n_tim, 1.0, mine, near)
+    return correlate_call(n_inp, n_tim, 1.0 / (n_tim * spec_dev * AVG), mine, far, partial)
 
 
 def solution(mesh):

time: 153 us -> 145 us (0.948)
  Pallas kernels: 57 us -> 42.6 us
  local copies, waits for them, and re-layouts: 5.96 us -> 14.9 us
  other arithmetic: 8.03 us -> 5.64 us
    pallas_call x5, Pallas kernels: 57 us -> 42.6 us  [the longest x3 22.5 us: channel_call(): pl.pallas_call(functools.partial(channel_kernel, plan, len(xs)), out_shap...]
    unnamed x18 -> x24, local copies, waits for them, and re-layouts: 5.23 us -> 14.8 us
    ppermute x3 -> x2, waiting for transfers between devices: 0.01 us -> 3.48 us  [the longest x1 3.48 us: body(): before = lax.ppermute(own3, 'tim', ahead)]
    all_to_all x1, waiting for transfers between devices: 29.4 us -> 27.4 us  [body(): lax.all_to_all(near, ('inp', 'tim'), split_axis=0, concat_axis=0, tiled=T...]
    concatenate x2 -> x0, other arithmetic: 1.6 us -> none  [the longest x1 1.55 us: body(): jnp.concatenate([own[0][:, MIXED:], own[1][:, MIXED:]])]
    ppermute x3 -> x2, starting transfers between devices: 7 us -> 6.02 us  [the longest x1 4.58 us: body(): before = lax.ppermute(own3, 'tim', ahead)]
    convert_element_type x1 -> x2, other arithmetic: 4.74 us -> 4.31 us  [samples(): (voltages[:, :, s * F:(s + count) * F].astype(jnp.float32) * factor).asty...]
  transfers between devices with their start and end apart: 5 -> 4, of which waited for: 2 -> 3; matrix products, arithmetic and copies ran while one was open for 1% -> 1% of each run, Pallas kernels for 28% -> 23%
where the time goes in v3:
time: 145 us
  waiting for transfers between devices  58.9 us (41%)
  Pallas kernels  42.6 us (29%)
  starting transfers between devices  22.3 us (15%)
  local copies, waits for them, and re-layouts  14.9 us (10%)
  other arithmetic  5.64 us (4%)
    all_to_all x1, waiting for transfers between devices, body(): lax.all_to_all(far, ('inp', 'tim'), split_axis=0, concat_axis=0, tiled=True)  28 us
    all_to_all x1, waiting for transfers between devices, body(): lax.all_to_all(near, ('inp', 'tim'), split_axis=0, concat_axis=0, tiled=T...  27.4 us
    pallas_call x3, Pallas kernels, channel_call(): pl.pallas_call(functools.partial(channel_kernel, plan, len(xs)), out_shap...  22.5 us
    pallas_call x2, Pallas kernels, correlate_call(): pl.pallas_call(functools.partial(correlate_kernel, n_tim, scale), out_sha...  20.2 us
    unnamed x24, local copies, waits for them, and re-layouts  14.8 us
    all_to_all x1, starting transfers between devices, body(): lax.all_to_all(near, ('inp', 'tim'), split_axis=0, concat_axis=0, tiled=T...  11.7 us
    ppermute x1, starting transfers between devices, body(): before = lax.ppermute(own3, 'tim', ahead)  4.58 us
    all_to_all x1, starting transfers between devices, body(): lax.all_to_all(far, ('inp', 'tim'), split_axis=0, concat_axis=0, tiled=True)  4.57 us
  transfers between devices with their start and end apart: 4, of which 3 were waited for; matrix products, arithmetic and copies ran while one was open for 1% of the time, Pallas kernels for 23%

profile of v3, /device:TPU:1, one launch (start us, length us, event | category | flops | bytes accessed | tf_op | source)
XLA Modules:
  0.0 144.5 jit_solution(3638720098451153600)
XLA Ops:
  0.0 0.7 exponential_multiply_fusion
  0.7 0.2 broadcast_select_fusion
  0.9 0.0 copy-start.10
  0.9 2.8 %multiply_convert_fusion.refs_0_ = bf16[2,64,8192]{2,1,0:T(8,128)(2,1)S(1)} fusion(s32[2,64,16384]{2,1,0:T(8,128)} %param.6, f32[64,8192]{1,0:T(8,128)S(1)} %broadcast_select_fusion), kind=kLoop, calls=%fused_computation | loop fusion | flops 3145728 | bytes 8388608 | tf_op jit(solution)/shard_map/convert_element_type | solution.py:308
  3.7 1.4 collective-permute-start.1
  5.1 0.4 copy-done.10
  5.6 0.0 copy-start.11
  5.6 0.0 copy-start.9
  5.6 1.5 %multiply_convert_fusion.1 = (bf16[2,64,4096]{2,1,0:T(8,128)(2,1)}, bf16[2,64,4096]{2,1,0:T(8,128)(2,1)S(1)}) fusion(s32[2,64,16384]{2,1,0:T(8,128)S(1)} %copy-done.10, f32[64]{0:T(128)S(1)} %get-tuple-element.11, f32[64]{0:T(128)S(1)} %get-tuple-element.12), kind=kLoop, calls=%fused_computation.1 | loop fusion | flops 3145728 | bytes 6291968 | tf_op jit(solution)/shard_map/convert_element_type | solution.py:308
  7.1 4.6 %collective-permute-start = (bf16[2,64,4096]{2,1,0:T(8,128)(2,1)}, bf16[2,64,4096]{2,1,0:T(8,128)(2,1)}, u32[]{:S(2)}, u32[]{:S(2)}) collective-permute-start(bf16[2,64,4096]{2,1,0:T(8,128)(2,1)} %get-tuple-element.9.refs_2_), channel_id=1, source_target_pairs={{0,1},{1,2},{2,3},{3,4},{4,5},{5,6},{6,7},{8,9},{9,10},{10,11},{11... | collective-permute-start | bytes 3145736 | tf_op jit(solution)/shard_map/ppermute | solution.py:313
  11.7 0.0 copy-done.11
  11.7 0.2 convert_reduce_fusion
  11.9 0.1 select_reduce_fusion
  12.1 0.0 copy-done.9
  12.1 0.0 copy-start.4
  12.1 1.1 copy-done.4
  13.2 0.0 copy-start.7
  13.2 1.0 copy-done.7
  14.2 0.0 copy-start.5
  14.2 6.0 %channels.3.refs_6_ = bf16[128,2,24,128]{3,2,1,0:T(8,128)(2,1)S(1)} custom-call(s32[257]{0:T(512)S(1)} %pad_add_fusion.first_ref, bf16[2,64,8192]{2,1,0:T(8,128)(2,1)S(1)} %multiply_convert_fusion.refs_0_, bf16[2,64,4096]{2,1,0:T(8,128)(2,1)S(1)} %get-tuple-element.10.refs_1_, bf16[2,64,4096]{2,1,0:T(8,128)(2,1)} %get-tuple-element.9.refs_2_, ...), custom_call_target="tpu_custom_call" | custom-call | flops 1000000000 | bytes 8388608 | tf_op jit(solution)/shard_map/channels/pallas_call | solution.py:177
  20.3 3.5 %collective-permute-done.refs_2_ = bf16[2,64,4096]{2,1,0:T(8,128)(2,1)} collective-permute-done((bf16[2,64,4096]{2,1,0:T(8,128)(2,1)}, bf16[2,64,4096]{2,1,0:T(8,128)(2,1)}, u32[]{:S(2)}, u32[]{:S(2)}) %collective-permute-start) | collective-permute-done | bytes 1048608 | tf_op jit(solution)/shard_map/ppermute | solution.py:313
  23.7 0.0 copy-done.5
  23.7 6.3 %channels.4 = bf16[128,2,48,128]{3,2,1,0:T(8,128)(2,1)S(1)} custom-call(s32[257]{0:T(512)S(1)} %pad_add_fusion.first_ref, bf16[2,64,8192]{2,1,0:T(8,128)(2,1)S(1)} %multiply_convert_fusion.refs_0_, bf16[2,64,4096]{2,1,0:T(8,128)(2,1)S(1)} %get-tuple-element.10.refs_1_, bf16[2,64,4096]{2,1,0:T(8,128)(2,1)} %collective-permute-done.refs_2_, ...), custom_call_target="tpu_custom_call" | custom-call | flops 1000000000 | bytes 8388608 | tf_op jit(solution)/shard_map/channels/pallas_call | solution.py:177
  30.0 0.0 copy-start.1
  30.0 1.7 %copy-done.1 = bf16[128,2,48,128]{3,2,1,0:T(8,128)(2,1)} copy-done((bf16[128,2,48,128]{3,2,1,0:T(8,128)(2,1)}, bf16[128,2,48,128]{3,2,1,0:T(8,128)(2,1)S(1)}, u32[]{:S(2)}) %copy-start.1) | copy-done | bytes 3145752
  31.7 0.0 collective-permute-done.1.refs_3_
  31.7 11.7 %all-to-all-start.1 = ((bf16[128,2,48,128]{3,2,1,0:T(8,128)(2,1)}), bf16[128,2,48,128]{3,2,1,0:T(8,128)(2,1)}, u32[]{:S(2)}, u32[]{:S(2)}) async-start(bf16[128,2,48,128]{3,2,1,0:T(8,128)(2,1)} %copy-done.1), calls=%async_computation.1 | async-start | bytes 6291456 | tf_op jit(solution)/shard_map/all_to_all | solution.py:335
  43.4 0.0 copy-start.6
  43.4 1.1 copy-done.6
  44.5 0.0 copy-start.8
  44.5 1.0 copy-done.8
  45.5 10.1 %channels.5 = bf16[128,2,48,128]{3,2,1,0:T(8,128)(2,1)S(1)} custom-call(s32[257]{0:T(512)S(1)} %pad_add_fusion.first_ref, bf16[2,64,8192]{2,1,0:T(8,128)(2,1)S(1)} %multiply_convert_fusion.refs_0_, bf16[2,64,4096]{2,1,0:T(8,128)(2,1)S(1)} %get-tuple-element.10.refs_1_, bf16[2,64,4096]{2,1,0:T(8,128)(2,1)} %get-tuple-element.9.refs_2_, ...), custom_call_target="tpu_custom_call" | custom-call | flops 2000000000 | bytes 8388608 | tf_op jit(solution)/shard_map/channels/pallas_call | solution.py:177
  55.7 0.0 copy-start
  55.7 1.7 %copy-done = bf16[128,2,48,128]{3,2,1,0:T(8,128)(2,1)} copy-done((bf16[128,2,48,128]{3,2,1,0:T(8,128)(2,1)}, bf16[128,2,48,128]{3,2,1,0:T(8,128)(2,1)S(1)}, u32[]{:S(2)}) %copy-start) | copy-done | bytes 3145752
  57.3 27.4 %all-to-all-done.1.piece = bf16[128,2,48,128]{3,2,1,0:T(8,128)(2,1)} async-done(((bf16[128,2,48,128]{3,2,1,0:T(8,128)(2,1)}), bf16[128,2,48,128]{3,2,1,0:T(8,128)(2,1)}, u32[]{:S(2)}, u32[]{:S(2)}) %all-to-all-start.1) | async-done | bytes 3145760 | tf_op jit(solution)/shard_map/all_to_all | solution.py:335
  84.8 4.6 %all-to-all-start = ((bf16[128,2,48,128]{3,2,1,0:T(8,128)(2,1)}), bf16[128,2,48,128]{3,2,1,0:T(8,128)(2,1)S(1)}, u32[]{:S(2)}, u32[]{:S(2)}) async-start(bf16[128,2,48,128]{3,2,1,0:T(8,128)(2,1)} %copy-done), calls=%async_computation | async-start | bytes 6291456 | tf_op jit(solution)/shard_map/all_to_all | solution.py:338
  89.3 0.1 fusion
  89.5 0.1 dynamic_slice.3.valid_ref
  89.5 10.2 %correlate.2.refs_0_ = f32[2,1024,1024]{2,1,0:T(8,128)S(1)} custom-call(s32[2]{0:T(128)S(1)} %dynamic_slice.3.valid_ref, bf16[128,2,48,128]{3,2,1,0:T(8,128)(2,1)} %all-to-all-done.1.piece), custom_call_target="tpu_custom_call" | custom-call | flops 5000000000 | bytes 19922944 | tf_op jit(solution)/shard_map/correlate/pallas_call | solution.py:277
  99.8 0.0 copy-start.2
  99.8 3.4 %copy-done.2 = f32[2,1024,1024]{2,1,0:T(8,128)} copy-done((f32[2,1024,1024]{2,1,0:T(8,128)}, f32[2,1024,1024]{2,1,0:T(8,128)S(1)}, u32[]{:S(2)}) %copy-start.2) | copy-done | bytes 8388632
  103.2 28.0 %all-to-all-done.piece = bf16[128,2,48,128]{3,2,1,0:T(8,128)(2,1)S(1)} async-done(((bf16[128,2,48,128]{3,2,1,0:T(8,128)(2,1)}), bf16[128,2,48,128]{3,2,1,0:T(8,128)(2,1)S(1)}, u32[]{:S(2)}, u32[]{:S(2)}) %all-to-all-start) | async-done | bytes 3145760 | tf_op jit(solution)/shard_map/all_to_all | solution.py:338
  131.2 0.0 copy-start.3
  131.2 3.4 %copy-done.3 = f32[2,1024,1024]{2,1,0:T(8,128)S(1)} copy-done((f32[2,1024,1024]{2,1,0:T(8,128)S(1)}, f32[2,1024,1024]{2,1,0:T(8,128)}, u32[]{:S(2)}) %copy-start.3) | copy-done | bytes 8388632
  134.5 10.0 %correlate.3 = f32[2,1024,1024]{2,1,0:T(8,128)} custom-call(s32[2]{0:T(128)S(1)} %dynamic_slice.3.valid_ref, bf16[128,2,48,128]{3,2,1,0:T(8,128)(2,1)S(1)} %all-to-all-done.piece, f32[2,1024,1024]{2,1,0:T(8,128)S(1)} %copy-done.3), custom_call_target="tpu_custom_call" | custom-call | flops 5000000000 | bytes 19922944 | tf_op jit(solution)/shard_map/correlate/pallas_call | solution.py:277
  (6 shorter events, 0.0 us)
Async XLA Ops:
  0.9 4.6 %copy-start.10 = (s32[2,64,16384]{2,1,0:T(8,128)S(1)}, s32[2,64,16384]{2,1,0:T(8,128)}, u32[]{:S(2)}) copy-start(s32[2,64,16384]{2,1,0:T(8,128)} %param.6) | copy-start | bytes 25165828
  3.7 28.0 %collective-permute-start.1 = (bf16[2,64,8192]{2,1,0:T(8,128)(2,1)S(1)}, bf16[2,64,8192]{2,1,0:T(8,128)(2,1)}, u32[]{:S(2)}, u32[]{:S(2)}) collective-permute-start(bf16[2,64,8192]{2,1,0:T(8,128)(2,1)S(1)} %multiply_convert_fusion.refs_0_), channel_id=1, source_target_pairs={{0,7},{1,0},{2,1},{3,2},{4,3},{5,4},{6,5},{7,6},{8,15},{9,8},{10,9... | collective-permute-start | bytes 6291464 | tf_op jit(solution)/shard_map/ppermute | solution.py:314
  5.6 6.1 %copy-start.11 = (s32[144]{0:T(256)S(1)}, s32[144]{0:T(256)}, u32[]{:S(2)}) copy-start(s32[144]{0:T(256)} %param.8) | copy-start | bytes 1732
  5.6 6.5 %copy-start.9 = (f32[2,16,8,256]{3,2,1,0:T(8,128)S(1)}, f32[2,16,8,256]{3,2,1,0:T(8,128)}, u32[]{:S(2)}) copy-start(f32[2,16,8,256]{3,2,1,0:T(8,128)} %constant.54.clone.refs_4_.refs_5_) | copy-start | bytes 786436
  7.1 16.6 %collective-permute-start = (bf16[2,64,4096]{2,1,0:T(8,128)(2,1)}, bf16[2,64,4096]{2,1,0:T(8,128)(2,1)}, u32[]{:S(2)}, u32[]{:S(2)}) collective-permute-start(bf16[2,64,4096]{2,1,0:T(8,128)(2,1)} %get-tuple-element.9.refs_2_), channel_id=1, source_target_pairs={{0,1},{1,2},{2,3},{3,4},{4,5},{5,6},{6,7},{8,9},{9,10},{10,11},{11... | collective-permute-start | bytes 3145736 | tf_op jit(solution)/shard_map/ppermute | solution.py:313
  12.1 1.1 copy-start.4
  13.2 1.0 copy-start.7
  14.2 9.5 %copy-start.5 = (f32[5,8,4096]{2,1,0:T(8,128)S(1)}, f32[5,8,4096]{2,1,0:T(8,128)}, u32[]{:S(2)}) copy-start(f32[5,8,4096]{2,1,0:T(8,128)} %constant.53.clone.refs_3_.refs_4_) | copy-start | bytes 1966084
  30.0 1.7 %copy-start.1 = (bf16[128,2,48,128]{3,2,1,0:T(8,128)(2,1)}, bf16[128,2,48,128]{3,2,1,0:T(8,128)(2,1)S(1)}, u32[]{:S(2)}) copy-start(bf16[128,2,48,128]{3,2,1,0:T(8,128)(2,1)S(1)} %channels.4) | copy-start | bytes 9437188
  31.7 53.1 %all-to-all-start.1 = ((bf16[128,2,48,128]{3,2,1,0:T(8,128)(2,1)}), bf16[128,2,48,128]{3,2,1,0:T(8,128)(2,1)}, u32[]{:S(2)}, u32[]{:S(2)}) async-start(bf16[128,2,48,128]{3,2,1,0:T(8,128)(2,1)} %copy-done.1), calls=%async_computation.1 | async-start | bytes 6291456 | tf_op jit(solution)/shard_map/all_to_all | solution.py:335
  43.4 1.1 copy-start.6
  44.5 1.0 copy-start.8
  55.7 1.7 %copy-start = (bf16[128,2,48,128]{3,2,1,0:T(8,128)(2,1)}, bf16[128,2,48,128]{3,2,1,0:T(8,128)(2,1)S(1)}, u32[]{:S(2)}) copy-start(bf16[128,2,48,128]{3,2,1,0:T(8,128)(2,1)S(1)} %channels.5) | copy-start | bytes 9437188
  84.8 46.4 %all-to-all-start = ((bf16[128,2,48,128]{3,2,1,0:T(8,128)(2,1)}), bf16[128,2,48,128]{3,2,1,0:T(8,128)(2,1)S(1)}, u32[]{:S(2)}, u32[]{:S(2)}) async-start(bf16[128,2,48,128]{3,2,1,0:T(8,128)(2,1)} %copy-done), calls=%async_computation | async-start | bytes 6291456 | tf_op jit(solution)/shard_map/all_to_all | solution.py:338
  99.8 3.4 %copy-start.2 = (f32[2,1024,1024]{2,1,0:T(8,128)}, f32[2,1024,1024]{2,1,0:T(8,128)S(1)}, u32[]{:S(2)}) copy-start(f32[2,1024,1024]{2,1,0:T(8,128)S(1)} %correlate.2.refs_0_) | copy-start | bytes 25165828
  131.2 3.4 %copy-start.3 = (f32[2,1024,1024]{2,1,0:T(8,128)S(1)}, f32[2,1024,1024]{2,1,0:T(8,128)}, u32[]{:S(2)}) copy-start(f32[2,1024,1024]{2,1,0:T(8,128)} %copy-done.2) | copy-start | bytes 25165828

commit v4 on v3

--- a/solution.py
+++ b/solution.py
@@ -22,21 +22,15 @@
 TILE = 256
 
 
-def window_table():
+def row_table():
     length = TAPS * F
     steps = np.arange(length, dtype=np.float64)
     centre = (steps + 0.5 - length / 2.0) / F
     taper = 0.5 - 0.5 * np.cos(2.0 * math.pi * (steps + 0.5) / length)
-    table = (np.sinc(centre) * taper).reshape(TAPS, 1, F)
-    table = np.concatenate([table, np.zeros((1, 1, F))], axis=0)
-    return np.broadcast_to(table, (TAPS + 1, 8, F)).astype(np.float32)
-
-
-def twist_table():
-    phase = np.arange(R1)[:, None] * np.arange(R2)[None, :]
-    angle = 2.0 * math.pi * phase / F
-    table = np.stack([np.cos(angle), np.sin(angle)]) / math.sqrt(F)
-    return np.broadcast_to(table[:, :, None, :], (2, R1, 8, R2)).astype(np.float32)
+    taps = (np.sinc(centre) * taper).reshape(TAPS, F)
+    angle = 2.0 * math.pi * (np.arange(R1)[:, None] * np.arange(R2)[None, :]).reshape(1, F) / F
+    rows = [taps, np.cos(angle) / math.sqrt(F), np.sin(angle) / math.sqrt(F), np.zeros((2, F))]
+    return np.concatenate(rows, axis=0).astype(np.float32)
 
 
 def radix_table():
@@ -92,8 +86,8 @@
 
 
 def channel_kernel(plan, count, first_ref, *refs):
-    xs, (window, twist, table) = refs[:count], refs[count : count + 3]
-    prior, (out, turned, spectrum) = refs[count + 3 : -3], refs[-3:]
+    xs, (rows_table, table) = refs[:count], refs[count : count + 2]
+    prior, (out, turned, spectrum) = refs[count + 2 : -3], refs[-3:]
     step = pl.program_id(0)
     spectra = len(plan)
     block = 16
@@ -118,8 +112,10 @@
                             index, place = blocks[tap]
                             shifted = pl.ds(pl.multiple_of(base + n * R2 + place * F, LANES), LANES)
                             value = xs[index][c, members, shifted].astype(jnp.float32)[8 * r : 8 * r + 8]
-                            which = tap if tap >= cut else jnp.where(wrapped, TAPS, tap)
-                            term = window[which, :, lanes] * value
+                            weight = rows_table[tap : tap + 1, lanes]
+                            if tap < cut:
+                                weight = jnp.where(wrapped, 0.0, weight)
+                            term = weight * value
                             total = term if total is None else total + term
                         parts.append(total.astype(jnp.bfloat16).astype(jnp.float32))
                     series.append(tuple(parts))
@@ -127,7 +123,8 @@
                 row = pl.ds(pl.multiple_of(step * block + s * inputs + 8 * r, 8), 8)
                 for m in range(R1):
                     re, im = result[m]
-                    cosine, sine = twist[0, m, :, lanes2], twist[1, m, :, lanes2]
+                    lanes = pl.ds(pl.multiple_of(base + m * R2, LANES), LANES)
+                    cosine, sine = [rows_table[TAPS + k : TAPS + 1 + k, lanes] for k in range(2)]
                     turned[m, row, lanes2] = re * cosine + im * sine
                     turned[m, row, lanes3] = im * cosine - re * sine
         return carry
@@ -167,7 +164,7 @@
         lax.fori_loop(0, out.shape[0], place, 0, unroll=2)
 
 
-def channel_call(plan, first, xs, window, twist, table, prior=()):
+def channel_call(plan, first, xs, rows_table, table, prior=()):
     owners = (first.shape[0] - 1) // CAP
     block = 16
     inputs = xs[0].shape[1]
@@ -180,7 +177,7 @@
         grid_spec=pltpu.PrefetchScalarGridSpec(
             num_scalar_prefetch=1,
             grid=(inputs // block,),
-            in_specs=[held] * (len(xs) + 3 + len(prior)),
+            in_specs=[held] * (len(xs) + 2 + len(prior)),
             out_specs=held,
             scratch_shapes=[
                 pltpu.VMEM((R1, spectra * inputs, 2 * R2), jnp.float32),
@@ -190,7 +187,7 @@
         compiler_params=pltpu.CompilerParams(vmem_limit_bytes=CHANNEL_VMEM),
         cost_estimate=pl.CostEstimate(flops=10**9 * spectra, bytes_accessed=8 * 2**20, transcendentals=0),
         name="channels",
-    )(first, *xs, window, twist, table, *prior)
+    )(first, *xs, rows_table, table, *prior)
 
 
 def correlate_kernel(n_tim, scale, valid_ref, piece, *refs):
@@ -248,10 +245,10 @@
                 imag = jnp.dot(rows_i[which, rows, half:], other, preferred_element_type=jnp.float32)
             value = real if imag is None else imag if real is None else jnp.where(upper, real, imag)
             if partial is not None:
-                value = value + partial[which, rows, lanes]
+                value = value + partial[which, rows, lanes].astype(jnp.float32)
             value = jnp.where(keep, value * scale, 0.0)
             if held:
-                out[which, rows, lanes] = value
+                out[which, rows, lanes] = value.astype(out.dtype)
             else:
                 out[0, :, lanes] = value
 
@@ -276,7 +273,7 @@
     more = [] if partial is None else [partial]
     return pl.pallas_call(
         functools.partial(correlate_kernel, n_tim, scale),
-        out_shape=jax.ShapeDtypeStruct((CAP, width, width), jnp.float32),
+        out_shape=jax.ShapeDtypeStruct((CAP, width, width), jnp.float32 if more else jnp.bfloat16),
         grid_spec=pltpu.PrefetchScalarGridSpec(
             num_scalar_prefetch=1,
             grid=(CAP, width // tile),
@@ -310,6 +307,7 @@
     own01, own2, own3 = samples(0, 2), samples(2, 1), samples(3, 1)
     ahead = [(source, source + 1) for source in range(n_tim - 1)]
     back = [(source, (source - 1) % n_tim) for source in range(n_tim)]
+    own01, own3 = lax.optimization_barrier((own01, own3))
     before = lax.ppermute(own3, "tim", ahead)
     after = lax.ppermute(own01, "tim", back)
 
@@ -321,13 +319,11 @@
     me = lax.axis_index("inp") * n_tim + lax.axis_index("tim")
     mine = lax.dynamic_slice(valid, (me * CAP,), (CAP,))
 
-    window = jnp.asarray(window_table())
-    twist = jnp.asarray(twist_table())
     table = jnp.asarray(radix_table()).astype(jnp.bfloat16)
 
     last = (lax.axis_index("tim") == n_tim - 1).astype(jnp.int32)
     first = jnp.concatenate([first, last[None]])
-    tables = (window, twist, table)
+    tables = (jnp.asarray(row_table()), table)
     x0, x1, x2, x3 = (0, 0), (0, 1), (1, 0), (2, 0)
     third = channel_call([((x0, x1, x2, x3), 0)], first, (own01, own2, own3), *tables)
     near = channel_call([(((2, 0), x0, x1, x2), 0)], first, (own01, own2, before), *tables, prior=(third,))

time: 145 us -> 146 us (level)
  waiting for transfers between devices: 58.9 us -> 65.4 us
  local copies, waits for them, and re-layouts: 14.9 us -> 11.6 us
  starting transfers between devices: 22.3 us -> 20.6 us
    unnamed x24 -> x20, local copies, waits for them, and re-layouts: 14.8 us -> 11.5 us
    ppermute x1, waiting for transfers between devices: 0.01 us -> 2.23 us  [body(): after = lax.ppermute(own01, 'tim', back)]
    all_to_all x1, waiting for transfers between devices: 27.4 us -> 29 us  [body(): lax.all_to_all(near, ('inp', 'tim'), split_axis=0, concat_axis=0, tiled=T...]
  transfers between devices with their start and end apart: 4 -> 4, of which waited for: 3 -> 4; matrix products, arithmetic and copies ran while one was open for 1% -> 0% of each run, Pallas kernels for 23% -> 22%
where the time goes in v4:
time: 146 us; the launch traced here: 145 us
  waiting for transfers between devices  65.4 us (45%)
  Pallas kernels  41.7 us (29%)
  starting transfers between devices  20.6 us (14%)
  local copies, waits for them, and re-layouts  11.6 us (8%)
  other arithmetic  5.65 us (4%)
    all_to_all x1, waiting for transfers between devices, body(): lax.all_to_all(far, ('inp', 'tim'), split_axis=0, concat_axis=0, tiled=True)  29.3 us
    all_to_all x1, waiting for transfers between devices, body(): lax.all_to_all(near, ('inp', 'tim'), split_axis=0, concat_axis=0, tiled=T...  29 us
    pallas_call x3, Pallas kernels, channel_call(): pl.pallas_call(functools.partial(channel_kernel, plan, len(xs)), out_shap...  21.4 us
    pallas_call x2, Pallas kernels, correlate_call(): pl.pallas_call(functools.partial(correlate_kernel, n_tim, scale), out_sha...  20.3 us
    unnamed x20, local copies, waits for them, and re-layouts  11.5 us
    all_to_all x1, starting transfers between devices, body(): lax.all_to_all(near, ('inp', 'tim'), split_axis=0, concat_axis=0, tiled=T...  11.4 us
    ppermute x1, waiting for transfers between devices, body(): before = lax.ppermute(own3, 'tim', ahead)  4.88 us
    all_to_all x1, starting transfers between devices, body(): lax.all_to_all(far, ('inp', 'tim'), split_axis=0, concat_axis=0, tiled=True)  4.57 us
  transfers between devices with their start and end apart: 4, of which 4 were waited for; matrix products, arithmetic and copies ran while one was open for 0% of the time, Pallas kernels for 22%

profile of v4, /device:TPU:1, one launch (start us, length us, event | category | flops | bytes accessed | tf_op | source)
XLA Modules:
  0.0 145.1 jit_solution(9621280211346078490)
XLA Ops:
  0.0 0.7 exponential_multiply_fusion
  0.7 0.2 broadcast_select_fusion
  0.9 0.0 copy-start.8
  0.9 2.8 %multiply_convert_fusion.refs_0_ = bf16[2,64,8192]{2,1,0:T(8,128)(2,1)S(1)} fusion(s32[2,64,16384]{2,1,0:T(8,128)} %param.5, f32[64,8192]{1,0:T(8,128)S(1)} %broadcast_select_fusion), kind=kLoop, calls=%fused_computation | loop fusion | flops 3145728 | bytes 8388608 | tf_op jit(solution)/shard_map/convert_element_type | solution.py:305
  3.7 1.9 %copy-done.8 = s32[2,64,16384]{2,1,0:T(8,128)S(1)} copy-done((s32[2,64,16384]{2,1,0:T(8,128)S(1)}, s32[2,64,16384]{2,1,0:T(8,128)}, u32[]{:S(2)}) %copy-start.8) | copy-done | bytes 8388632
  5.6 0.0 copy-start.9
  5.6 0.0 copy-start.5
  5.6 1.5 %multiply_convert_fusion.1 = (bf16[2,64,4096]{2,1,0:T(8,128)(2,1)S(1)}, bf16[2,64,4096]{2,1,0:T(8,128)(2,1)}) fusion(s32[2,64,16384]{2,1,0:T(8,128)S(1)} %copy-done.8, f32[64]{0:T(128)S(1)} %get-tuple-element.15, f32[64]{0:T(128)S(1)} %get-tuple-element.16), kind=kLoop, calls=%fused_computation.1 | loop fusion | flops 3145728 | bytes 6291968 | tf_op jit(solution)/shard_map/convert_element_type | solution.py:305
  7.1 1.4 collective-permute-start.1
  8.5 3.2 %collective-permute-start = (bf16[2,64,4096]{2,1,0:T(8,128)(2,1)}, bf16[2,64,4096]{2,1,0:T(8,128)(2,1)}, u32[]{:S(2)}, u32[]{:S(2)}) collective-permute-start(bf16[2,64,4096]{2,1,0:T(8,128)(2,1)} %get-tuple-element.10.refs_2_), channel_id=1, source_target_pairs={{0,1},{1,2},{2,3},{3,4},{4,5},{5,6},{6,7},{8,9},{9,10},{10,11},{11... | collective-permute-start | bytes 3145736 | tf_op jit(solution)/shard_map/ppermute | solution.py:311
  11.7 0.0 copy-done.9
  11.7 0.2 convert_reduce_fusion
  11.9 0.1 select_reduce_fusion
  12.1 0.0 copy-done.5
  12.1 0.0 copy-start.2
  12.1 1.0 copy-done.2
  13.1 0.0 copy-start.3
  13.1 5.7 %channels.3.refs_5_ = bf16[128,2,24,128]{3,2,1,0:T(8,128)(2,1)S(1)} custom-call(s32[257]{0:T(512)S(1)} %pad_add_fusion.first_ref, bf16[2,64,8192]{2,1,0:T(8,128)(2,1)S(1)} %multiply_convert_fusion.refs_0_, bf16[2,64,4096]{2,1,0:T(8,128)(2,1)S(1)} %get-tuple-element.13.refs_1_, bf16[2,64,4096]{2,1,0:T(8,128)(2,1)} %get-tuple-element.10.refs_2_, ...), custom_call_target="tpu_custom_call" | custom-call | flops 1000000000 | bytes 8388608 | tf_op jit(solution)/shard_map/channels/pallas_call | solution.py:174
  18.9 4.9 %collective-permute-done.refs_2_ = bf16[2,64,4096]{2,1,0:T(8,128)(2,1)} collective-permute-done((bf16[2,64,4096]{2,1,0:T(8,128)(2,1)}, bf16[2,64,4096]{2,1,0:T(8,128)(2,1)}, u32[]{:S(2)}, u32[]{:S(2)}) %collective-permute-start) | collective-permute-done | bytes 1048608 | tf_op jit(solution)/shard_map/ppermute | solution.py:311
  23.7 0.0 copy-done.3
  23.8 6.0 %channels.4 = bf16[128,2,48,128]{3,2,1,0:T(8,128)(2,1)S(1)} custom-call(s32[257]{0:T(512)S(1)} %pad_add_fusion.first_ref, bf16[2,64,8192]{2,1,0:T(8,128)(2,1)S(1)} %multiply_convert_fusion.refs_0_, bf16[2,64,4096]{2,1,0:T(8,128)(2,1)S(1)} %get-tuple-element.13.refs_1_, bf16[2,64,4096]{2,1,0:T(8,128)(2,1)} %collective-permute-done.refs_2_, ...), custom_call_target="tpu_custom_call" | custom-call | flops 1000000000 | bytes 8388608 | tf_op jit(solution)/shard_map/channels/pallas_call | solution.py:174
  29.7 0.0 copy-start.1
  29.7 1.7 %copy-done.1 = bf16[128,2,48,128]{3,2,1,0:T(8,128)(2,1)} copy-done((bf16[128,2,48,128]{3,2,1,0:T(8,128)(2,1)}, bf16[128,2,48,128]{3,2,1,0:T(8,128)(2,1)S(1)}, u32[]{:S(2)}) %copy-start.1) | copy-done | bytes 3145752
  31.4 2.2 %collective-permute-done.1.refs_3_ = bf16[2,64,8192]{2,1,0:T(8,128)(2,1)} collective-permute-done((bf16[2,64,8192]{2,1,0:T(8,128)(2,1)S(1)}, bf16[2,64,8192]{2,1,0:T(8,128)(2,1)}, u32[]{:S(2)}, u32[]{:S(2)}) %collective-permute-start.1) | collective-permute-done | bytes 2097184 | tf_op jit(solution)/shard_map/ppermute | solution.py:312
  33.6 11.4 %all-to-all-start.1 = ((bf16[128,2,48,128]{3,2,1,0:T(8,128)(2,1)}), bf16[128,2,48,128]{3,2,1,0:T(8,128)(2,1)}, u32[]{:S(2)}, u32[]{:S(2)}) async-start(bf16[128,2,48,128]{3,2,1,0:T(8,128)(2,1)} %copy-done.1), calls=%async_computation.1 | async-start | bytes 6291456 | tf_op jit(solution)/shard_map/all_to_all | solution.py:331
  45.1 0.0 copy-start.4
  45.1 1.0 copy-done.4
  46.1 9.7 %channels.5 = bf16[128,2,48,128]{3,2,1,0:T(8,128)(2,1)S(1)} custom-call(s32[257]{0:T(512)S(1)} %pad_add_fusion.first_ref, bf16[2,64,8192]{2,1,0:T(8,128)(2,1)S(1)} %multiply_convert_fusion.refs_0_, bf16[2,64,4096]{2,1,0:T(8,128)(2,1)S(1)} %get-tuple-element.13.refs_1_, bf16[2,64,4096]{2,1,0:T(8,128)(2,1)} %get-tuple-element.10.refs_2_, ...), custom_call_target="tpu_custom_call" | custom-call | flops 2000000000 | bytes 8388608 | tf_op jit(solution)/shard_map/channels/pallas_call | solution.py:174
  55.8 0.0 copy-start
  55.8 1.7 %copy-done = bf16[128,2,48,128]{3,2,1,0:T(8,128)(2,1)} copy-done((bf16[128,2,48,128]{3,2,1,0:T(8,128)(2,1)}, bf16[128,2,48,128]{3,2,1,0:T(8,128)(2,1)S(1)}, u32[]{:S(2)}) %copy-start) | copy-done | bytes 3145752
  57.5 29.0 %all-to-all-done.1.piece = bf16[128,2,48,128]{3,2,1,0:T(8,128)(2,1)} async-done(((bf16[128,2,48,128]{3,2,1,0:T(8,128)(2,1)}), bf16[128,2,48,128]{3,2,1,0:T(8,128)(2,1)}, u32[]{:S(2)}, u32[]{:S(2)}) %all-to-all-start.1) | async-done | bytes 3145760 | tf_op jit(solution)/shard_map/all_to_all | solution.py:331
  86.4 4.6 %all-to-all-start = ((bf16[128,2,48,128]{3,2,1,0:T(8,128)(2,1)}), bf16[128,2,48,128]{3,2,1,0:T(8,128)(2,1)S(1)}, u32[]{:S(2)}, u32[]{:S(2)}) async-start(bf16[128,2,48,128]{3,2,1,0:T(8,128)(2,1)} %copy-done), calls=%async_computation | async-start | bytes 6291456 | tf_op jit(solution)/shard_map/all_to_all | solution.py:334
  91.0 0.1 fusion
  91.1 0.1 dynamic_slice.3.valid_ref
  91.2 10.3 %correlate.2.refs_0_ = bf16[2,1024,1024]{2,1,0:T(8,128)(2,1)S(1)} custom-call(s32[2]{0:T(128)S(1)} %dynamic_slice.3.valid_ref, bf16[128,2,48,128]{3,2,1,0:T(8,128)(2,1)} %all-to-all-done.1.piece), custom_call_target="tpu_custom_call" | custom-call | flops 5000000000 | bytes 19922944 | tf_op jit(solution)/shard_map/correlate/pallas_call | solution.py:274
  101.5 0.0 copy-start.6
  101.5 2.0 %copy-done.6 = bf16[2,1024,1024]{2,1,0:T(8,128)(2,1)} copy-done((bf16[2,1024,1024]{2,1,0:T(8,128)(2,1)}, bf16[2,1024,1024]{2,1,0:T(8,128)(2,1)S(1)}, u32[]{:S(2)}) %copy-start.6) | copy-done | bytes 4194328
  103.5 29.3 %all-to-all-done.piece = bf16[128,2,48,128]{3,2,1,0:T(8,128)(2,1)S(1)} async-done(((bf16[128,2,48,128]{3,2,1,0:T(8,128)(2,1)}), bf16[128,2,48,128]{3,2,1,0:T(8,128)(2,1)S(1)}, u32[]{:S(2)}, u32[]{:S(2)}) %all-to-all-start) | async-done | bytes 3145760 | tf_op jit(solution)/shard_map/all_to_all | solution.py:334
  132.8 0.0 copy-start.7
  132.8 2.2 %copy-done.7 = bf16[2,1024,1024]{2,1,0:T(8,128)(2,1)S(1)} copy-done((bf16[2,1024,1024]{2,1,0:T(8,128)(2,1)S(1)}, bf16[2,1024,1024]{2,1,0:T(8,128)(2,1)}, u32[]{:S(2)}) %copy-start.7) | copy-done | bytes 4194328
  135.0 10.0 %correlate.3 = f32[2,1024,1024]{2,1,0:T(8,128)} custom-call(s32[2]{0:T(128)S(1)} %dynamic_slice.3.valid_ref, bf16[128,2,48,128]{3,2,1,0:T(8,128)(2,1)S(1)} %all-to-all-done.piece, bf16[2,1024,1024]{2,1,0:T(8,128)(2,1)S(1)} %copy-done.7), custom_call_target="tpu_custom_call" | custom-call | flops 5000000000 | bytes 19922944 | tf_op jit(solution)/shard_map/correlate/pallas_call | solution.py:274
  (6 shorter events, 0.0 us)
Async XLA Ops:
  0.9 4.6 %copy-start.8 = (s32[2,64,16384]{2,1,0:T(8,128)S(1)}, s32[2,64,16384]{2,1,0:T(8,128)}, u32[]{:S(2)}) copy-start(s32[2,64,16384]{2,1,0:T(8,128)} %param.5) | copy-start | bytes 25165828
  5.6 6.2 %copy-start.9 = (s32[144]{0:T(256)S(1)}, s32[144]{0:T(256)}, u32[]{:S(2)}) copy-start(s32[144]{0:T(256)} %param.7) | copy-start | bytes 1732
  5.6 6.5 %copy-start.5 = (f32[8,4096]{1,0:T(8,128)S(1)}, f32[8,4096]{1,0:T(8,128)}, u32[]{:S(2)}) copy-start(f32[8,4096]{1,0:T(8,128)} %constant.52.clone.refs_3_.refs_4_) | copy-start | bytes 393220
  7.1 26.5 %collective-permute-start.1 = (bf16[2,64,8192]{2,1,0:T(8,128)(2,1)S(1)}, bf16[2,64,8192]{2,1,0:T(8,128)(2,1)}, u32[]{:S(2)}, u32[]{:S(2)}) collective-permute-start(bf16[2,64,8192]{2,1,0:T(8,128)(2,1)S(1)} %multiply_convert_fusion.refs_0_), channel_id=1, source_target_pairs={{0,7},{1,0},{2,1},{3,2},{4,3},{5,4},{6,5},{7,6},{8,15},{9,8},{10,9... | collective-permute-start | bytes 6291464 | tf_op jit(solution)/shard_map/ppermute | solution.py:312
  8.5 15.2 %collective-permute-start = (bf16[2,64,4096]{2,1,0:T(8,128)(2,1)}, bf16[2,64,4096]{2,1,0:T(8,128)(2,1)}, u32[]{:S(2)}, u32[]{:S(2)}) collective-permute-start(bf16[2,64,4096]{2,1,0:T(8,128)(2,1)} %get-tuple-element.10.refs_2_), channel_id=1, source_target_pairs={{0,1},{1,2},{2,3},{3,4},{4,5},{5,6},{6,7},{8,9},{9,10},{10,11},{11... | collective-permute-start | bytes 3145736 | tf_op jit(solution)/shard_map/ppermute | solution.py:311
  12.1 1.0 copy-start.2
  13.1 10.6 %copy-start.3 = (bf16[512,512]{1,0:T(8,128)(2,1)S(1)}, bf16[512,512]{1,0:T(8,128)(2,1)}, u32[]{:S(2)}) copy-start(bf16[512,512]{1,0:T(8,128)(2,1)} %constant.54.refs_4_.refs_5_) | copy-start | bytes 1572868
  29.7 1.7 %copy-start.1 = (bf16[128,2,48,128]{3,2,1,0:T(8,128)(2,1)}, bf16[128,2,48,128]{3,2,1,0:T(8,128)(2,1)S(1)}, u32[]{:S(2)}) copy-start(bf16[128,2,48,128]{3,2,1,0:T(8,128)(2,1)S(1)} %channels.4) | copy-start | bytes 9437188
  33.6 52.8 %all-to-all-start.1 = ((bf16[128,2,48,128]{3,2,1,0:T(8,128)(2,1)}), bf16[128,2,48,128]{3,2,1,0:T(8,128)(2,1)}, u32[]{:S(2)}, u32[]{:S(2)}) async-start(bf16[128,2,48,128]{3,2,1,0:T(8,128)(2,1)} %copy-done.1), calls=%async_computation.1 | async-start | bytes 6291456 | tf_op jit(solution)/shard_map/all_to_all | solution.py:331
  45.1 1.0 copy-start.4
  55.8 1.7 %copy-start = (bf16[128,2,48,128]{3,2,1,0:T(8,128)(2,1)}, bf16[128,2,48,128]{3,2,1,0:T(8,128)(2,1)S(1)}, u32[]{:S(2)}) copy-start(bf16[128,2,48,128]{3,2,1,0:T(8,128)(2,1)S(1)} %channels.5) | copy-start | bytes 9437188
  86.4 46.4 %all-to-all-start = ((bf16[128,2,48,128]{3,2,1,0:T(8,128)(2,1)}), bf16[128,2,48,128]{3,2,1,0:T(8,128)(2,1)S(1)}, u32[]{:S(2)}, u32[]{:S(2)}) async-start(bf16[128,2,48,128]{3,2,1,0:T(8,128)(2,1)} %copy-done), calls=%async_computation | async-start | bytes 6291456 | tf_op jit(solution)/shard_map/all_to_all | solution.py:334
  101.5 2.0 %copy-start.6 = (bf16[2,1024,1024]{2,1,0:T(8,128)(2,1)}, bf16[2,1024,1024]{2,1,0:T(8,128)(2,1)S(1)}, u32[]{:S(2)}) copy-start(bf16[2,1024,1024]{2,1,0:T(8,128)(2,1)S(1)} %correlate.2.refs_0_) | copy-start | bytes 12582916
  132.8 2.2 %copy-start.7 = (bf16[2,1024,1024]{2,1,0:T(8,128)(2,1)S(1)}, bf16[2,1024,1024]{2,1,0:T(8,128)(2,1)}, u32[]{:S(2)}) copy-start(bf16[2,1024,1024]{2,1,0:T(8,128)(2,1)} %copy-done.6) | copy-start | bytes 12582916

commit v5 on v4

--- a/solution.py
+++ b/solution.py
@@ -18,7 +18,7 @@
 R2 = 256
 LANES = 128
 CHANNEL_VMEM = 30 * 2**20
-CORRELATE_VMEM = 34 * 2**20
+CORRELATE_VMEM = 50 * 2**20
 TILE = 256
 
 
@@ -95,41 +95,47 @@
     slots = out.shape[0] * out.shape[1]
     wrapped = first_ref[slots] != 0
 
-    def columns(half, carry):
+    def columns(s, blocks, cut, half):
         base = half * LANES
-        members = pl.ds(pl.multiple_of(step * block, block), block)
         lanes2 = pl.ds(pl.multiple_of(base, LANES), LANES)
         lanes3 = pl.ds(pl.multiple_of(base + R2, LANES), LANES)
-        for s, (blocks, cut) in enumerate(plan):
-            for r in range(block // 8):
-                series = []
-                for n in range(R1):
-                    lanes = pl.ds(pl.multiple_of(base + n * R2, LANES), LANES)
-                    parts = []
-                    for c in range(2):
-                        total = None
-                        for tap in range(TAPS):
-                            index, place = blocks[tap]
-                            shifted = pl.ds(pl.multiple_of(base + n * R2 + place * F, LANES), LANES)
-                            value = xs[index][c, members, shifted].astype(jnp.float32)[8 * r : 8 * r + 8]
-                            weight = rows_table[tap : tap + 1, lanes]
-                            if tap < cut:
-                                weight = jnp.where(wrapped, 0.0, weight)
-                            term = weight * value
-                            total = term if total is None else total + term
-                        parts.append(total.astype(jnp.bfloat16).astype(jnp.float32))
-                    series.append(tuple(parts))
-                result = sixteen(series)
-                row = pl.ds(pl.multiple_of(step * block + s * inputs + 8 * r, 8), 8)
-                for m in range(R1):
-                    re, im = result[m]
-                    lanes = pl.ds(pl.multiple_of(base + m * R2, LANES), LANES)
-                    cosine, sine = [rows_table[TAPS + k : TAPS + 1 + k, lanes] for k in range(2)]
-                    turned[m, row, lanes2] = re * cosine + im * sine
-                    turned[m, row, lanes3] = im * cosine - re * sine
-        return carry
-
-    lax.fori_loop(0, R2 // LANES, columns, 0)
+        for r in range(block // 8):
+            series = []
+            for n in range(R1):
+                lanes = pl.ds(pl.multiple_of(base + n * R2, LANES), LANES)
+                parts = []
+                for c in range(2):
+                    total = None
+                    for tap in range(TAPS):
+                        index, skip = blocks[tap]
+                        members = pl.ds(pl.multiple_of(step * block - skip, block), block)
+                        value = xs[index][c, members, lanes].astype(jnp.float32)[8 * r : 8 * r + 8]
+                        weight = rows_table[tap : tap + 1, lanes]
+                        if tap < cut:
+                            weight = jnp.where(wrapped, 0.0, weight)
+                        term = weight * value
+                        total = term if total is None else total + term
+                    parts.append(total.astype(jnp.bfloat16).astype(jnp.float32))
+                series.append(tuple(parts))
+            result = sixteen(series)
+            row = pl.ds(pl.multiple_of(step * block + s * inputs + 8 * r, 8), 8)
+            for m in range(R1):
+                re, im = result[m]
+                lanes = pl.ds(pl.multiple_of(base + m * R2, LANES), LANES)
+                cosine, sine = [rows_table[TAPS + k : TAPS + 1 + k, lanes] for k in range(2)]
+                turned[m, row, lanes2] = re * cosine + im * sine
+                turned[m, row, lanes3] = im * cosine - re * sine
+
+    def filtered(s, blocks, cut):
+        lax.fori_loop(0, R2 // LANES, lambda half, carry: (columns(s, blocks, cut, half), carry)[1], 0)
+
+    middle = pl.num_programs(0) // 2
+    for s, options in enumerate(plan):
+        if len(options) == 1:
+            filtered(s, *options[0])
+        else:
+            pl.when(step < middle)(functools.partial(filtered, s, *options[0]))
+            pl.when(step >= middle)(functools.partial(filtered, s, *options[1]))
 
     @pl.when(step == pl.num_programs(0) - 1)
     def _():
@@ -190,9 +196,13 @@
     )(first, *xs, rows_table, table, *prior)
 
 
-def correlate_kernel(n_tim, scale, valid_ref, piece, *refs):
-    partial = refs[0] if len(refs) == 4 else None
-    out, rows_k, rows_i = refs[-3:]
+def correlate_kernel(n_tim, mixed, scale, valid_ref, piece, *refs):
+    if len(refs) == 6:
+        partial_hbm, out, rows_k, rows_i, partial, arrived = refs
+        fetch = [pltpu.make_async_copy(partial_hbm.at[k], partial.at[k], arrived.at[k]) for k in range(CAP)]
+    else:
+        out, rows_k, rows_i = refs
+        partial = fetch = None
     slot, block = pl.program_id(0), pl.program_id(1)
     depth, width = rows_k.shape[1], rows_k.shape[2]
     held = partial is None
@@ -202,7 +212,7 @@
 
     def arrange(which, q):
         lane = lax.broadcasted_iota(jnp.int32, (2 * AVG, LANES), 1)
-        low = lane < LANES // 2
+        low, lower = lane < LANES // 2, lane % (LANES // 2) < LANES // 4
         lanes = pl.ds(pl.multiple_of(q * LANES, LANES), LANES)
 
         base = 0
@@ -211,6 +221,14 @@
                 [piece[(2 * q + e) * n_tim + 2 * u + v, which].astype(jnp.float32) for v in range(2)]
                 for e in range(2)
             ]
+            if mixed:
+                for e in range(2):
+                    for v in range(2):
+                        later = (2 * u + v + 1) % n_tim
+                        other = piece[(2 * q + e) * n_tim + later, which].astype(jnp.float32)[AVG:]
+                        mine = group[e][v]
+                        turn = jnp.where(lower[:AVG], other, mine[AVG:])
+                        group[e][v] = jnp.concatenate([mine[:AVG], turn], axis=0)
             for s in range(piece.shape[2] // AVG):
                 even, odd = [
                     jnp.concatenate([group[e][v][AVG * s : AVG * s + AVG] for v in range(2)], axis=0)
@@ -227,7 +245,14 @@
 
     @pl.when(jnp.logical_and(slot == 0, block == 0))
     def _():
+        if fetch is not None:
+            for copy in fetch:
+                copy.start()
         lax.fori_loop(0, width // LANES, lambda q, carry: (arrange(0, q), carry)[1], 0)
+
+    if fetch is not None:
+        for which in range(CAP):
+            pl.when(jnp.logical_and(slot == which, block == 0))(fetch[which].wait)
 
     def strip(which, i):
         upper = lax.broadcasted_iota(jnp.int32, (tile, tile), 0) <= lax.broadcasted_iota(
@@ -264,7 +289,7 @@
                 strip(which, i)
 
 
-def correlate_call(n_inp, n_tim, scale, valid, piece, partial=None):
+def correlate_call(n_inp, n_tim, mixed, scale, valid, piece, partial=None):
     width = n_inp * LANES // 2
     depth = n_tim * piece.shape[2] * 2
     tile = TILE
@@ -272,17 +297,19 @@
     held = pl.BlockSpec(memory_space=pltpu.VMEM)
     more = [] if partial is None else [partial]
     return pl.pallas_call(
-        functools.partial(correlate_kernel, n_tim, scale),
+        functools.partial(correlate_kernel, n_tim, mixed, scale),
         out_shape=jax.ShapeDtypeStruct((CAP, width, width), jnp.float32 if more else jnp.bfloat16),
         grid_spec=pltpu.PrefetchScalarGridSpec(
             num_scalar_prefetch=1,
             grid=(CAP, width // tile),
-            in_specs=[held] + [held] * len(more),
+            in_specs=[held] + [pl.BlockSpec(memory_space=pl.ANY)] * len(more),
             out_specs=block if more else held,
             scratch_shapes=[
                 pltpu.VMEM((CAP, depth, width), jnp.bfloat16),
                 pltpu.VMEM((CAP, width, depth + depth // 2), jnp.bfloat16),
-            ],
+            ]
+            + [pltpu.VMEM(p.shape, p.dtype) for p in more]
+            + [pltpu.SemaphoreType.DMA((CAP,)) for _ in more],
         ),
         compiler_params=pltpu.CompilerParams(vmem_limit_bytes=CORRELATE_VMEM),
         cost_estimate=pl.CostEstimate(flops=5 * 10**9, bytes_accessed=19 * 2**20, transcendentals=0),
@@ -296,20 +323,19 @@
     devices = n_inp * n_tim
     spec_dev = voltages.shape[2] // F
     scale = jnp.exp2(scale_exps.astype(jnp.float32)) / 128.0
-    lane = lax.broadcasted_iota(jnp.int32, (1, 1, 2 * F), 2)
-
-    def samples(s, count):
-        factor = scale[None, :, s : s + 1]
-        if count == 2:
-            factor = jnp.where(lane < F, factor, scale[None, :, s + 1 : s + 2])
-        return (voltages[:, :, s * F : (s + count) * F].astype(jnp.float32) * factor).astype(jnp.bfloat16)
-
-    own01, own2, own3 = samples(0, 2), samples(2, 1), samples(3, 1)
+    own = [
+        (voltages[:, :, s * F : (s + 1) * F].astype(jnp.float32) * scale[None, :, s : s + 1]).astype(
+            jnp.bfloat16
+        )
+        for s in range(spec_dev)
+    ]
     ahead = [(source, source + 1) for source in range(n_tim - 1)]
     back = [(source, (source - 1) % n_tim) for source in range(n_tim)]
-    own01, own3 = lax.optimization_barrier((own01, own3))
-    before = lax.ppermute(own3, "tim", ahead)
-    after = lax.ppermute(own01, "tim", back)
+    half = voltages.shape[1] // 2
+    minus1 = lax.ppermute(own[3], "tim", ahead)
+    plus0 = lax.ppermute(own[0], "tim", back)
+    minus2 = lax.ppermute(own[2][:, :half], "tim", ahead)
+    plus1 = lax.ppermute(own[1][:, half:], "tim", back)
 
     rows = owner_rows(owner_table, CAP)
     match = rows[None, :] == jnp.arange(devices * CAP, dtype=jnp.int32)[:, None]
@@ -324,16 +350,17 @@
     last = (lax.axis_index("tim") == n_tim - 1).astype(jnp.int32)
     first = jnp.concatenate([first, last[None]])
     tables = (jnp.asarray(row_table()), table)
-    x0, x1, x2, x3 = (0, 0), (0, 1), (1, 0), (2, 0)
-    third = channel_call([((x0, x1, x2, x3), 0)], first, (own01, own2, own3), *tables)
-    near = channel_call([(((2, 0), x0, x1, x2), 0)], first, (own01, own2, before), *tables, prior=(third,))
-    near, after = lax.optimization_barrier((near, after))
+    x0, x1, x2, x3 = [(s, 0) for s in range(spec_dev)]
+    third = channel_call([[((x0, x1, x2, x3), 0)]], first, own, *tables)
+    near = channel_call([[(((3, 0), x0, x1, x2), 0)]], first, (*own[:3], minus1), *tables, prior=(third,))
+    near, plus0, minus2, plus1 = lax.optimization_barrier((near, plus0, minus2, plus1))
     near = lax.all_to_all(near, ("inp", "tim"), split_axis=0, concat_axis=0, tiled=True)
-    plan = [((x1, x2, x3, (3, 0)), 3), ((x2, x3, (3, 0), (3, 1)), 2)]
-    far = channel_call(plan, first, (own01, own2, own3, after), *tables)
+    m1, m2, p0, p1 = (4, 0), (5, 0), (6, 0), (7, half)
+    plan = [[((x1, x2, x3, p0), 3)], [((m2, m1, x0, x1), 0), ((x2, x3, p0, p1), 2)]]
+    far = channel_call(plan, first, (*own, minus1, minus2, plus0, plus1), *tables)
     far = lax.all_to_all(far, ("inp", "tim"), split_axis=0, concat_axis=0, tiled=True)
-    partial = correlate_call(n_inp, n_tim, 1.0, mine, near)
-    return correlate_call(n_inp, n_tim, 1.0 / (n_tim * spec_dev * AVG), mine, far, partial)
+    partial = correlate_call(n_inp, n_tim, False, 1.0, mine, near)
+    return correlate_call(n_inp, n_tim, True, 1.0 / (n_tim * spec_dev * AVG), mine, far, partial)
 
 
 def solution(mesh):

time: 146 us -> 141 us (0.966)
  waiting for transfers between devices: 65.4 us -> 58 us
  local copies, waits for them, and re-layouts: 11.6 us -> 7.15 us
  starting transfers between devices: 20.6 us -> 24.1 us
  Pallas kernels: 41.7 us -> 44.2 us
    ppermute x2 -> x4, waiting for transfers between devices: 7.11 us -> 0.01 us  [the longest x1 0.01 us: body(): minus1 = lax.ppermute(own[3], 'tim', ahead)]
    unnamed x20 -> x14, local copies, waits for them, and re-layouts: 11.5 us -> 5.38 us
    ppermute x2 -> x4, starting transfers between devices: 4.59 us -> 8.37 us  [the longest x1 4.72 us: body(): minus1 = lax.ppermute(own[3], 'tim', ahead)]
    pallas_call x2, Pallas kernels: 20.3 us -> 22.3 us  [correlate_call(): pl.pallas_call(functools.partial(correlate_kernel, n_tim, mixed, scale),...]
    slice x0 -> x2, local copies, waits for them, and re-layouts: none -> 1.68 us  [the longest x1 0.85 us: body(): minus2 = lax.ppermute(own[2][:, :half], 'tim', ahead)]
    convert_element_type x2 -> x1, other arithmetic: 4.31 us -> 5.78 us  [body(): (voltages[:, :, s * F:(s + 1) * F].astype(jnp.float32) * scale[None, :, s...]
  transfers between devices with their start and end apart: 4 -> 6, of which waited for: 4 -> 2; matrix products, arithmetic and copies ran while one was open for 0% -> 2% of each run, Pallas kernels for 22% -> 24%
where the time goes in v5:
time: 141 us
  waiting for transfers between devices  58 us (41%)
  Pallas kernels  44.2 us (31%)
  starting transfers between devices  24.1 us (17%)
  local copies, waits for them, and re-layouts  7.15 us (5%)
  other arithmetic  6.89 us (5%)
    all_to_all x1, waiting for transfers between devices, body(): lax.all_to_all(far, ('inp', 'tim'), split_axis=0, concat_axis=0, tiled=True)  29.4 us
    all_to_all x1, waiting for transfers between devices, body(): lax.all_to_all(near, ('inp', 'tim'), split_axis=0, concat_axis=0, tiled=T...  28.5 us
    pallas_call x2, Pallas kernels, correlate_call(): pl.pallas_call(functools.partial(correlate_kernel, n_tim, mixed, scale),...  22.3 us
    pallas_call x3, Pallas kernels, channel_call(): pl.pallas_call(functools.partial(channel_kernel, plan, len(xs)), out_shap...  21.9 us
    all_to_all x1, starting transfers between devices, body(): lax.all_to_all(near, ('inp', 'tim'), split_axis=0, concat_axis=0, tiled=T...  11.2 us
    convert_element_type x1, other arithmetic, body(): (voltages[:, :, s * F:(s + 1) * F].astype(jnp.float32) * scale[None, :, s...  5.78 us
    unnamed x14, local copies, waits for them, and re-layouts  5.38 us
    ppermute x1, starting transfers between devices, body(): minus1 = lax.ppermute(own[3], 'tim', ahead)  4.72 us
  transfers between devices with their start and end apart: 6, of which 2 were waited for; matrix products, arithmetic and copies ran while one was open for 2% of the time, Pallas kernels for 24%

profile of v5, /device:TPU:1, one launch (start us, length us, event | category | flops | bytes accessed | tf_op | source)
XLA Modules:
  0.0 140.6 jit_solution(5673043220306252554)
XLA Ops:
  0.0 0.7 exponential_multiply_fusion
  0.7 5.8 %multiply_convert_fusion = (bf16[2,64,4096]{2,1,0:T(8,128)(2,1)}, bf16[2,64,4096]{2,1,0:T(8,128)(2,1)S(1)}, bf16[2,64,4096]{2,1,0:T(8,128)(2,1)S(1)}, bf16[2,64,4096]{2,1,0:T(8,128)(2,1)S(1)}) fusion(s32[2,64,16384]{2,1,0:T(8,128)} %param.5, f32[64]{0:T(128)S(1)} %get-tuple-element.17, f32[64]{0:T(128)S(1)} %get-tuple-element.19, f32[64]{0:T(128)S(1)} %get-tuple-element.20, ...), kind=kLoop, calls=%fused_computation | loop fusion | flops 6291456 | bytes 12583936 | tf_op jit(solution)/shard_map/convert_element_type | solution.py:327
  6.5 0.0 copy-start.6
  6.5 0.0 copy-start.5
  6.5 4.7 %collective-permute-start = (bf16[2,64,4096]{2,1,0:T(8,128)(2,1)}, bf16[2,64,4096]{2,1,0:T(8,128)(2,1)}, u32[]{:S(2)}, u32[]{:S(2)}) collective-permute-start(bf16[2,64,4096]{2,1,0:T(8,128)(2,1)} %get-tuple-element.13.refs_3_), channel_id=1, source_target_pairs={{0,1},{1,2},{2,3},{3,4},{4,5},{5,6},{6,7},{8,9},{9,10},{10,11},{11... | collective-permute-start | bytes 3145736 | tf_op jit(solution)/shard_map/ppermute | solution.py:335
  11.2 0.0 collective-permute-start.1
  11.2 0.8 slice.40
  12.1 3.6 %collective-permute-start.2 = (bf16[2,32,4096]{2,1,0:T(8,128)(2,1)}, bf16[2,32,4096]{2,1,0:T(8,128)(2,1)}, u32[]{:S(2)}, u32[]{:S(2)}) collective-permute-start(bf16[2,32,4096]{2,1,0:T(8,128)(2,1)} %slice.40), channel_id=1, source_target_pairs={{0,1},{1,2},{2,3},{3,4},{4,5},{5,6},{6,7},{8,9},{9,10},{10,11},{11... | collective-permute-start | bytes 1572872 | tf_op jit(solution)/shard_map/ppermute | solution.py:337
  15.7 0.8 slice.41
  16.5 0.0 collective-permute-start.3
  16.6 0.0 copy-done.6
  16.6 0.2 convert_reduce_fusion
  16.8 0.1 select_reduce_fusion
  16.9 0.0 copy-done.5
  16.9 0.0 copy-start.2
  16.9 1.0 copy-done.2
  18.0 0.0 copy-start.3
  18.0 5.8 %channels.3.refs_6_ = bf16[128,2,24,128]{3,2,1,0:T(8,128)(2,1)S(1)} custom-call(s32[257]{0:T(512)S(1)} %pad_add_fusion.first_ref, bf16[2,64,4096]{2,1,0:T(8,128)(2,1)S(1)} %get-tuple-element.15.refs_0_, bf16[2,64,4096]{2,1,0:T(8,128)(2,1)S(1)} %get-tuple-element.14.refs_1_, bf16[2,64,4096]{2,1,0:T(8,128)(2,1)S(1)} %get-tuple-element.16.refs_2_, ...), custom_call_target="tpu_custom_call" | custom-call | flops 1000000000 | bytes 8388608 | tf_op jit(solution)/shard_map/channels/pallas_call | solution.py:180
  23.7 0.0 collective-permute-done.refs_3_.refs_4_
  23.7 0.0 copy-done.3
  23.7 6.0 %channels.4 = bf16[128,2,48,128]{3,2,1,0:T(8,128)(2,1)S(1)} custom-call(s32[257]{0:T(512)S(1)} %pad_add_fusion.first_ref, bf16[2,64,4096]{2,1,0:T(8,128)(2,1)S(1)} %get-tuple-element.15.refs_0_, bf16[2,64,4096]{2,1,0:T(8,128)(2,1)S(1)} %get-tuple-element.14.refs_1_, bf16[2,64,4096]{2,1,0:T(8,128)(2,1)S(1)} %get-tuple-element.16.refs_2_, ...), custom_call_target="tpu_custom_call" | custom-call | flops 1000000000 | bytes 8388608 | tf_op jit(solution)/shard_map/channels/pallas_call | solution.py:180
  29.8 0.0 copy-start.1
  29.8 1.6 %copy-done.1 = bf16[128,2,48,128]{3,2,1,0:T(8,128)(2,1)} copy-done((bf16[128,2,48,128]{3,2,1,0:T(8,128)(2,1)}, bf16[128,2,48,128]{3,2,1,0:T(8,128)(2,1)S(1)}, u32[]{:S(2)}) %copy-start.1) | copy-done | bytes 3145752
  31.4 0.0 collective-permute-done.2.refs_5_
  31.4 0.0 collective-permute-done.3.refs_7_
  31.4 0.0 collective-permute-done.1.refs_6_
  31.4 11.2 %all-to-all-start.1 = ((bf16[128,2,48,128]{3,2,1,0:T(8,128)(2,1)}), bf16[128,2,48,128]{3,2,1,0:T(8,128)(2,1)}, u32[]{:S(2)}, u32[]{:S(2)}) async-start(bf16[128,2,48,128]{3,2,1,0:T(8,128)(2,1)} %copy-done.1), calls=%async_computation.1 | async-start | bytes 6291456 | tf_op jit(solution)/shard_map/all_to_all | solution.py:357
  42.6 0.0 copy-start.4
  42.6 1.0 copy-done.4
  43.7 10.1 %channels.5 = bf16[128,2,48,128]{3,2,1,0:T(8,128)(2,1)S(1)} custom-call(s32[257]{0:T(512)S(1)} %pad_add_fusion.first_ref, bf16[2,64,4096]{2,1,0:T(8,128)(2,1)S(1)} %get-tuple-element.15.refs_0_, bf16[2,64,4096]{2,1,0:T(8,128)(2,1)S(1)} %get-tuple-element.14.refs_1_, bf16[2,64,4096]{2,1,0:T(8,128)(2,1)S(1)} %get-tuple-element.16.refs_2_, ...), custom_call_target="tpu_custom_call" | custom-call | flops 2000000000 | bytes 8388608 | tf_op jit(solution)/shard_map/channels/pallas_call | solution.py:180
  53.8 0.0 copy-start
  53.8 1.7 %copy-done = bf16[128,2,48,128]{3,2,1,0:T(8,128)(2,1)} copy-done((bf16[128,2,48,128]{3,2,1,0:T(8,128)(2,1)}, bf16[128,2,48,128]{3,2,1,0:T(8,128)(2,1)S(1)}, u32[]{:S(2)}) %copy-start) | copy-done | bytes 3145752
  55.5 28.5 %all-to-all-done.1.piece = bf16[128,2,48,128]{3,2,1,0:T(8,128)(2,1)} async-done(((bf16[128,2,48,128]{3,2,1,0:T(8,128)(2,1)}), bf16[128,2,48,128]{3,2,1,0:T(8,128)(2,1)}, u32[]{:S(2)}, u32[]{:S(2)}) %all-to-all-start.1) | async-done | bytes 3145760 | tf_op jit(solution)/shard_map/all_to_all | solution.py:357
  84.0 4.6 %all-to-all-start = ((bf16[128,2,48,128]{3,2,1,0:T(8,128)(2,1)}), bf16[128,2,48,128]{3,2,1,0:T(8,128)(2,1)S(1)}, u32[]{:S(2)}, u32[]{:S(2)}) async-start(bf16[128,2,48,128]{3,2,1,0:T(8,128)(2,1)} %copy-done), calls=%async_computation | async-start | bytes 6291456 | tf_op jit(solution)/shard_map/all_to_all | solution.py:361
  88.6 0.1 fusion
  88.7 0.1 dynamic_slice.3.valid_ref
  88.8 12.2 %correlate.2.refs_0_ = bf16[2,1024,1024]{2,1,0:T(8,128)(2,1)} custom-call(s32[2]{0:T(128)S(1)} %dynamic_slice.3.valid_ref, bf16[128,2,48,128]{3,2,1,0:T(8,128)(2,1)} %all-to-all-done.1.piece), custom_call_target="tpu_custom_call" | custom-call | flops 5000000000 | bytes 19922944 | tf_op jit(solution)/shard_map/correlate/pallas_call | solution.py:299
  101.0 29.4 %all-to-all-done.piece = bf16[128,2,48,128]{3,2,1,0:T(8,128)(2,1)S(1)} async-done(((bf16[128,2,48,128]{3,2,1,0:T(8,128)(2,1)}), bf16[128,2,48,128]{3,2,1,0:T(8,128)(2,1)S(1)}, u32[]{:S(2)}, u32[]{:S(2)}) %all-to-all-start) | async-done | bytes 3145760 | tf_op jit(solution)/shard_map/all_to_all | solution.py:361
  130.4 10.1 %correlate.3 = f32[2,1024,1024]{2,1,0:T(8,128)} custom-call(s32[2]{0:T(128)S(1)} %dynamic_slice.3.valid_ref, bf16[128,2,48,128]{3,2,1,0:T(8,128)(2,1)S(1)} %all-to-all-done.piece, bf16[2,1024,1024]{2,1,0:T(8,128)(2,1)} %correlate.2.refs_0_), custom_call_target="tpu_custom_call" | custom-call | flops 5000000000 | bytes 19922944 | tf_op jit(solution)/shard_map/correlate/pallas_call | solution.py:299
  (5 shorter events, 0.0 us)
Async XLA Ops:
  6.5 10.1 %copy-start.6 = (s32[144]{0:T(256)S(1)}, s32[144]{0:T(256)}, u32[]{:S(2)}) copy-start(s32[144]{0:T(256)} %param.7) | copy-start | bytes 1732
  6.5 10.4 %copy-start.5 = (f32[8,4096]{1,0:T(8,128)S(1)}, f32[8,4096]{1,0:T(8,128)}, u32[]{:S(2)}) copy-start(f32[8,4096]{1,0:T(8,128)} %constant.51.clone.refs_4_.refs_8_) | copy-start | bytes 393220
  6.5 17.2 %collective-permute-start = (bf16[2,64,4096]{2,1,0:T(8,128)(2,1)}, bf16[2,64,4096]{2,1,0:T(8,128)(2,1)}, u32[]{:S(2)}, u32[]{:S(2)}) collective-permute-start(bf16[2,64,4096]{2,1,0:T(8,128)(2,1)} %get-tuple-element.13.refs_3_), channel_id=1, source_target_pairs={{0,1},{1,2},{2,3},{3,4},{4,5},{5,6},{6,7},{8,9},{9,10},{10,11},{11... | collective-permute-start | bytes 3145736 | tf_op jit(solution)/shard_map/ppermute | solution.py:335
  11.2 20.2 %collective-permute-start.1 = (bf16[2,64,4096]{2,1,0:T(8,128)(2,1)S(1)}, bf16[2,64,4096]{2,1,0:T(8,128)(2,1)}, u32[]{:S(2)}, u32[]{:S(2)}) collective-permute-start(bf16[2,64,4096]{2,1,0:T(8,128)(2,1)S(1)} %get-tuple-element.15.refs_0_), channel_id=1, source_target_pairs={{0,7},{1,0},{2,1},{3,2},{4,3},{5,4},{6,5},{7,6},{8,15},{9,8},{10,9... | collective-permute-start | bytes 3145736 | tf_op jit(solution)/shard_map/ppermute | solution.py:336
  12.1 19.3 %collective-permute-start.2 = (bf16[2,32,4096]{2,1,0:T(8,128)(2,1)}, bf16[2,32,4096]{2,1,0:T(8,128)(2,1)}, u32[]{:S(2)}, u32[]{:S(2)}) collective-permute-start(bf16[2,32,4096]{2,1,0:T(8,128)(2,1)} %slice.40), channel_id=1, source_target_pairs={{0,1},{1,2},{2,3},{3,4},{4,5},{5,6},{6,7},{8,9},{9,10},{10,11},{11... | collective-permute-start | bytes 1572872 | tf_op jit(solution)/shard_map/ppermute | solution.py:337
  16.5 14.9 %collective-permute-start.3 = (bf16[2,32,4096]{2,1,0:T(8,128)(2,1)}, bf16[2,32,4096]{2,1,0:T(8,128)(2,1)}, u32[]{:S(2)}, u32[]{:S(2)}) collective-permute-start(bf16[2,32,4096]{2,1,0:T(8,128)(2,1)} %slice.41), channel_id=1, source_target_pairs={{0,7},{1,0},{2,1},{3,2},{4,3},{5,4},{6,5},{7,6},{8,15},{9,8},{10,9... | collective-permute-start | bytes 1572872 | tf_op jit(solution)/shard_map/ppermute | solution.py:338
  16.9 1.0 copy-start.2
  18.0 5.8 %copy-start.3 = (bf16[512,512]{1,0:T(8,128)(2,1)S(1)}, bf16[512,512]{1,0:T(8,128)(2,1)}, u32[]{:S(2)}) copy-start(bf16[512,512]{1,0:T(8,128)(2,1)} %constant.53.refs_5_.refs_9_) | copy-start | bytes 1572868
  29.8 1.6 %copy-start.1 = (bf16[128,2,48,128]{3,2,1,0:T(8,128)(2,1)}, bf16[128,2,48,128]{3,2,1,0:T(8,128)(2,1)S(1)}, u32[]{:S(2)}) copy-start(bf16[128,2,48,128]{3,2,1,0:T(8,128)(2,1)S(1)} %channels.4) | copy-start | bytes 9437188
  31.4 52.6 %all-to-all-start.1 = ((bf16[128,2,48,128]{3,2,1,0:T(8,128)(2,1)}), bf16[128,2,48,128]{3,2,1,0:T(8,128)(2,1)}, u32[]{:S(2)}, u32[]{:S(2)}) async-start(bf16[128,2,48,128]{3,2,1,0:T(8,128)(2,1)} %copy-done.1), calls=%async_computation.1 | async-start | bytes 6291456 | tf_op jit(solution)/shard_map/all_to_all | solution.py:357
  42.6 1.0 copy-start.4
  53.8 1.7 %copy-start = (bf16[128,2,48,128]{3,2,1,0:T(8,128)(2,1)}, bf16[128,2,48,128]{3,2,1,0:T(8,128)(2,1)S(1)}, u32[]{:S(2)}) copy-start(bf16[128,2,48,128]{3,2,1,0:T(8,128)(2,1)S(1)} %channels.5) | copy-start | bytes 9437188
  84.0 46.4 %all-to-all-start = ((bf16[128,2,48,128]{3,2,1,0:T(8,128)(2,1)}), bf16[128,2,48,128]{3,2,1,0:T(8,128)(2,1)S(1)}, u32[]{:S(2)}, u32[]{:S(2)}) async-start(bf16[128,2,48,128]{3,2,1,0:T(8,128)(2,1)} %copy-done), calls=%async_computation | async-start | bytes 6291456 | tf_op jit(solution)/shard_map/all_to_all | solution.py:361

commit v6 on v5

--- a/solution.py
+++ b/solution.py
@@ -17,6 +17,7 @@
 R1 = 16
 R2 = 256
 LANES = 128
+SAMPLE_VMEM = 46 * 2**20
 CHANNEL_VMEM = 30 * 2**20
 CORRELATE_VMEM = 50 * 2**20
 TILE = 256
@@ -83,6 +84,47 @@
         for d in range(4):
             out[c + 4 * d] = row[d]
     return out
+
+
+def sample_kernel(exps, voltages, *outs):
+    wholes, low2, high1 = outs[:-2], outs[-2], outs[-1]
+    step, block = pl.program_id(0), voltages.shape[1]
+    half = low2.shape[1]
+    rows = pl.ds(pl.multiple_of(step * block, block), block)
+    factor = jnp.left_shift(1, exps[rows, :]).astype(jnp.float32) * (1.0 / 128.0)
+    for s, whole in enumerate(wholes):
+        for c in range(2):
+            value = voltages[c, :, s * F : (s + 1) * F].astype(jnp.float32) * factor[:, s : s + 1]
+            value = value.astype(jnp.bfloat16)
+            whole[c, rows, :] = value
+            if s == 2:
+
+                @pl.when(step * block < half)
+                def _():
+                    low2[c, rows, :] = value
+
+            if s == 1:
+
+                @pl.when(step * block >= half)
+                def _():
+                    high1[c, pl.ds(pl.multiple_of(step * block - half, block), block), :] = value
+
+
+def sample_call(voltages, exps):
+    inputs, spectra = exps.shape
+    block = 16
+    held = pl.BlockSpec(memory_space=pltpu.VMEM)
+    shapes = [(2, inputs, F)] * spectra + [(2, inputs // 2, F)] * 2
+    return pl.pallas_call(
+        sample_kernel,
+        out_shape=[jax.ShapeDtypeStruct(shape, jnp.bfloat16) for shape in shapes],
+        grid=(inputs // block,),
+        in_specs=[held, pl.BlockSpec((2, block, spectra * F), lambda i: (0, i, 0))],
+        out_specs=[held] * len(shapes),
+        compiler_params=pltpu.CompilerParams(vmem_limit_bytes=SAMPLE_VMEM),
+        cost_estimate=pl.CostEstimate(flops=10**7, bytes_accessed=13 * 2**20, transcendentals=0),
+        name="samples",
+    )(exps, voltages)
 
 
 def channel_kernel(plan, count, first_ref, *refs):
@@ -322,20 +364,14 @@
     n_tim = lax.axis_size("tim")
     devices = n_inp * n_tim
     spec_dev = voltages.shape[2] // F
-    scale = jnp.exp2(scale_exps.astype(jnp.float32)) / 128.0
-    own = [
-        (voltages[:, :, s * F : (s + 1) * F].astype(jnp.float32) * scale[None, :, s : s + 1]).astype(
-            jnp.bfloat16
-        )
-        for s in range(spec_dev)
-    ]
+    *own, low2, high1 = sample_call(voltages, scale_exps)
     ahead = [(source, source + 1) for source in range(n_tim - 1)]
     back = [(source, (source - 1) % n_tim) for source in range(n_tim)]
     half = voltages.shape[1] // 2
     minus1 = lax.ppermute(own[3], "tim", ahead)
     plus0 = lax.ppermute(own[0], "tim", back)
-    minus2 = lax.ppermute(own[2][:, :half], "tim", ahead)
-    plus1 = lax.ppermute(own[1][:, half:], "tim", back)
+    minus2 = lax.ppermute(low2, "tim", ahead)
+    plus1 = lax.ppermute(high1, "tim", back)
 
     rows = owner_rows(owner_table, CAP)
     match = rows[None, :] == jnp.arange(devices * CAP, dtype=jnp.int32)[:, None]

time: 141 us -> 141 us (level)
  Pallas kernels: 44.2 us -> 53.7 us
  other arithmetic: 6.89 us -> 0.43 us
  local copies, waits for them, and re-layouts: 7.15 us -> 2.93 us
    pallas_call x0 -> x1, Pallas kernels: none -> 6.06 us  [sample_call(): pl.pallas_call(sample_kernel, out_shape=[jax.ShapeDtypeStruct(shape, jnp....]
    convert_element_type x1 -> x0, other arithmetic: 5.78 us -> none  [body(): (voltages[:, :, s * F:(s + 1) * F].astype(jnp.float32) * scale[None, :, s...]
    pallas_call x3, Pallas kernels: 21.9 us -> 25.3 us  [channel_call(): pl.pallas_call(functools.partial(channel_kernel, plan, len(xs)), out_shap...]
    unnamed x14 -> x9, local copies, waits for them, and re-layouts: 5.38 us -> 2.85 us
    slice x2 -> x0, local copies, waits for them, and re-layouts: 1.68 us -> none  [the longest x1 0.85 us: body(): minus2 = lax.ppermute(own[2][:, :half], 'tim', ahead)]
  transfers between devices with their start and end apart: 6 -> 6, of which waited for: 2 -> 4; matrix products, arithmetic and copies ran while one was open for 2% -> 0% of each run, Pallas kernels for 24% -> 27%
where the time goes in v6:
time: 141 us
  waiting for transfers between devices  59.3 us (42%)
  Pallas kernels  53.7 us (38%)
  starting transfers between devices  24.2 us (17%)
  local copies, waits for them, and re-layouts  2.93 us (2%)
    all_to_all x1, waiting for transfers between devices, body(): lax.all_to_all(far, ('inp', 'tim'), split_axis=0, concat_axis=0, tiled=True)  29.4 us
    all_to_all x1, waiting for transfers between devices, body(): lax.all_to_all(near, ('inp', 'tim'), split_axis=0, concat_axis=0, tiled=T...  28.5 us
    pallas_call x3, Pallas kernels, channel_call(): pl.pallas_call(functools.partial(channel_kernel, plan, len(xs)), out_shap...  25.3 us
    pallas_call x2, Pallas kernels, correlate_call(): pl.pallas_call(functools.partial(correlate_kernel, n_tim, mixed, scale),...  22.3 us
    all_to_all x1, starting transfers between devices, body(): lax.all_to_all(near, ('inp', 'tim'), split_axis=0, concat_axis=0, tiled=T...  11.4 us
    pallas_call x1, Pallas kernels, sample_call(): pl.pallas_call(sample_kernel, out_shape=[jax.ShapeDtypeStruct(shape, jnp....  6.06 us
    ppermute x1, starting transfers between devices, body(): minus1 = lax.ppermute(own[3], 'tim', ahead)  4.58 us
    all_to_all x1, starting transfers between devices, body(): lax.all_to_all(far, ('inp', 'tim'), split_axis=0, concat_axis=0, tiled=True)  4.57 us
  transfers between devices with their start and end apart: 6, of which 4 were waited for; matrix products, arithmetic and copies ran while one was open for 0% of the time, Pallas kernels for 27%

profile of v6, /device:TPU:1, one launch (start us, length us, event | category | flops | bytes accessed | tf_op | source)
XLA Modules:
  0.0 140.9 jit_solution(10498965880849203353)
XLA Ops:
  0.0 0.8 copy.7.exps
  0.8 0.0 copy-start.3
  0.8 0.0 copy-start.2
  0.8 6.1 %samples.1 = (bf16[2,64,4096]{2,1,0:T(8,128)(2,1)S(1)}, bf16[2,64,4096]{2,1,0:T(8,128)(2,1)S(1)}, bf16[2,64,4096]{2,1,0:T(8,128)(2,1)S(1)}, bf16[2,64,4096]{2,1,...) custom-call(s32[64,4]{1,0:T(8,128)S(1)} %copy.7.exps, s32[2,64,16384]{2,1,0:T(8,128)} %voltages.1), custom_call_target="tpu_custom_call" | custom-call | flops 10000000 | bytes 13631488 | tf_op jit(solution)/shard_map/samples/pallas_call | solution.py:118
  6.8 4.6 %collective-permute-start = (bf16[2,64,4096]{2,1,0:T(8,128)(2,1)}, bf16[2,64,4096]{2,1,0:T(8,128)(2,1)}, u32[]{:S(2)}, u32[]{:S(2)}) collective-permute-start(bf16[2,64,4096]{2,1,0:T(8,128)(2,1)} %get-tuple-element.18.refs_3_), channel_id=1, source_target_pairs={{0,1},{1,2},{2,3},{3,4},{4,5},{5,6},{6,7},{8,9},{9,10},{10,11},{11... | collective-permute-start | bytes 3145736 | tf_op jit(solution)/shard_map/ppermute | solution.py:371
  11.4 0.0 collective-permute-start.1
  11.5 3.6 %collective-permute-start.2 = (bf16[2,32,4096]{2,1,0:T(8,128)(2,1)}, bf16[2,32,4096]{2,1,0:T(8,128)(2,1)}, u32[]{:S(2)}, u32[]{:S(2)}) collective-permute-start(bf16[2,32,4096]{2,1,0:T(8,128)(2,1)} %get-tuple-element.19), channel_id=1, source_target_pairs={{0,1},{1,2},{2,3},{3,4},{4,5},{5,6},{6,7},{8,9},{9,10},{10,11},{11... | collective-permute-start | bytes 1572872 | tf_op jit(solution)/shard_map/ppermute | solution.py:373
  15.1 0.0 collective-permute-start.3
  15.1 0.0 copy-done.3
  15.1 0.2 convert_reduce_fusion
  15.3 0.1 select_reduce_fusion
  15.5 0.0 copy-done.2
  15.5 0.0 copy-start
  15.5 1.0 copy-done
  16.5 5.8 %channels.3.refs_6_ = bf16[128,2,24,128]{3,2,1,0:T(8,128)(2,1)S(1)} custom-call(s32[257]{0:T(512)S(1)} %pad_add_fusion.first_ref, bf16[2,64,4096]{2,1,0:T(8,128)(2,1)S(1)} %get-tuple-element.15.refs_0_, bf16[2,64,4096]{2,1,0:T(8,128)(2,1)S(1)} %get-tuple-element.16.refs_1_, bf16[2,64,4096]{2,1,0:T(8,128)(2,1)S(1)} %get-tuple-element.17.refs_2_, ...), custom_call_target="tpu_custom_call" | custom-call | flops 1000000000 | bytes 8388608 | tf_op jit(solution)/shard_map/channels/pallas_call | solution.py:222
  22.3 1.1 collective-permute-done.refs_3_.refs_4_
  23.5 7.6 %channels.4 = bf16[128,2,48,128]{3,2,1,0:T(8,128)(2,1)} custom-call(s32[257]{0:T(512)S(1)} %pad_add_fusion.first_ref, bf16[2,64,4096]{2,1,0:T(8,128)(2,1)S(1)} %get-tuple-element.15.refs_0_, bf16[2,64,4096]{2,1,0:T(8,128)(2,1)S(1)} %get-tuple-element.16.refs_1_, bf16[2,64,4096]{2,1,0:T(8,128)(2,1)S(1)} %get-tuple-element.17.refs_2_, ...), custom_call_target="tpu_custom_call" | custom-call | flops 1000000000 | bytes 8388608 | tf_op jit(solution)/shard_map/channels/pallas_call | solution.py:222
  31.1 0.0 collective-permute-done.2.refs_5_
  31.1 0.3 collective-permute-done.3.refs_7_
  31.4 0.0 collective-permute-done.1.refs_6_
  31.4 11.4 %all-to-all-start.1 = ((bf16[128,2,48,128]{3,2,1,0:T(8,128)(2,1)}), bf16[128,2,48,128]{3,2,1,0:T(8,128)(2,1)}, u32[]{:S(2)}, u32[]{:S(2)}) async-start(bf16[128,2,48,128]{3,2,1,0:T(8,128)(2,1)} %channels.4), calls=%async_computation.1 | async-start | bytes 6291456 | tf_op jit(solution)/shard_map/all_to_all | solution.py:393
  42.8 0.0 copy-start.1
  42.8 1.0 copy-done.1
  43.9 11.9 %channels.5 = bf16[128,2,48,128]{3,2,1,0:T(8,128)(2,1)} custom-call(s32[257]{0:T(512)S(1)} %pad_add_fusion.first_ref, bf16[2,64,4096]{2,1,0:T(8,128)(2,1)S(1)} %get-tuple-element.15.refs_0_, bf16[2,64,4096]{2,1,0:T(8,128)(2,1)S(1)} %get-tuple-element.16.refs_1_, bf16[2,64,4096]{2,1,0:T(8,128)(2,1)S(1)} %get-tuple-element.17.refs_2_, ...), custom_call_target="tpu_custom_call" | custom-call | flops 2000000000 | bytes 8388608 | tf_op jit(solution)/shard_map/channels/pallas_call | solution.py:222
  55.8 28.5 %all-to-all-done.1.piece = bf16[128,2,48,128]{3,2,1,0:T(8,128)(2,1)} async-done(((bf16[128,2,48,128]{3,2,1,0:T(8,128)(2,1)}), bf16[128,2,48,128]{3,2,1,0:T(8,128)(2,1)}, u32[]{:S(2)}, u32[]{:S(2)}) %all-to-all-start.1) | async-done | bytes 3145760 | tf_op jit(solution)/shard_map/all_to_all | solution.py:393
  84.2 4.6 %all-to-all-start = ((bf16[128,2,48,128]{3,2,1,0:T(8,128)(2,1)}), bf16[128,2,48,128]{3,2,1,0:T(8,128)(2,1)S(1)}, u32[]{:S(2)}, u32[]{:S(2)}) async-start(bf16[128,2,48,128]{3,2,1,0:T(8,128)(2,1)} %channels.5), calls=%async_computation | async-start | bytes 6291456 | tf_op jit(solution)/shard_map/all_to_all | solution.py:397
  88.8 0.1 fusion
  88.9 0.1 dynamic_slice.3.valid_ref
  89.0 12.2 %correlate.2.refs_0_ = bf16[2,1024,1024]{2,1,0:T(8,128)(2,1)} custom-call(s32[2]{0:T(128)S(1)} %dynamic_slice.3.valid_ref, bf16[128,2,48,128]{3,2,1,0:T(8,128)(2,1)} %all-to-all-done.1.piece), custom_call_target="tpu_custom_call" | custom-call | flops 5000000000 | bytes 19922944 | tf_op jit(solution)/shard_map/correlate/pallas_call | solution.py:341
  101.2 29.4 %all-to-all-done.piece = bf16[128,2,48,128]{3,2,1,0:T(8,128)(2,1)S(1)} async-done(((bf16[128,2,48,128]{3,2,1,0:T(8,128)(2,1)}), bf16[128,2,48,128]{3,2,1,0:T(8,128)(2,1)S(1)}, u32[]{:S(2)}, u32[]{:S(2)}) %all-to-all-start) | async-done | bytes 3145760 | tf_op jit(solution)/shard_map/all_to_all | solution.py:397
  130.6 10.1 %correlate.3 = f32[2,1024,1024]{2,1,0:T(8,128)} custom-call(s32[2]{0:T(128)S(1)} %dynamic_slice.3.valid_ref, bf16[128,2,48,128]{3,2,1,0:T(8,128)(2,1)S(1)} %all-to-all-done.piece, bf16[2,1024,1024]{2,1,0:T(8,128)(2,1)} %correlate.2.refs_0_), custom_call_target="tpu_custom_call" | custom-call | flops 5000000000 | bytes 19922944 | tf_op jit(solution)/shard_map/correlate/pallas_call | solution.py:341
  (4 shorter events, 0.0 us)
Async XLA Ops:
  0.8 14.4 %copy-start.3 = (s32[144]{0:T(256)S(1)}, s32[144]{0:T(256)}, u32[]{:S(2)}) copy-start(s32[144]{0:T(256)} %param.7) | copy-start | bytes 1732
  0.8 14.7 %copy-start.2 = (f32[8,4096]{1,0:T(8,128)S(1)}, f32[8,4096]{1,0:T(8,128)}, u32[]{:S(2)}) copy-start(f32[8,4096]{1,0:T(8,128)} %constant.46.clone.refs_4_.refs_8_) | copy-start | bytes 393220
  6.8 16.6 %collective-permute-start = (bf16[2,64,4096]{2,1,0:T(8,128)(2,1)}, bf16[2,64,4096]{2,1,0:T(8,128)(2,1)}, u32[]{:S(2)}, u32[]{:S(2)}) collective-permute-start(bf16[2,64,4096]{2,1,0:T(8,128)(2,1)} %get-tuple-element.18.refs_3_), channel_id=1, source_target_pairs={{0,1},{1,2},{2,3},{3,4},{4,5},{5,6},{6,7},{8,9},{9,10},{10,11},{11... | collective-permute-start | bytes 3145736 | tf_op jit(solution)/shard_map/ppermute | solution.py:371
  11.4 20.0 %collective-permute-start.1 = (bf16[2,64,4096]{2,1,0:T(8,128)(2,1)S(1)}, bf16[2,64,4096]{2,1,0:T(8,128)(2,1)}, u32[]{:S(2)}, u32[]{:S(2)}) collective-permute-start(bf16[2,64,4096]{2,1,0:T(8,128)(2,1)S(1)} %get-tuple-element.15.refs_0_), channel_id=1, source_target_pairs={{0,7},{1,0},{2,1},{3,2},{4,3},{5,4},{6,5},{7,6},{8,15},{9,8},{10,9... | collective-permute-start | bytes 3145736 | tf_op jit(solution)/shard_map/ppermute | solution.py:372
  11.5 19.6 %collective-permute-start.2 = (bf16[2,32,4096]{2,1,0:T(8,128)(2,1)}, bf16[2,32,4096]{2,1,0:T(8,128)(2,1)}, u32[]{:S(2)}, u32[]{:S(2)}) collective-permute-start(bf16[2,32,4096]{2,1,0:T(8,128)(2,1)} %get-tuple-element.19), channel_id=1, source_target_pairs={{0,1},{1,2},{2,3},{3,4},{4,5},{5,6},{6,7},{8,9},{9,10},{10,11},{11... | collective-permute-start | bytes 1572872 | tf_op jit(solution)/shard_map/ppermute | solution.py:373
  15.1 16.3 %collective-permute-start.3 = (bf16[2,32,4096]{2,1,0:T(8,128)(2,1)}, bf16[2,32,4096]{2,1,0:T(8,128)(2,1)}, u32[]{:S(2)}, u32[]{:S(2)}) collective-permute-start(bf16[2,32,4096]{2,1,0:T(8,128)(2,1)} %get-tuple-element.20), channel_id=1, source_target_pairs={{0,7},{1,0},{2,1},{3,2},{4,3},{5,4},{6,5},{7,6},{8,15},{9,8},{10,9... | collective-permute-start | bytes 1572872 | tf_op jit(solution)/shard_map/ppermute | solution.py:374
  15.5 1.0 copy-start
  31.4 52.8 %all-to-all-start.1 = ((bf16[128,2,48,128]{3,2,1,0:T(8,128)(2,1)}), bf16[128,2,48,128]{3,2,1,0:T(8,128)(2,1)}, u32[]{:S(2)}, u32[]{:S(2)}) async-start(bf16[128,2,48,128]{3,2,1,0:T(8,128)(2,1)} %channels.4), calls=%async_computation.1 | async-start | bytes 6291456 | tf_op jit(solution)/shard_map/all_to_all | solution.py:393
  42.8 1.0 copy-start.1
  84.2 46.4 %all-to-all-start = ((bf16[128,2,48,128]{3,2,1,0:T(8,128)(2,1)}), bf16[128,2,48,128]{3,2,1,0:T(8,128)(2,1)S(1)}, u32[]{:S(2)}, u32[]{:S(2)}) async-start(bf16[128,2,48,128]{3,2,1,0:T(8,128)(2,1)} %channels.5), calls=%async_computation | async-start | bytes 6291456 | tf_op jit(solution)/shard_map/all_to_all | solution.py:397

commit v7 on v6

--- a/solution.py
+++ b/solution.py
@@ -86,43 +86,46 @@
     return out
 
 
-def sample_kernel(exps, voltages, *outs):
-    wholes, low2, high1 = outs[:-2], outs[-2], outs[-1]
+def sample_kernel(first, count, exps, voltages, *outs):
+    wholes, halves = outs[:count], outs[count:]
     step, block = pl.program_id(0), voltages.shape[1]
-    half = low2.shape[1]
     rows = pl.ds(pl.multiple_of(step * block, block), block)
     factor = jnp.left_shift(1, exps[rows, :]).astype(jnp.float32) * (1.0 / 128.0)
-    for s, whole in enumerate(wholes):
+    for k, whole in enumerate(wholes):
+        s = first + k
         for c in range(2):
-            value = voltages[c, :, s * F : (s + 1) * F].astype(jnp.float32) * factor[:, s : s + 1]
+            value = voltages[c, :, k * F : (k + 1) * F].astype(jnp.float32) * factor[:, s : s + 1]
             value = value.astype(jnp.bfloat16)
             whole[c, rows, :] = value
-            if s == 2:
-
-                @pl.when(step * block < half)
+            if halves and s == 2:
+
+                @pl.when(step * block < halves[0].shape[1])
                 def _():
-                    low2[c, rows, :] = value
-
-            if s == 1:
+                    halves[0][c, rows, :] = value
+
+            if halves and s == 1:
+                half = halves[1].shape[1]
 
                 @pl.when(step * block >= half)
                 def _():
-                    high1[c, pl.ds(pl.multiple_of(step * block - half, block), block), :] = value
-
-
-def sample_call(voltages, exps):
-    inputs, spectra = exps.shape
+                    halves[1][c, pl.ds(pl.multiple_of(step * block - half, block), block), :] = value
+
+
+def sample_call(voltages, exps, first, count, halves):
+    inputs = exps.shape[0]
     block = 16
     held = pl.BlockSpec(memory_space=pltpu.VMEM)
-    shapes = [(2, inputs, F)] * spectra + [(2, inputs // 2, F)] * 2
+    shapes = [(2, inputs, F)] * count + [(2, inputs // 2, F)] * (2 if halves else 0)
     return pl.pallas_call(
-        sample_kernel,
+        functools.partial(sample_kernel, first, count),
         out_shape=[jax.ShapeDtypeStruct(shape, jnp.bfloat16) for shape in shapes],
         grid=(inputs // block,),
-        in_specs=[held, pl.BlockSpec((2, block, spectra * F), lambda i: (0, i, 0))],
+        in_specs=[held, pl.BlockSpec((2, block, count * F), lambda i: (0, i, first // count))],
         out_specs=[held] * len(shapes),
         compiler_params=pltpu.CompilerParams(vmem_limit_bytes=SAMPLE_VMEM),
-        cost_estimate=pl.CostEstimate(flops=10**7, bytes_accessed=13 * 2**20, transcendentals=0),
+        cost_estimate=pl.CostEstimate(
+            flops=10**7, bytes_accessed=(3 * count + len(shapes) - count) * 2**20, transcendentals=0
+        ),
         name="samples",
     )(exps, voltages)
 
@@ -364,7 +367,10 @@
     n_tim = lax.axis_size("tim")
     devices = n_inp * n_tim
     spec_dev = voltages.shape[2] // F
-    *own, low2, high1 = sample_call(voltages, scale_exps)
+    (last_own,) = sample_call(voltages, scale_exps, spec_dev - 1, 1, False)
+    last_own, held_back = lax.optimization_barrier((last_own, voltages))
+    *own, low2, high1 = sample_call(held_back, scale_exps, 0, spec_dev - 1, True)
+    own.append(last_own)
     ahead = [(source, source + 1) for source in range(n_tim - 1)]
     back = [(source, (source - 1) % n_tim) for source in range(n_tim)]
     half = voltages.shape[1] // 2

time: 141 us -> 143 us (1.014)
  local copies, waits for them, and re-layouts: 2.93 us -> 6.35 us
    unnamed x9 -> x15, local copies, waits for them, and re-layouts: 2.85 us -> 6.27 us
    pallas_call x3, Pallas kernels: 25.3 us -> 23.8 us  [channel_call(): pl.pallas_call(functools.partial(channel_kernel, plan, len(xs)), out_shap...]
    pallas_call x1 -> x2, Pallas kernels: 6.06 us -> 7.54 us  [sample_call(): pl.pallas_call(functools.partial(sample_kernel, first, count), out_shape=...]
  transfers between devices with their start and end apart: 6 -> 6, of which waited for: 4 -> 3; matrix products, arithmetic and copies ran while one was open for 0% -> 0% of each run, Pallas kernels for 27% -> 29%
where the time goes in v7:
time: 143 us; the launch traced here: 142 us
  waiting for transfers between devices  58.4 us (41%)
  Pallas kernels  53.6 us (37%)
  starting transfers between devices  23.2 us (16%)
  local copies, waits for them, and re-layouts  6.35 us (4%)
    all_to_all x1, waiting for transfers between devices, body(): lax.all_to_all(far, ('inp', 'tim'), split_axis=0, concat_axis=0, tiled=True)  29.4 us
    all_to_all x1, waiting for transfers between devices, body(): lax.all_to_all(near, ('inp', 'tim'), split_axis=0, concat_axis=0, tiled=T...  27.5 us
    pallas_call x3, Pallas kernels, channel_call(): pl.pallas_call(functools.partial(channel_kernel, plan, len(xs)), out_shap...  23.8 us
    pallas_call x2, Pallas kernels, correlate_call(): pl.pallas_call(functools.partial(correlate_kernel, n_tim, mixed, scale),...  22.3 us
    all_to_all x1, starting transfers between devices, body(): lax.all_to_all(near, ('inp', 'tim'), split_axis=0, concat_axis=0, tiled=T...  10.2 us
    pallas_call x2, Pallas kernels, sample_call(): pl.pallas_call(functools.partial(sample_kernel, first, count), out_shape=...  7.54 us
    unnamed x15, local copies, waits for them, and re-layouts  6.27 us
    ppermute x1, starting transfers between devices, body(): minus1 = lax.ppermute(own[3], 'tim', ahead)  4.73 us
  transfers between devices with their start and end apart: 6, of which 3 were waited for; matrix products, arithmetic and copies ran while one was open for 0% of the time, Pallas kernels for 29%

profile of v7, /device:TPU:1, one launch (start us, length us, event | category | flops | bytes accessed | tf_op | source)
XLA Modules:
  0.0 142.3 jit_solution(9978455509473711089)
XLA Ops:
  0.0 0.8 copy.9.exps
  0.8 2.6 %samples.2.refs_3_ = bf16[2,64,4096]{2,1,0:T(8,128)(2,1)S(1)} custom-call(s32[64,4]{1,0:T(8,128)S(1)} %copy.9.exps, s32[2,64,16384]{2,1,0:T(8,128)} %voltages.2), custom_call_target="tpu_custom_call" | custom-call | flops 10000000 | bytes 3145728 | tf_op jit(solution)/shard_map/samples/pallas_call | solution.py:119
  3.3 0.0 copy-start.6
  3.3 0.0 copy-start.5
  3.4 4.7 %collective-permute-start = (bf16[2,64,4096]{2,1,0:T(8,128)(2,1)S(1)}, bf16[2,64,4096]{2,1,0:T(8,128)(2,1)}, u32[]{:S(2)}, u32[]{:S(2)}) collective-permute-start(bf16[2,64,4096]{2,1,0:T(8,128)(2,1)S(1)} %samples.2.refs_3_), channel_id=1, source_target_pairs={{0,1},{1,2},{2,3},{3,4},{4,5},{5,6},{6,7},{8,9},{9,10},{10,11},{11... | collective-permute-start | bytes 3145736 | tf_op jit(solution)/shard_map/ppermute | solution.py:377
  8.1 5.0 %samples.3 = (bf16[2,64,4096]{2,1,0:T(8,128)(2,1)S(1)}, bf16[2,64,4096]{2,1,0:T(8,128)(2,1)S(1)}, bf16[2,64,4096]{2,1,0:T(8,128)(2,1)S(1)}, bf16[2,32,4096]{2,1,0:T(8,128)(2,1)}, bf16[2,32,4096]{2,1,0:T(8,128)(2,1)}) custom-call(s32[64,4]{1,0:T(8,128)S(1)} %copy.9.exps, s32[2,64,16384]{2,1,0:T(8,128)} %voltages.2), custom_call_target="tpu_custom_call" | custom-call | flops 10000000 | bytes 11534336 | tf_op jit(solution)/shard_map/samples/pallas_call | solution.py:119
  13.1 0.0 copy-start
  13.1 1.0 copy-done
  14.1 0.0 collective-permute-start.1
  14.1 3.6 %collective-permute-start.2 = (bf16[2,32,4096]{2,1,0:T(8,128)(2,1)}, bf16[2,32,4096]{2,1,0:T(8,128)(2,1)}, u32[]{:S(2)}, u32[]{:S(2)}) collective-permute-start(bf16[2,32,4096]{2,1,0:T(8,128)(2,1)} %get-tuple-element.21), channel_id=1, source_target_pairs={{0,1},{1,2},{2,3},{3,4},{4,5},{5,6},{6,7},{8,9},{9,10},{10,11},{11... | collective-permute-start | bytes 1572872 | tf_op jit(solution)/shard_map/ppermute | solution.py:379
  17.7 0.0 collective-permute-start.3
  17.7 0.0 copy-done.6
  17.7 0.2 convert_reduce_fusion
  17.9 0.1 select_reduce_fusion
  18.1 0.0 copy-done.5
  18.1 0.0 copy-start.1
  18.1 1.2 copy-done.1
  19.3 0.0 copy-start.3
  19.3 1.0 copy-done.3
  20.4 4.6 %channels.3.refs_6_ = bf16[128,2,24,128]{3,2,1,0:T(8,128)(2,1)S(1)} custom-call(s32[257]{0:T(512)S(1)} %pad_add_fusion.first_ref, bf16[2,64,4096]{2,1,0:T(8,128)(2,1)S(1)} %get-tuple-element.17.refs_0_, bf16[2,64,4096]{2,1,0:T(8,128)(2,1)S(1)} %get-tuple-element.18.refs_1_, bf16[2,64,4096]{2,1,0:T(8,128)(2,1)S(1)} %copy-done.1, ...), custom_call_target="tpu_custom_call" | custom-call | flops 1000000000 | bytes 8388608 | tf_op jit(solution)/shard_map/channels/pallas_call | solution.py:225
  24.9 0.0 collective-permute-done.refs_3_.refs_4_
  25.0 7.6 %channels.4 = bf16[128,2,48,128]{3,2,1,0:T(8,128)(2,1)} custom-call(s32[257]{0:T(512)S(1)} %pad_add_fusion.first_ref, bf16[2,64,4096]{2,1,0:T(8,128)(2,1)S(1)} %get-tuple-element.17.refs_0_, bf16[2,64,4096]{2,1,0:T(8,128)(2,1)S(1)} %get-tuple-element.18.refs_1_, bf16[2,64,4096]{2,1,0:T(8,128)(2,1)S(1)} %copy-done.1, ...), custom_call_target="tpu_custom_call" | custom-call | flops 1000000000 | bytes 8388608 | tf_op jit(solution)/shard_map/channels/pallas_call | solution.py:225
  32.6 0.0 collective-permute-done.2.refs_5_
  32.6 1.4 collective-permute-done.3.refs_7_
  34.0 0.0 collective-permute-done.1.refs_6_
  34.0 10.2 %all-to-all-start.1 = ((bf16[128,2,48,128]{3,2,1,0:T(8,128)(2,1)}), bf16[128,2,48,128]{3,2,1,0:T(8,128)(2,1)}, u32[]{:S(2)}, u32[]{:S(2)}) async-start(bf16[128,2,48,128]{3,2,1,0:T(8,128)(2,1)} %channels.4), calls=%async_computation.1 | async-start | bytes 6291456 | tf_op jit(solution)/shard_map/all_to_all | solution.py:399
  44.2 0.0 copy-start.2
  44.2 1.2 copy-done.2
  45.5 0.0 copy-start.4
  45.5 1.0 copy-done.4
  46.5 11.6 %channels.5 = bf16[128,2,48,128]{3,2,1,0:T(8,128)(2,1)} custom-call(s32[257]{0:T(512)S(1)} %pad_add_fusion.first_ref, bf16[2,64,4096]{2,1,0:T(8,128)(2,1)S(1)} %get-tuple-element.17.refs_0_, bf16[2,64,4096]{2,1,0:T(8,128)(2,1)S(1)} %get-tuple-element.18.refs_1_, bf16[2,64,4096]{2,1,0:T(8,128)(2,1)S(1)} %copy-done.2, ...), custom_call_target="tpu_custom_call" | custom-call | flops 2000000000 | bytes 8388608 | tf_op jit(solution)/shard_map/channels/pallas_call | solution.py:225
  58.1 27.5 %all-to-all-done.1.piece = bf16[128,2,48,128]{3,2,1,0:T(8,128)(2,1)} async-done(((bf16[128,2,48,128]{3,2,1,0:T(8,128)(2,1)}), bf16[128,2,48,128]{3,2,1,0:T(8,128)(2,1)}, u32[]{:S(2)}, u32[]{:S(2)}) %all-to-all-start.1) | async-done | bytes 3145760 | tf_op jit(solution)/shard_map/all_to_all | solution.py:399
  85.6 4.6 %all-to-all-start = ((bf16[128,2,48,128]{3,2,1,0:T(8,128)(2,1)}), bf16[128,2,48,128]{3,2,1,0:T(8,128)(2,1)S(1)}, u32[]{:S(2)}, u32[]{:S(2)}) async-start(bf16[128,2,48,128]{3,2,1,0:T(8,128)(2,1)} %channels.5), calls=%async_computation | async-start | bytes 6291456 | tf_op jit(solution)/shard_map/all_to_all | solution.py:403
  90.2 0.1 fusion
  90.3 0.1 dynamic_slice.3.valid_ref
  90.4 12.2 %correlate.2.refs_0_ = bf16[2,1024,1024]{2,1,0:T(8,128)(2,1)} custom-call(s32[2]{0:T(128)S(1)} %dynamic_slice.3.valid_ref, bf16[128,2,48,128]{3,2,1,0:T(8,128)(2,1)} %all-to-all-done.1.piece), custom_call_target="tpu_custom_call" | custom-call | flops 5000000000 | bytes 19922944 | tf_op jit(solution)/shard_map/correlate/pallas_call | solution.py:344
  102.6 29.4 %all-to-all-done.piece = bf16[128,2,48,128]{3,2,1,0:T(8,128)(2,1)S(1)} async-done(((bf16[128,2,48,128]{3,2,1,0:T(8,128)(2,1)}), bf16[128,2,48,128]{3,2,1,0:T(8,128)(2,1)S(1)}, u32[]{:S(2)}, u32[]{:S(2)}) %all-to-all-start) | async-done | bytes 3145760 | tf_op jit(solution)/shard_map/all_to_all | solution.py:403
  132.0 10.1 %correlate.3 = f32[2,1024,1024]{2,1,0:T(8,128)} custom-call(s32[2]{0:T(128)S(1)} %dynamic_slice.3.valid_ref, bf16[128,2,48,128]{3,2,1,0:T(8,128)(2,1)S(1)} %all-to-all-done.piece, bf16[2,1024,1024]{2,1,0:T(8,128)(2,1)} %correlate.2.refs_0_), custom_call_target="tpu_custom_call" | custom-call | flops 5000000000 | bytes 19922944 | tf_op jit(solution)/shard_map/correlate/pallas_call | solution.py:344
  (4 shorter events, 0.0 us)
Async XLA Ops:
  3.3 14.4 %copy-start.6 = (s32[144]{0:T(256)S(1)}, s32[144]{0:T(256)}, u32[]{:S(2)}) copy-start(s32[144]{0:T(256)} %param.7) | copy-start | bytes 1732
  3.3 14.7 %copy-start.5 = (f32[8,4096]{1,0:T(8,128)S(1)}, f32[8,4096]{1,0:T(8,128)}, u32[]{:S(2)}) copy-start(f32[8,4096]{1,0:T(8,128)} %constant.46.clone.refs_4_.refs_8_) | copy-start | bytes 393220
  3.4 21.6 %collective-permute-start = (bf16[2,64,4096]{2,1,0:T(8,128)(2,1)S(1)}, bf16[2,64,4096]{2,1,0:T(8,128)(2,1)}, u32[]{:S(2)}, u32[]{:S(2)}) collective-permute-start(bf16[2,64,4096]{2,1,0:T(8,128)(2,1)S(1)} %samples.2.refs_3_), channel_id=1, source_target_pairs={{0,1},{1,2},{2,3},{3,4},{4,5},{5,6},{6,7},{8,9},{9,10},{10,11},{11... | collective-permute-start | bytes 3145736 | tf_op jit(solution)/shard_map/ppermute | solution.py:377
  13.1 1.0 copy-start
  14.1 19.9 %collective-permute-start.1 = (bf16[2,64,4096]{2,1,0:T(8,128)(2,1)S(1)}, bf16[2,64,4096]{2,1,0:T(8,128)(2,1)}, u32[]{:S(2)}, u32[]{:S(2)}) collective-permute-start(bf16[2,64,4096]{2,1,0:T(8,128)(2,1)S(1)} %get-tuple-element.17.refs_0_), channel_id=1, source_target_pairs={{0,7},{1,0},{2,1},{3,2},{4,3},{5,4},{6,5},{7,6},{8,15},{9,8},{10,9... | collective-permute-start | bytes 3145736 | tf_op jit(solution)/shard_map/ppermute | solution.py:378
  14.1 18.5 %collective-permute-start.2 = (bf16[2,32,4096]{2,1,0:T(8,128)(2,1)}, bf16[2,32,4096]{2,1,0:T(8,128)(2,1)}, u32[]{:S(2)}, u32[]{:S(2)}) collective-permute-start(bf16[2,32,4096]{2,1,0:T(8,128)(2,1)} %get-tuple-element.21), channel_id=1, source_target_pairs={{0,1},{1,2},{2,3},{3,4},{4,5},{5,6},{6,7},{8,9},{9,10},{10,11},{11... | collective-permute-start | bytes 1572872 | tf_op jit(solution)/shard_map/ppermute | solution.py:379
  17.7 16.3 %collective-permute-start.3 = (bf16[2,32,4096]{2,1,0:T(8,128)(2,1)}, bf16[2,32,4096]{2,1,0:T(8,128)(2,1)}, u32[]{:S(2)}, u32[]{:S(2)}) collective-permute-start(bf16[2,32,4096]{2,1,0:T(8,128)(2,1)} %get-tuple-element.22), channel_id=1, source_target_pairs={{0,7},{1,0},{2,1},{3,2},{4,3},{5,4},{6,5},{7,6},{8,15},{9,8},{10,9... | collective-permute-start | bytes 1572872 | tf_op jit(solution)/shard_map/ppermute | solution.py:380
  18.1 1.2 copy-start.1
  19.3 1.0 copy-start.3
  34.0 51.6 %all-to-all-start.1 = ((bf16[128,2,48,128]{3,2,1,0:T(8,128)(2,1)}), bf16[128,2,48,128]{3,2,1,0:T(8,128)(2,1)}, u32[]{:S(2)}, u32[]{:S(2)}) async-start(bf16[128,2,48,128]{3,2,1,0:T(8,128)(2,1)} %channels.4), calls=%async_computation.1 | async-start | bytes 6291456 | tf_op jit(solution)/shard_map/all_to_all | solution.py:399
  44.2 1.2 copy-start.2
  45.5 1.0 copy-start.4
  85.6 46.4 %all-to-all-start = ((bf16[128,2,48,128]{3,2,1,0:T(8,128)(2,1)}), bf16[128,2,48,128]{3,2,1,0:T(8,128)(2,1)S(1)}, u32[]{:S(2)}, u32[]{:S(2)}) async-start(bf16[128,2,48,128]{3,2,1,0:T(8,128)(2,1)} %channels.5), calls=%async_computation | async-start | bytes 6291456 | tf_op jit(solution)/shard_map/all_to_all | solution.py:403

commit v8 on v6

--- a/solution.py
+++ b/solution.py
@@ -92,11 +92,14 @@
     half = low2.shape[1]
     rows = pl.ds(pl.multiple_of(step * block, block), block)
     factor = jnp.left_shift(1, exps[rows, :]).astype(jnp.float32) * (1.0 / 128.0)
-    for s, whole in enumerate(wholes):
+    each = voltages.shape[2] // F
+
+    def make(s):
+        k = s % each
         for c in range(2):
-            value = voltages[c, :, s * F : (s + 1) * F].astype(jnp.float32) * factor[:, s : s + 1]
+            value = voltages[c, :, k * F : (k + 1) * F].astype(jnp.float32) * factor[:, s : s + 1]
             value = value.astype(jnp.bfloat16)
-            whole[c, rows, :] = value
+            wholes[s][c, rows, :] = value
             if s == 2:
 
                 @pl.when(step * block < half)
@@ -108,6 +111,13 @@
                 @pl.when(step * block >= half)
                 def _():
                     high1[c, pl.ds(pl.multiple_of(step * block - half, block), block), :] = value
+
+    for part in range(len(wholes) // each):
+
+        @pl.when(pl.program_id(1) == part)
+        def _():
+            for k in range(each):
+                make(part * each + k)
 
 
 def sample_call(voltages, exps):
@@ -118,8 +128,8 @@
     return pl.pallas_call(
         sample_kernel,
         out_shape=[jax.ShapeDtypeStruct(shape, jnp.bfloat16) for shape in shapes],
-        grid=(inputs // block,),
-        in_specs=[held, pl.BlockSpec((2, block, spectra * F), lambda i: (0, i, 0))],
+        grid=(inputs // block, spectra),
+        in_specs=[held, pl.BlockSpec((2, block, F), lambda i, h: (0, i, h))],
         out_specs=[held] * len(shapes),
         compiler_params=pltpu.CompilerParams(vmem_limit_bytes=SAMPLE_VMEM),
         cost_estimate=pl.CostEstimate(flops=10**7, bytes_accessed=13 * 2**20, transcendentals=0),

time: 141 us -> 147 us (1.043)
  Pallas kernels: 53.7 us -> 59 us
    pallas_call x1, Pallas kernels: 6.06 us -> 11.4 us  [sample_call(): pl.pallas_call(sample_kernel, out_shape=[jax.ShapeDtypeStruct(shape, jnp....]
  transfers between devices with their start and end apart: 6 -> 6, of which waited for: 4 -> 4; matrix products, arithmetic and copies ran while one was open for 0% -> 0% of each run, Pallas kernels for 27% -> 26%
where the time goes in v8:
time: 147 us; the launch traced here: 146 us
  waiting for transfers between devices  59.3 us (40%)
  Pallas kernels  59 us (40%)
  starting transfers between devices  24.2 us (16%)
  local copies, waits for them, and re-layouts  2.93 us (2%)
    all_to_all x1, waiting for transfers between devices, body(): lax.all_to_all(far, ('inp', 'tim'), split_axis=0, concat_axis=0, tiled=True)  29.4 us
    all_to_all x1, waiting for transfers between devices, body(): lax.all_to_all(near, ('inp', 'tim'), split_axis=0, concat_axis=0, tiled=T...  28.5 us
    pallas_call x3, Pallas kernels, channel_call(): pl.pallas_call(functools.partial(channel_kernel, plan, len(xs)), out_shap...  25.3 us
    pallas_call x2, Pallas kernels, correlate_call(): pl.pallas_call(functools.partial(correlate_kernel, n_tim, mixed, scale),...  22.3 us
    all_to_all x1, starting transfers between devices, body(): lax.all_to_all(near, ('inp', 'tim'), split_axis=0, concat_axis=0, tiled=T...  11.4 us
    pallas_call x1, Pallas kernels, sample_call(): pl.pallas_call(sample_kernel, out_shape=[jax.ShapeDtypeStruct(shape, jnp....  11.4 us
    ppermute x1, starting transfers between devices, body(): minus1 = lax.ppermute(own[3], 'tim', ahead)  4.58 us
    all_to_all x1, starting transfers between devices, body(): lax.all_to_all(far, ('inp', 'tim'), split_axis=0, concat_axis=0, tiled=True)  4.57 us
  transfers between devices with their start and end apart: 6, of which 4 were waited for; matrix products, arithmetic and copies ran while one was open for 0% of the time, Pallas kernels for 26%

profile of v8, /device:TPU:1, one launch (start us, length us, event | category | flops | bytes accessed | tf_op | source)
XLA Modules:
  0.0 146.2 jit_solution(390233453326166728)
XLA Ops:
  0.0 0.8 copy.7.exps
  0.8 0.0 copy-start.3
  0.8 0.0 copy-start.2
  0.8 11.4 %samples.1 = (bf16[2,64,4096]{2,1,0:T(8,128)(2,1)S(1)}, bf16[2,64,4096]{2,1,0:T(8,128)(2,1)S(1)}, bf16[2,64,4096]{2,1,0:T(8,128)(2,1)S(1)}, bf16[2,64,4096]{2,1,...) custom-call(s32[64,4]{1,0:T(8,128)S(1)} %copy.7.exps, s32[2,64,16384]{2,1,0:T(8,128)} %voltages.1), custom_call_target="tpu_custom_call" | custom-call | flops 10000000 | bytes 13631488 | tf_op jit(solution)/shard_map/samples/pallas_call | solution.py:128
  12.2 4.6 %collective-permute-start = (bf16[2,64,4096]{2,1,0:T(8,128)(2,1)}, bf16[2,64,4096]{2,1,0:T(8,128)(2,1)}, u32[]{:S(2)}, u32[]{:S(2)}) collective-permute-start(bf16[2,64,4096]{2,1,0:T(8,128)(2,1)} %get-tuple-element.18.refs_3_), channel_id=1, source_target_pairs={{0,1},{1,2},{2,3},{3,4},{4,5},{5,6},{6,7},{8,9},{9,10},{10,11},{11... | collective-permute-start | bytes 3145736 | tf_op jit(solution)/shard_map/ppermute | solution.py:381
  16.7 0.0 collective-permute-start.1
  16.8 3.6 %collective-permute-start.2 = (bf16[2,32,4096]{2,1,0:T(8,128)(2,1)}, bf16[2,32,4096]{2,1,0:T(8,128)(2,1)}, u32[]{:S(2)}, u32[]{:S(2)}) collective-permute-start(bf16[2,32,4096]{2,1,0:T(8,128)(2,1)} %get-tuple-element.19), channel_id=1, source_target_pairs={{0,1},{1,2},{2,3},{3,4},{4,5},{5,6},{6,7},{8,9},{9,10},{10,11},{11... | collective-permute-start | bytes 1572872 | tf_op jit(solution)/shard_map/ppermute | solution.py:383
  20.4 0.0 collective-permute-start.3
  20.4 0.0 copy-done.3
  20.4 0.2 convert_reduce_fusion
  20.6 0.1 select_reduce_fusion
  20.8 0.0 copy-done.2
  20.8 0.0 copy-start
  20.8 1.0 copy-done
  21.8 5.8 %channels.3.refs_6_ = bf16[128,2,24,128]{3,2,1,0:T(8,128)(2,1)S(1)} custom-call(s32[257]{0:T(512)S(1)} %pad_add_fusion.first_ref, bf16[2,64,4096]{2,1,0:T(8,128)(2,1)S(1)} %get-tuple-element.15.refs_0_, bf16[2,64,4096]{2,1,0:T(8,128)(2,1)S(1)} %get-tuple-element.16.refs_1_, bf16[2,64,4096]{2,1,0:T(8,128)(2,1)S(1)} %get-tuple-element.17.refs_2_, ...), custom_call_target="tpu_custom_call" | custom-call | flops 1000000000 | bytes 8388608 | tf_op jit(solution)/shard_map/channels/pallas_call | solution.py:232
  27.7 1.1 collective-permute-done.refs_3_.refs_4_
  28.8 7.6 %channels.4 = bf16[128,2,48,128]{3,2,1,0:T(8,128)(2,1)} custom-call(s32[257]{0:T(512)S(1)} %pad_add_fusion.first_ref, bf16[2,64,4096]{2,1,0:T(8,128)(2,1)S(1)} %get-tuple-element.15.refs_0_, bf16[2,64,4096]{2,1,0:T(8,128)(2,1)S(1)} %get-tuple-element.16.refs_1_, bf16[2,64,4096]{2,1,0:T(8,128)(2,1)S(1)} %get-tuple-element.17.refs_2_, ...), custom_call_target="tpu_custom_call" | custom-call | flops 1000000000 | bytes 8388608 | tf_op jit(solution)/shard_map/channels/pallas_call | solution.py:232
  36.4 0.0 collective-permute-done.2.refs_5_
  36.4 0.3 collective-permute-done.3.refs_7_
  36.7 0.0 collective-permute-done.1.refs_6_
  36.7 11.4 %all-to-all-start.1 = ((bf16[128,2,48,128]{3,2,1,0:T(8,128)(2,1)}), bf16[128,2,48,128]{3,2,1,0:T(8,128)(2,1)}, u32[]{:S(2)}, u32[]{:S(2)}) async-start(bf16[128,2,48,128]{3,2,1,0:T(8,128)(2,1)} %channels.4), calls=%async_computation.1 | async-start | bytes 6291456 | tf_op jit(solution)/shard_map/all_to_all | solution.py:403
  48.1 0.0 copy-start.1
  48.2 1.0 copy-done.1
  49.2 11.9 %channels.5 = bf16[128,2,48,128]{3,2,1,0:T(8,128)(2,1)} custom-call(s32[257]{0:T(512)S(1)} %pad_add_fusion.first_ref, bf16[2,64,4096]{2,1,0:T(8,128)(2,1)S(1)} %get-tuple-element.15.refs_0_, bf16[2,64,4096]{2,1,0:T(8,128)(2,1)S(1)} %get-tuple-element.16.refs_1_, bf16[2,64,4096]{2,1,0:T(8,128)(2,1)S(1)} %get-tuple-element.17.refs_2_, ...), custom_call_target="tpu_custom_call" | custom-call | flops 2000000000 | bytes 8388608 | tf_op jit(solution)/shard_map/channels/pallas_call | solution.py:232
  61.1 28.5 %all-to-all-done.1.piece = bf16[128,2,48,128]{3,2,1,0:T(8,128)(2,1)} async-done(((bf16[128,2,48,128]{3,2,1,0:T(8,128)(2,1)}), bf16[128,2,48,128]{3,2,1,0:T(8,128)(2,1)}, u32[]{:S(2)}, u32[]{:S(2)}) %all-to-all-start.1) | async-done | bytes 3145760 | tf_op jit(solution)/shard_map/all_to_all | solution.py:403
  89.5 4.6 %all-to-all-start = ((bf16[128,2,48,128]{3,2,1,0:T(8,128)(2,1)}), bf16[128,2,48,128]{3,2,1,0:T(8,128)(2,1)S(1)}, u32[]{:S(2)}, u32[]{:S(2)}) async-start(bf16[128,2,48,128]{3,2,1,0:T(8,128)(2,1)} %channels.5), calls=%async_computation | async-start | bytes 6291456 | tf_op jit(solution)/shard_map/all_to_all | solution.py:407
  94.1 0.1 fusion
  94.2 0.1 dynamic_slice.3.valid_ref
  94.3 12.2 %correlate.2.refs_0_ = bf16[2,1024,1024]{2,1,0:T(8,128)(2,1)} custom-call(s32[2]{0:T(128)S(1)} %dynamic_slice.3.valid_ref, bf16[128,2,48,128]{3,2,1,0:T(8,128)(2,1)} %all-to-all-done.1.piece), custom_call_target="tpu_custom_call" | custom-call | flops 5000000000 | bytes 19922944 | tf_op jit(solution)/shard_map/correlate/pallas_call | solution.py:351
  106.5 29.4 %all-to-all-done.piece = bf16[128,2,48,128]{3,2,1,0:T(8,128)(2,1)S(1)} async-done(((bf16[128,2,48,128]{3,2,1,0:T(8,128)(2,1)}), bf16[128,2,48,128]{3,2,1,0:T(8,128)(2,1)S(1)}, u32[]{:S(2)}, u32[]{:S(2)}) %all-to-all-start) | async-done | bytes 3145760 | tf_op jit(solution)/shard_map/all_to_all | solution.py:407
  135.9 10.1 %correlate.3 = f32[2,1024,1024]{2,1,0:T(8,128)} custom-call(s32[2]{0:T(128)S(1)} %dynamic_slice.3.valid_ref, bf16[128,2,48,128]{3,2,1,0:T(8,128)(2,1)S(1)} %all-to-all-done.piece, bf16[2,1024,1024]{2,1,0:T(8,128)(2,1)} %correlate.2.refs_0_), custom_call_target="tpu_custom_call" | custom-call | flops 5000000000 | bytes 19922944 | tf_op jit(solution)/shard_map/correlate/pallas_call | solution.py:351
  (4 shorter events, 0.0 us)
Async XLA Ops:
  0.8 19.7 %copy-start.3 = (s32[144]{0:T(256)S(1)}, s32[144]{0:T(256)}, u32[]{:S(2)}) copy-start(s32[144]{0:T(256)} %param.7) | copy-start | bytes 1732
  0.8 20.0 %copy-start.2 = (f32[8,4096]{1,0:T(8,128)S(1)}, f32[8,4096]{1,0:T(8,128)}, u32[]{:S(2)}) copy-start(f32[8,4096]{1,0:T(8,128)} %constant.46.clone.refs_4_.refs_8_) | copy-start | bytes 393220
  12.2 16.6 %collective-permute-start = (bf16[2,64,4096]{2,1,0:T(8,128)(2,1)}, bf16[2,64,4096]{2,1,0:T(8,128)(2,1)}, u32[]{:S(2)}, u32[]{:S(2)}) collective-permute-start(bf16[2,64,4096]{2,1,0:T(8,128)(2,1)} %get-tuple-element.18.refs_3_), channel_id=1, source_target_pairs={{0,1},{1,2},{2,3},{3,4},{4,5},{5,6},{6,7},{8,9},{9,10},{10,11},{11... | collective-permute-start | bytes 3145736 | tf_op jit(solution)/shard_map/ppermute | solution.py:381
  16.7 20.0 %collective-permute-start.1 = (bf16[2,64,4096]{2,1,0:T(8,128)(2,1)S(1)}, bf16[2,64,4096]{2,1,0:T(8,128)(2,1)}, u32[]{:S(2)}, u32[]{:S(2)}) collective-permute-start(bf16[2,64,4096]{2,1,0:T(8,128)(2,1)S(1)} %get-tuple-element.15.refs_0_), channel_id=1, source_target_pairs={{0,7},{1,0},{2,1},{3,2},{4,3},{5,4},{6,5},{7,6},{8,15},{9,8},{10,9... | collective-permute-start | bytes 3145736 | tf_op jit(solution)/shard_map/ppermute | solution.py:382
  16.8 19.6 %collective-permute-start.2 = (bf16[2,32,4096]{2,1,0:T(8,128)(2,1)}, bf16[2,32,4096]{2,1,0:T(8,128)(2,1)}, u32[]{:S(2)}, u32[]{:S(2)}) collective-permute-start(bf16[2,32,4096]{2,1,0:T(8,128)(2,1)} %get-tuple-element.19), channel_id=1, source_target_pairs={{0,1},{1,2},{2,3},{3,4},{4,5},{5,6},{6,7},{8,9},{9,10},{10,11},{11... | collective-permute-start | bytes 1572872 | tf_op jit(solution)/shard_map/ppermute | solution.py:383
  20.4 16.3 %collective-permute-start.3 = (bf16[2,32,4096]{2,1,0:T(8,128)(2,1)}, bf16[2,32,4096]{2,1,0:T(8,128)(2,1)}, u32[]{:S(2)}, u32[]{:S(2)}) collective-permute-start(bf16[2,32,4096]{2,1,0:T(8,128)(2,1)} %get-tuple-element.20), channel_id=1, source_target_pairs={{0,7},{1,0},{2,1},{3,2},{4,3},{5,4},{6,5},{7,6},{8,15},{9,8},{10,9... | collective-permute-start | bytes 1572872 | tf_op jit(solution)/shard_map/ppermute | solution.py:384
  20.8 1.0 copy-start
  36.7 52.8 %all-to-all-start.1 = ((bf16[128,2,48,128]{3,2,1,0:T(8,128)(2,1)}), bf16[128,2,48,128]{3,2,1,0:T(8,128)(2,1)}, u32[]{:S(2)}, u32[]{:S(2)}) async-start(bf16[128,2,48,128]{3,2,1,0:T(8,128)(2,1)} %channels.4), calls=%async_computation.1 | async-start | bytes 6291456 | tf_op jit(solution)/shard_map/all_to_all | solution.py:403
  48.1 1.0 copy-start.1
  89.5 46.4 %all-to-all-start = ((bf16[128,2,48,128]{3,2,1,0:T(8,128)(2,1)}), bf16[128,2,48,128]{3,2,1,0:T(8,128)(2,1)S(1)}, u32[]{:S(2)}, u32[]{:S(2)}) async-start(bf16[128,2,48,128]{3,2,1,0:T(8,128)(2,1)} %channels.5), calls=%async_computation | async-start | bytes 6291456 | tf_op jit(solution)/shard_map/all_to_all | solution.py:407

commit v9 on v5

--- a/solution.py
+++ b/solution.py
@@ -167,7 +167,7 @@
                 out[owner, slot] = rows.astype(jnp.bfloat16)
             return carry
 
-        lax.fori_loop(0, out.shape[0], place, 0, unroll=2)
+        lax.fori_loop(0, out.shape[0], place, 0, unroll=8)
 
 
 def channel_call(plan, first, xs, rows_table, table, prior=()):

time: 141 us -> 141 us (level)
  transfers between devices with their start and end apart: 6 -> 6, of which waited for: 2 -> 3; matrix products, arithmetic and copies ran while one was open for 2% -> 2% of each run, Pallas kernels for 24% -> 24%
where the time goes in v9:
time: 141 us; the launch traced here: 140 us
  waiting for transfers between devices  58.5 us (41%)
  Pallas kernels  43.4 us (31%)
  starting transfers between devices  24.1 us (17%)
  local copies, waits for them, and re-layouts  7.15 us (5%)
  other arithmetic  6.89 us (5%)
    all_to_all x1, waiting for transfers between devices, body(): lax.all_to_all(far, ('inp', 'tim'), split_axis=0, concat_axis=0, tiled=True)  29.4 us
    all_to_all x1, waiting for transfers between devices, body(): lax.all_to_all(near, ('inp', 'tim'), split_axis=0, concat_axis=0, tiled=T...  28.8 us
    pallas_call x2, Pallas kernels, correlate_call(): pl.pallas_call(functools.partial(correlate_kernel, n_tim, mixed, scale),...  22.3 us
    pallas_call x3, Pallas kernels, channel_call(): pl.pallas_call(functools.partial(channel_kernel, plan, len(xs)), out_shap...  21.1 us
    all_to_all x1, starting transfers between devices, body(): lax.all_to_all(near, ('inp', 'tim'), split_axis=0, concat_axis=0, tiled=T...  11.1 us
    convert_element_type x1, other arithmetic, body(): (voltages[:, :, s * F:(s + 1) * F].astype(jnp.float32) * scale[None, :, s...  5.78 us
    unnamed x14, local copies, waits for them, and re-layouts  5.38 us
    ppermute x1, starting transfers between devices, body(): minus1 = lax.ppermute(own[3], 'tim', ahead)  4.72 us
  transfers between devices with their start and end apart: 6, of which 3 were waited for; matrix products, arithmetic and copies ran while one was open for 2% of the time, Pallas kernels for 24%

profile of v9, /device:TPU:1, one launch (start us, length us, event | category | flops | bytes accessed | tf_op | source)
XLA Modules:
  0.0 140.4 jit_solution(14529077966576814701)
XLA Ops:
  0.0 0.7 exponential_multiply_fusion
  0.7 5.8 %multiply_convert_fusion = (bf16[2,64,4096]{2,1,0:T(8,128)(2,1)}, bf16[2,64,4096]{2,1,0:T(8,128)(2,1)S(1)}, bf16[2,64,4096]{2,1,0:T(8,128)(2,1)S(1)}, bf16[2,64,4096]{2,1,0:T(8,128)(2,1)S(1)}) fusion(s32[2,64,16384]{2,1,0:T(8,128)} %param.5, f32[64]{0:T(128)S(1)} %get-tuple-element.17, f32[64]{0:T(128)S(1)} %get-tuple-element.19, f32[64]{0:T(128)S(1)} %get-tuple-element.20, ...), kind=kLoop, calls=%fused_computation | loop fusion | flops 6291456 | bytes 12583936 | tf_op jit(solution)/shard_map/convert_element_type | solution.py:327
  6.5 0.0 copy-start.6
  6.5 0.0 copy-start.5
  6.5 4.7 %collective-permute-start = (bf16[2,64,4096]{2,1,0:T(8,128)(2,1)}, bf16[2,64,4096]{2,1,0:T(8,128)(2,1)}, u32[]{:S(2)}, u32[]{:S(2)}) collective-permute-start(bf16[2,64,4096]{2,1,0:T(8,128)(2,1)} %get-tuple-element.13.refs_3_), channel_id=1, source_target_pairs={{0,1},{1,2},{2,3},{3,4},{4,5},{5,6},{6,7},{8,9},{9,10},{10,11},{11... | collective-permute-start | bytes 3145736 | tf_op jit(solution)/shard_map/ppermute | solution.py:335
  11.2 0.0 collective-permute-start.1
  11.2 0.8 slice.40
  12.1 3.6 %collective-permute-start.2 = (bf16[2,32,4096]{2,1,0:T(8,128)(2,1)}, bf16[2,32,4096]{2,1,0:T(8,128)(2,1)}, u32[]{:S(2)}, u32[]{:S(2)}) collective-permute-start(bf16[2,32,4096]{2,1,0:T(8,128)(2,1)} %slice.40), channel_id=1, source_target_pairs={{0,1},{1,2},{2,3},{3,4},{4,5},{5,6},{6,7},{8,9},{9,10},{10,11},{11... | collective-permute-start | bytes 1572872 | tf_op jit(solution)/shard_map/ppermute | solution.py:337
  15.7 0.8 slice.41
  16.5 0.0 collective-permute-start.3
  16.6 0.0 copy-done.6
  16.6 0.2 convert_reduce_fusion
  16.8 0.1 select_reduce_fusion
  16.9 0.0 copy-done.5
  16.9 0.0 copy-start.2
  16.9 1.0 copy-done.2
  18.0 0.0 copy-start.3
  18.0 5.5 %channels.3.refs_6_ = bf16[128,2,24,128]{3,2,1,0:T(8,128)(2,1)S(1)} custom-call(s32[257]{0:T(512)S(1)} %pad_add_fusion.first_ref, bf16[2,64,4096]{2,1,0:T(8,128)(2,1)S(1)} %get-tuple-element.15.refs_0_, bf16[2,64,4096]{2,1,0:T(8,128)(2,1)S(1)} %get-tuple-element.14.refs_1_, bf16[2,64,4096]{2,1,0:T(8,128)(2,1)S(1)} %get-tuple-element.16.refs_2_, ...), custom_call_target="tpu_custom_call" | custom-call | flops 1000000000 | bytes 8388608 | tf_op jit(solution)/shard_map/channels/pallas_call | solution.py:180
  23.5 0.0 collective-permute-done.refs_3_.refs_4_
  23.5 0.0 copy-done.3
  23.5 5.7 %channels.4 = bf16[128,2,48,128]{3,2,1,0:T(8,128)(2,1)S(1)} custom-call(s32[257]{0:T(512)S(1)} %pad_add_fusion.first_ref, bf16[2,64,4096]{2,1,0:T(8,128)(2,1)S(1)} %get-tuple-element.15.refs_0_, bf16[2,64,4096]{2,1,0:T(8,128)(2,1)S(1)} %get-tuple-element.14.refs_1_, bf16[2,64,4096]{2,1,0:T(8,128)(2,1)S(1)} %get-tuple-element.16.refs_2_, ...), custom_call_target="tpu_custom_call" | custom-call | flops 1000000000 | bytes 8388608 | tf_op jit(solution)/shard_map/channels/pallas_call | solution.py:180
  29.2 0.0 copy-start.1
  29.3 1.6 %copy-done.1 = bf16[128,2,48,128]{3,2,1,0:T(8,128)(2,1)} copy-done((bf16[128,2,48,128]{3,2,1,0:T(8,128)(2,1)}, bf16[128,2,48,128]{3,2,1,0:T(8,128)(2,1)S(1)}, u32[]{:S(2)}) %copy-start.1) | copy-done | bytes 3145752
  30.9 0.0 collective-permute-done.2.refs_5_
  30.9 0.3 collective-permute-done.3.refs_7_
  31.2 0.0 collective-permute-done.1.refs_6_
  31.2 11.1 %all-to-all-start.1 = ((bf16[128,2,48,128]{3,2,1,0:T(8,128)(2,1)}), bf16[128,2,48,128]{3,2,1,0:T(8,128)(2,1)}, u32[]{:S(2)}, u32[]{:S(2)}) async-start(bf16[128,2,48,128]{3,2,1,0:T(8,128)(2,1)} %copy-done.1), calls=%async_computation.1 | async-start | bytes 6291456 | tf_op jit(solution)/shard_map/all_to_all | solution.py:357
  42.3 0.0 copy-start.4
  42.3 1.0 copy-done.4
  43.4 9.9 %channels.5 = bf16[128,2,48,128]{3,2,1,0:T(8,128)(2,1)S(1)} custom-call(s32[257]{0:T(512)S(1)} %pad_add_fusion.first_ref, bf16[2,64,4096]{2,1,0:T(8,128)(2,1)S(1)} %get-tuple-element.15.refs_0_, bf16[2,64,4096]{2,1,0:T(8,128)(2,1)S(1)} %get-tuple-element.14.refs_1_, bf16[2,64,4096]{2,1,0:T(8,128)(2,1)S(1)} %get-tuple-element.16.refs_2_, ...), custom_call_target="tpu_custom_call" | custom-call | flops 2000000000 | bytes 8388608 | tf_op jit(solution)/shard_map/channels/pallas_call | solution.py:180
  53.2 0.0 copy-start
  53.2 1.7 %copy-done = bf16[128,2,48,128]{3,2,1,0:T(8,128)(2,1)} copy-done((bf16[128,2,48,128]{3,2,1,0:T(8,128)(2,1)}, bf16[128,2,48,128]{3,2,1,0:T(8,128)(2,1)S(1)}, u32[]{:S(2)}) %copy-start) | copy-done | bytes 3145752
  54.9 28.8 %all-to-all-done.1.piece = bf16[128,2,48,128]{3,2,1,0:T(8,128)(2,1)} async-done(((bf16[128,2,48,128]{3,2,1,0:T(8,128)(2,1)}), bf16[128,2,48,128]{3,2,1,0:T(8,128)(2,1)}, u32[]{:S(2)}, u32[]{:S(2)}) %all-to-all-start.1) | async-done | bytes 3145760 | tf_op jit(solution)/shard_map/all_to_all | solution.py:357
  83.7 4.6 %all-to-all-start = ((bf16[128,2,48,128]{3,2,1,0:T(8,128)(2,1)}), bf16[128,2,48,128]{3,2,1,0:T(8,128)(2,1)S(1)}, u32[]{:S(2)}, u32[]{:S(2)}) async-start(bf16[128,2,48,128]{3,2,1,0:T(8,128)(2,1)} %copy-done), calls=%async_computation | async-start | bytes 6291456 | tf_op jit(solution)/shard_map/all_to_all | solution.py:361
  88.3 0.1 fusion
  88.4 0.1 dynamic_slice.3.valid_ref
  88.5 12.2 %correlate.2.refs_0_ = bf16[2,1024,1024]{2,1,0:T(8,128)(2,1)} custom-call(s32[2]{0:T(128)S(1)} %dynamic_slice.3.valid_ref, bf16[128,2,48,128]{3,2,1,0:T(8,128)(2,1)} %all-to-all-done.1.piece), custom_call_target="tpu_custom_call" | custom-call | flops 5000000000 | bytes 19922944 | tf_op jit(solution)/shard_map/correlate/pallas_call | solution.py:299
  100.7 29.4 %all-to-all-done.piece = bf16[128,2,48,128]{3,2,1,0:T(8,128)(2,1)S(1)} async-done(((bf16[128,2,48,128]{3,2,1,0:T(8,128)(2,1)}), bf16[128,2,48,128]{3,2,1,0:T(8,128)(2,1)S(1)}, u32[]{:S(2)}, u32[]{:S(2)}) %all-to-all-start) | async-done | bytes 3145760 | tf_op jit(solution)/shard_map/all_to_all | solution.py:361
  130.1 10.1 %correlate.3 = f32[2,1024,1024]{2,1,0:T(8,128)} custom-call(s32[2]{0:T(128)S(1)} %dynamic_slice.3.valid_ref, bf16[128,2,48,128]{3,2,1,0:T(8,128)(2,1)S(1)} %all-to-all-done.piece, bf16[2,1024,1024]{2,1,0:T(8,128)(2,1)} %correlate.2.refs_0_), custom_call_target="tpu_custom_call" | custom-call | flops 5000000000 | bytes 19922944 | tf_op jit(solution)/shard_map/correlate/pallas_call | solution.py:299
  (5 shorter events, 0.0 us)
Async XLA Ops:
  6.5 10.1 %copy-start.6 = (s32[144]{0:T(256)S(1)}, s32[144]{0:T(256)}, u32[]{:S(2)}) copy-start(s32[144]{0:T(256)} %param.7) | copy-start | bytes 1732
  6.5 10.4 %copy-start.5 = (f32[8,4096]{1,0:T(8,128)S(1)}, f32[8,4096]{1,0:T(8,128)}, u32[]{:S(2)}) copy-start(f32[8,4096]{1,0:T(8,128)} %constant.51.clone.refs_4_.refs_8_) | copy-start | bytes 393220
  6.5 17.0 %collective-permute-start = (bf16[2,64,4096]{2,1,0:T(8,128)(2,1)}, bf16[2,64,4096]{2,1,0:T(8,128)(2,1)}, u32[]{:S(2)}, u32[]{:S(2)}) collective-permute-start(bf16[2,64,4096]{2,1,0:T(8,128)(2,1)} %get-tuple-element.13.refs_3_), channel_id=1, source_target_pairs={{0,1},{1,2},{2,3},{3,4},{4,5},{5,6},{6,7},{8,9},{9,10},{10,11},{11... | collective-permute-start | bytes 3145736 | tf_op jit(solution)/shard_map/ppermute | solution.py:335
  11.2 20.0 %collective-permute-start.1 = (bf16[2,64,4096]{2,1,0:T(8,128)(2,1)S(1)}, bf16[2,64,4096]{2,1,0:T(8,128)(2,1)}, u32[]{:S(2)}, u32[]{:S(2)}) collective-permute-start(bf16[2,64,4096]{2,1,0:T(8,128)(2,1)S(1)} %get-tuple-element.15.refs_0_), channel_id=1, source_target_pairs={{0,7},{1,0},{2,1},{3,2},{4,3},{5,4},{6,5},{7,6},{8,15},{9,8},{10,9... | collective-permute-start | bytes 3145736 | tf_op jit(solution)/shard_map/ppermute | solution.py:336
  12.1 18.8 %collective-permute-start.2 = (bf16[2,32,4096]{2,1,0:T(8,128)(2,1)}, bf16[2,32,4096]{2,1,0:T(8,128)(2,1)}, u32[]{:S(2)}, u32[]{:S(2)}) collective-permute-start(bf16[2,32,4096]{2,1,0:T(8,128)(2,1)} %slice.40), channel_id=1, source_target_pairs={{0,1},{1,2},{2,3},{3,4},{4,5},{5,6},{6,7},{8,9},{9,10},{10,11},{11... | collective-permute-start | bytes 1572872 | tf_op jit(solution)/shard_map/ppermute | solution.py:337
  16.5 14.6 %collective-permute-start.3 = (bf16[2,32,4096]{2,1,0:T(8,128)(2,1)}, bf16[2,32,4096]{2,1,0:T(8,128)(2,1)}, u32[]{:S(2)}, u32[]{:S(2)}) collective-permute-start(bf16[2,32,4096]{2,1,0:T(8,128)(2,1)} %slice.41), channel_id=1, source_target_pairs={{0,7},{1,0},{2,1},{3,2},{4,3},{5,4},{6,5},{7,6},{8,15},{9,8},{10,9... | collective-permute-start | bytes 1572872 | tf_op jit(solution)/shard_map/ppermute | solution.py:338
  16.9 1.0 copy-start.2
  18.0 5.6 %copy-start.3 = (bf16[512,512]{1,0:T(8,128)(2,1)S(1)}, bf16[512,512]{1,0:T(8,128)(2,1)}, u32[]{:S(2)}) copy-start(bf16[512,512]{1,0:T(8,128)(2,1)} %constant.53.refs_5_.refs_9_) | copy-start | bytes 1572868
  29.2 1.6 %copy-start.1 = (bf16[128,2,48,128]{3,2,1,0:T(8,128)(2,1)}, bf16[128,2,48,128]{3,2,1,0:T(8,128)(2,1)S(1)}, u32[]{:S(2)}) copy-start(bf16[128,2,48,128]{3,2,1,0:T(8,128)(2,1)S(1)} %channels.4) | copy-start | bytes 9437188
  31.2 52.5 %all-to-all-start.1 = ((bf16[128,2,48,128]{3,2,1,0:T(8,128)(2,1)}), bf16[128,2,48,128]{3,2,1,0:T(8,128)(2,1)}, u32[]{:S(2)}, u32[]{:S(2)}) async-start(bf16[128,2,48,128]{3,2,1,0:T(8,128)(2,1)} %copy-done.1), calls=%async_computation.1 | async-start | bytes 6291456 | tf_op jit(solution)/shard_map/all_to_all | solution.py:357
  42.3 1.0 copy-start.4
  53.2 1.7 %copy-start = (bf16[128,2,48,128]{3,2,1,0:T(8,128)(2,1)}, bf16[128,2,48,128]{3,2,1,0:T(8,128)(2,1)S(1)}, u32[]{:S(2)}) copy-start(bf16[128,2,48,128]{3,2,1,0:T(8,128)(2,1)S(1)} %channels.5) | copy-start | bytes 9437188
  83.7 46.4 %all-to-all-start = ((bf16[128,2,48,128]{3,2,1,0:T(8,128)(2,1)}), bf16[128,2,48,128]{3,2,1,0:T(8,128)(2,1)S(1)}, u32[]{:S(2)}, u32[]{:S(2)}) async-start(bf16[128,2,48,128]{3,2,1,0:T(8,128)(2,1)} %copy-done), calls=%async_computation | async-start | bytes 6291456 | tf_op jit(solution)/shard_map/all_to_all | solution.py:361
